TPU v7x, 128 devices: a whole 4x4x4 slice. The times are simulated.
128 devices in a mesh: patch: 32 (over y, x, core), slab: 4 (over z).
Axes of the slice: x: 4, y: 4, z: 4, core: 2. Of those that a mesh axis runs over, the one named last changes fastest.
Arguments:
- history: bfloat16 [512, 256, 128], P('patch', 'slab'), may hold values from -6 to 6
- interp_weights: bfloat16 [512, 32, 4], P('patch'), may hold values from -3 to 3
- pair_table: int32 [512, 32, 3], P('patch'), may hold values from 0 to 511, as said below
- coupling: bfloat16 [512, 32, 128, 128], P('patch', 'slab'), may hold values from -0.09375 to 0.09375
- self_inverse: bfloat16 [512, 128, 128], P('patch'), may hold values from -0.5 to 0.5
- incident: float32 [512, 4, 128], P('patch'), may hold values from -6 to 6
Outputs:
- amplitudes: bfloat16 [512, 4, 128], P('patch')
Inputs may be any that keep to these rules, and one draw needn't show every extreme that they name: pair_table[p, k] holds the observer patch (0 to 511), the first delay step (1 to 252) and the band width (1 to 4) of the k-th interaction whose sources are patch p's.
All inputs are finite; a program needn't handle non-finite values.
Results may differ from a plain program's by a relative error of at most 0.008.
Values may be sent and summed in bfloat16 or wider, within the bound.
No kernel may reach another device: no remote copies, remote signals or barrier semaphores. Data moves between devices by JAX's collectives and lax.ppermute only.
A program may use at most 64 MiB of HBM per device.

v0:
```python
import jax
import jax.numpy as jnp
from jax import lax
from jax.sharding import PartitionSpec as P

WMAX = 4
STEPS = 4


def on_device(history, interp_weights, pair_table, coupling, self_inverse, incident):
    patch_dev = history.shape[0]
    slab_len = history.shape[1]
    src_count = history.shape[2]
    local_pairs = coupling.shape[1]
    slab_id = lax.axis_index("slab")
    observer = pair_table[:, :, 0]
    first_delay = pair_table[:, :, 1]
    band_width = pair_table[:, :, 2]
    tap_index = jnp.arange(WMAX, dtype=jnp.int32)
    weights = jnp.where(
        tap_index[None, None, :] < band_width[:, :, None],
        interp_weights,
        jnp.zeros_like(interp_weights),
    )
    slab_rows = jnp.arange(slab_len, dtype=jnp.int32)
    pair_start = slab_id * local_pairs
    local_delay = lax.dynamic_slice_in_dim(first_delay, pair_start, local_pairs, 1)
    local_weights = lax.dynamic_slice_in_dim(weights, pair_start, local_pairs, 1)
    local_obs = lax.dynamic_slice_in_dim(observer, pair_start, local_pairs, 1).reshape(-1)
    step_rows = jnp.arange(STEPS, dtype=jnp.int32)
    new_amps = jnp.zeros((patch_dev, STEPS, src_count), jnp.bfloat16)
    for time_step in range(STEPS):
        step_list = jnp.full((1,), time_step, jnp.int32)
        target = first_delay[:, :, None] + tap_index[None, None, :] - 1 - slab_id * slab_len
        rows_hit = target[:, :, None, :] - step_list[None, None, :, None]
        onehot = rows_hit[..., None] == slab_rows
        tables = jnp.sum(
            jnp.where(onehot, weights[:, :, None, :, None], jnp.zeros((), jnp.bfloat16)), axis=3
        )
        stored = lax.psum_scatter(
            jnp.einsum("pcsl,plj->cpsj", tables, history, preferred_element_type=jnp.float32),
            "slab",
            scatter_dimension=0,
            tiled=True,
        )[:, :, 0]
        recent_time = time_step - local_delay[:, :, None] - tap_index[None, None, :]
        recent_hit = recent_time[..., None] == step_rows
        recent_table = jnp.sum(
            jnp.where(recent_hit, local_weights[..., None], jnp.zeros((), jnp.bfloat16)), axis=2
        )
        recent = jnp.einsum(
            "pkm,pmj->kpj", recent_table, new_amps, preferred_element_type=jnp.float32
        )
        driven = (stored + recent).astype(jnp.bfloat16)
        coupled = jnp.einsum("pkij,kpj->pki", coupling, driven, preferred_element_type=jnp.float32)
        contrib = coupled.reshape(-1, src_count)
        targets = jnp.arange(patch_dev * lax.axis_size("patch"), dtype=jnp.int32)
        field_onehot = (targets[:, None] == local_obs[None, :]).astype(jnp.float32)
        field_share = lax.psum_scatter(
            jnp.dot(
                field_onehot,
                contrib,
                precision=lax.Precision.HIGHEST,
                preferred_element_type=jnp.float32,
            ),
            "patch",
            scatter_dimension=0,
            tiled=True,
        )
        scattered = lax.psum(field_share, "slab")
        drive = (incident[:, time_step] - scattered).astype(jnp.bfloat16)
        amplitude = jnp.einsum(
            "pij,pj->pi", self_inverse, drive, preferred_element_type=jnp.float32
        ).astype(jnp.bfloat16)
        new_amps = new_amps.at[:, time_step].set(amplitude)
    return new_amps


def solution(mesh):
    in_specs = (
        P("patch", "slab", None),
        P("patch", None, None),
        P("patch", None, None),
        P("patch", "slab", None, None),
        P("patch", None, None),
        P("patch", None, None),
    )
    out_specs = P("patch", None, None)
    return jax.shard_map(
        on_device, mesh=mesh, in_specs=in_specs, out_specs=out_specs, check_vma=False
    )
```

profile of v0, /device:TPU:1, one launch (start us, length us, event | category | flops | bytes accessed | tf_op | source)
XLA Modules:
  0.0 452.1 jit_solution(12548510856071760224)
XLA Ops:
  6.6 0.8 fusion.62
  7.4 0.7 fusion.44
  8.1 2.1 fusion.16
  10.2 1.8 convolution_bitcast_fusion.3
  12.1 0.0 reduce-scatter.9.cloned.1.call-update
  12.1 0.0 reduce-scatter.11.cloned.1.call-start
  12.1 0.1 constant_dynamic-slice_fusion.1
  12.2 0.1 copy.61
  12.3 0.1 constant_dynamic-slice_fusion
  12.4 0.1 copy.27
  12.5 0.1 copy.28
  12.6 0.1 constant_dynamic-slice_fusion.2
  12.7 0.1 eq.173
  12.8 21.2 %reduce-scatter.9.cloned.1.call-done = f32[8,16,1,128]{3,0,1,2:T(8,128)} async-done(((f32[32,16,1,128]{3,0,1,2:T(8,128)}), f32[8,16,1,128]{3,0,1,2:T(8,128)}) %reduce-scatter.9.cloned.1.call-update) | async-done | bytes 65552 | tf_op jit(solution)/shard_map/reduce_scatter | solution.py:40
  34.0 1.0 fusion.11
  35.1 4.4 fusion.34
  39.5 1.0 fusion.23
  40.5 0.0 reduce-scatter.11.cloned.1.call-update
  40.5 0.0 reduce-scatter.13.cloned.1.call-start
  40.6 0.9 convolution_bitcast_fusion.2
  41.5 0.0 reduce-scatter.13.cloned.1.call-update
  41.5 0.0 reduce-scatter.15.cloned.1.call-start
  41.6 0.1 copy.31
  41.7 75.6 %reduce-scatter.11.cloned.1.call-done = f32[16,128]{1,0:T(8,128)} async-done(((f32[512,128]{1,0:T(8,128)}), f32[16,128]{1,0:T(8,128)}) %reduce-scatter.11.cloned.1.call-update) | async-done | bytes 8208 | tf_op jit(solution)/shard_map/reduce_scatter | solution.py:59
  117.3 9.0 %psum.28 = f32[16,128]{1,0:T(8,128)S(1)} all-reduce(f32[16,128]{1,0:T(8,128)} %reduce-scatter.11.cloned.1.call-done), channel_id=1, replica_groups=mesh['patch'=32,'slab'=4] {'slab'}, use_global_device_ids=true, to_apply=%region_4.5 | all-reduce | flops 2048 | bytes 16384 | tf_op jit(solution)/shard_map/psum | solution.py:70
  126.4 0.4 fusion.51
  126.8 13.0 %reduce-scatter.13.cloned.1.call-done = f32[8,16,1,128]{3,0,1,2:T(8,128)} async-done(((f32[32,16,1,128]{3,0,1,2:T(8,128)}), f32[8,16,1,128]{3,0,1,2:T(8,128)}) %reduce-scatter.13.cloned.1.call-update) | async-done | bytes 65552 | tf_op jit(solution)/shard_map/reduce_scatter | solution.py:40
  139.8 1.0 fusion.10
  140.9 4.4 fusion.32
  145.3 1.0 fusion.22
  146.3 0.0 reduce-scatter.15.cloned.1.call-update
  146.3 0.0 reduce-scatter.17.cloned.1.call-start
  146.4 0.9 convolution_bitcast_fusion.1
  147.3 0.0 reduce-scatter.17.cloned.1.call-update
  147.3 0.0 reduce-scatter.19.cloned.1.call-start
  147.3 0.1 copy.34
  147.4 75.7 %reduce-scatter.15.cloned.1.call-done = f32[16,128]{1,0:T(8,128)} async-done(((f32[512,128]{1,0:T(8,128)}), f32[16,128]{1,0:T(8,128)}) %reduce-scatter.15.cloned.1.call-update) | async-done | bytes 8208 | tf_op jit(solution)/shard_map/reduce_scatter | solution.py:59
  223.1 9.0 %psum.29 = f32[16,128]{1,0:T(8,128)S(1)} all-reduce(f32[16,128]{1,0:T(8,128)} %reduce-scatter.15.cloned.1.call-done), channel_id=1, replica_groups=mesh['patch'=32,'slab'=4] {'slab'}, use_global_device_ids=true, to_apply=%region_9.10 | all-reduce | flops 2048 | bytes 16384 | tf_op jit(solution)/shard_map/psum | solution.py:70
  232.2 0.4 fusion.49
  232.6 0.1 scatter.15
  232.6 12.7 %reduce-scatter.17.cloned.1.call-done = f32[8,16,1,128]{3,0,1,2:T(8,128)} async-done(((f32[32,16,1,128]{3,0,1,2:T(8,128)}), f32[8,16,1,128]{3,0,1,2:T(8,128)}) %reduce-scatter.17.cloned.1.call-update) | async-done | bytes 65552 | tf_op jit(solution)/shard_map/reduce_scatter | solution.py:40
  245.4 1.0 fusion.9
  246.4 4.4 fusion.30
  250.8 1.0 fusion.21
  251.8 0.0 reduce-scatter.19.cloned.1.call-update
  251.9 0.0 reduce-scatter.21.cloned.1.call-start
  251.9 0.9 convolution_bitcast_fusion
  252.8 0.0 reduce-scatter.21.cloned.1.call-update
  252.8 0.0 reduce-scatter.23.cloned.1.call-start
  252.9 0.1 copy.37
  253.0 75.7 %reduce-scatter.19.cloned.1.call-done = f32[16,128]{1,0:T(8,128)} async-done(((f32[512,128]{1,0:T(8,128)}), f32[16,128]{1,0:T(8,128)}) %reduce-scatter.19.cloned.1.call-update) | async-done | bytes 8208 | tf_op jit(solution)/shard_map/reduce_scatter | solution.py:59
  328.6 9.0 %psum.30 = f32[16,128]{1,0:T(8,128)S(1)} all-reduce(f32[16,128]{1,0:T(8,128)} %reduce-scatter.19.cloned.1.call-done), channel_id=1, replica_groups=mesh['patch'=32,'slab'=4] {'slab'}, use_global_device_ids=true, to_apply=%region_14.15 | all-reduce | flops 2048 | bytes 16384 | tf_op jit(solution)/shard_map/psum | solution.py:70
  337.7 0.4 fusion.47
  338.1 0.1 scatter.16
  338.1 0.0 copy-start.2
  338.2 13.0 %reduce-scatter.21.cloned.1.call-done = f32[8,16,1,128]{3,0,1,2:T(8,128)} async-done(((f32[32,16,1,128]{3,0,1,2:T(8,128)}), f32[8,16,1,128]{3,0,1,2:T(8,128)}) %reduce-scatter.21.cloned.1.call-update) | async-done | bytes 65552 | tf_op jit(solution)/shard_map/reduce_scatter | solution.py:40
  351.1 1.0 fusion.8
  352.2 4.4 fusion.28
  356.6 1.0 fusion.20
  357.6 0.0 reduce-scatter.23.cloned.1.call-update
  357.6 76.8 %reduce-scatter.23.cloned.1.call-done = f32[16,128]{1,0:T(8,128)} async-done(((f32[512,128]{1,0:T(8,128)}), f32[16,128]{1,0:T(8,128)}) %reduce-scatter.23.cloned.1.call-update) | async-done | bytes 8208 | tf_op jit(solution)/shard_map/reduce_scatter | solution.py:59
  434.4 9.0 %psum.31 = f32[16,128]{1,0:T(8,128)S(1)} all-reduce(f32[16,128]{1,0:T(8,128)} %reduce-scatter.23.cloned.1.call-done), channel_id=1, replica_groups=mesh['patch'=32,'slab'=4] {'slab'}, use_global_device_ids=true, to_apply=%region_19.20 | all-reduce | flops 2048 | bytes 16384 | tf_op jit(solution)/shard_map/psum | solution.py:70
  443.5 0.4 fusion.45
  443.9 1.4 scatter.19
  (27 shorter events, 0.3 us)
Async XLA Ops:
  6.5 119.8 %copy-start = (bf16[16,128,128]{2,1,0:T(8,128)(2,1)S(1)}, bf16[16,128,128]{2,1,0:T(8,128)(2,1)}, u32[]{:S(2)}) copy-start(bf16[16,128,128]{2,1,0:T(8,128)(2,1)} %param.18) | copy-start | bytes 1572868
  6.5 34.0 %copy-start.1 = (bf16[16,64,128]{2,1,0:T(8,128)(2,1)S(1)}, bf16[16,64,128]{2,1,0:T(8,128)(2,1)}, u32[]{:S(2)}) copy-start(bf16[16,64,128]{2,1,0:T(8,128)(2,1)} %param.14) | copy-start | bytes 786436
  6.5 35.0 %copy-start.3 = (f32[16,4,128]{2,1,0:T(4,128)S(1)}, f32[16,4,128]{2,1,0:T(4,128)}, u32[]{:S(2)}) copy-start(f32[16,4,128]{2,1,0:T(4,128)} %param.19) | copy-start | bytes 98308
  6.5 27.5 %reduce-scatter.9.cloned.1.call-start = ((), (), s32[]{:S(2)}) async-start(), calls=%async_computation.8 | async-start | bytes 327680 | tf_op jit(solution)/shard_map/reduce_scatter | solution.py:40
  12.1 105.2 %reduce-scatter.11.cloned.1.call-start = ((), (), s32[]{:S(2)}) async-start(), calls=%async_computation.9 | async-start | bytes 270336 | tf_op jit(solution)/shard_map/reduce_scatter | solution.py:59
  40.5 99.3 %reduce-scatter.13.cloned.1.call-start = ((), (), s32[]{:S(2)}) async-start(), calls=%async_computation.10 | async-start | bytes 327680 | tf_op jit(solution)/shard_map/reduce_scatter | solution.py:40
  41.5 181.6 %reduce-scatter.15.cloned.1.call-start = ((), (), s32[]{:S(2)}) async-start(), calls=%async_computation.11 | async-start | bytes 270336 | tf_op jit(solution)/shard_map/reduce_scatter | solution.py:59
  146.3 99.0 %reduce-scatter.17.cloned.1.call-start = ((), (), s32[]{:S(2)}) async-start(), calls=%async_computation.12 | async-start | bytes 327680 | tf_op jit(solution)/shard_map/reduce_scatter | solution.py:40
  147.3 181.4 %reduce-scatter.19.cloned.1.call-start = ((), (), s32[]{:S(2)}) async-start(), calls=%async_computation.13 | async-start | bytes 270336 | tf_op jit(solution)/shard_map/reduce_scatter | solution.py:59
  251.9 99.3 %reduce-scatter.21.cloned.1.call-start = ((), (), s32[]{:S(2)}) async-start(), calls=%async_computation.14 | async-start | bytes 327680 | tf_op jit(solution)/shard_map/reduce_scatter | solution.py:40
  252.8 181.6 %reduce-scatter.23.cloned.1.call-start = ((), (), s32[]{:S(2)}) async-start(), calls=%async_computation.15 | async-start | bytes 270336 | tf_op jit(solution)/shard_map/reduce_scatter | solution.py:59
  338.1 105.7 %copy-start.2 = (bf16[16,4,128]{2,1,0:T(4,128)(2,1)}, bf16[16,4,128]{2,1,0:T(4,128)(2,1)S(1)}, u32[]{:S(2)}) copy-start(bf16[16,4,128]{2,1,0:T(4,128)(2,1)S(1)} %scatter.16) | copy-start | bytes 49156
Sparse Core Ops, SparseCore 0:
  12.2 21.7 reduce-scatter.8
  40.6 76.6 reduce-scatter.10
  119.8 19.9 reduce-scatter.12
  146.4 76.6 reduce-scatter.14
  225.3 19.9 reduce-scatter.16
  252.0 76.6 reduce-scatter.18
  331.1 19.9 reduce-scatter.20
  357.8 76.5 reduce-scatter.22
where the time goes:
time: 456 us; the launch traced here: 452 us
  waiting for transfers between devices  364 us (80%)
  blocking collectives  36.2 us (8%)
  matrix products  31.8 us (7%)
  between operations  13.7 us (3%)
    reduce_scatter x4, waiting for transfers between devices, on_device(): lax.psum_scatter(jnp.dot(field_onehot, contrib, precision=lax.Precision.H...  304 us
    reduce_scatter x4, waiting for transfers between devices, on_device(): lax.psum_scatter(jnp.einsum('pcsl,plj->cpsj', tables, history, preferred_...  60 us
    psum x4, blocking collectives, on_device(): scattered = lax.psum(field_share, 'slab')  36.2 us
    dot_general x4, matrix products, on_device(): jnp.einsum('pkij,kpj->pki', coupling, driven, preferred_element_type=jnp....  17.7 us
  transfers between devices with their start and end apart: 8, of which 8 were waited for; matrix products, arithmetic and copies ran while one was open for 1% of the time, Pallas kernels for 0%

commit v1 on v0

v1 whole, which is shorter than its diff:
```python
import jax
import jax.numpy as jnp
from jax import lax
from jax.experimental import pallas as pl
from jax.experimental.pallas import tpu as pltpu
from jax.sharding import PartitionSpec as P

WMAX = 4
STEPS = 4
LAGS = STEPS - 1

BF16 = jnp.bfloat16
F32 = jnp.float32


def dot_f32(a, b, contract):
    return lax.dot_general(a, b, (contract, ((), ())), preferred_element_type=F32)


def history_kernel(rows_ref, hist_ref, *outs):
    own_ref, send_refs = outs[0], outs[1:]
    patches, slab_len, src = hist_ref.shape
    slabs = len(send_refs) // 2 + 1
    pairs = rows_ref.shape[2] // STEPS
    local = pairs // slabs
    h = lax.broadcasted_iota(jnp.int32, (slab_len, STEPS * pairs), 0).astype(F32)
    for p in range(0, patches, 2):
        parts = []
        for q in (p, p + 1):
            j = h - rows_ref[q, 0:1, :]
            table = jnp.where(j == 0, rows_ref[q, 1:2, :], 0.0)
            for tap in range(1, WMAX):
                table = jnp.where(j == tap, rows_ref[q, tap + 1 : tap + 2, :], table)
            parts.append(dot_f32(table.astype(BF16), hist_ref[q], ((0,), (0,))))
        at = pl.ds(p * local, 2 * local)
        for n in range(STEPS):
            for s in range(slabs):
                lo = n * pairs + s * local
                both = jnp.concatenate([part[lo : lo + local] for part in parts], axis=0)
                if s == 0:
                    own_ref[n, at, :] = both
                elif n == 0:
                    send_refs[s - 1][0, at, :] = both.astype(BF16)
                else:
                    send_refs[slabs - 2 + s][n - 1, at, :] = both.astype(BF16)


def field_of(driven, obs_ref, coup_ref, send_ref):
    rows, src = driven.shape
    patches = coup_ref.shape[0]
    local = rows // patches
    row_id = lax.broadcasted_iota(jnp.int32, (local, src), 0)
    coupled = []
    for p in range(patches):
        mine = driven[p * local : (p + 1) * local].astype(BF16)
        full = dot_f32(mine, coup_ref[p].reshape(local * src, src), ((1,), (1,)))
        out = full[:, :src]
        for k in range(1, local):
            out = jnp.where(row_id == k, full[:, k * src : (k + 1) * src], out)
        coupled.append(out)
    coupled = jnp.concatenate(coupled, axis=0).astype(BF16)
    blocks, slabs, dev_rows, _ = send_ref.shape
    targets = lax.broadcasted_iota(jnp.int32, (blocks * dev_rows, rows), 0)
    onehot = jnp.where(targets == obs_ref[0:1, :], 1.0, 0.0).astype(BF16)
    field = dot_f32(onehot, coupled, ((1,), (0,))).astype(BF16)
    field = field.reshape(blocks, dev_rows, src)
    for s in range(slabs):
        send_ref[:, s] = field


def first_kernel(own_ref, a_ref, b_ref, c_ref, obs_ref, coup_ref, send_ref):
    driven = own_ref[0] + a_ref[0].astype(F32) + b_ref[0].astype(F32) + c_ref[0].astype(F32)
    field_of(driven, obs_ref, coup_ref, send_ref)


def amplitude_of(step, recv_ref, inc_ref, sinv_ref):
    sources, patches, src = recv_ref.shape
    total = jnp.sum(recv_ref[...].astype(F32), axis=0)
    drive = (inc_ref[step] - total).astype(BF16)
    row_id = lax.broadcasted_iota(jnp.int32, (patches, src), 0)
    amp = jnp.zeros((patches, src), F32)
    full = dot_f32(drive, sinv_ref[...].reshape(patches * src, src), ((1,), (1,)))
    for p in range(patches):
        amp = jnp.where(row_id == p, full[:, p * src : (p + 1) * src], amp)
    return amp.astype(BF16)


def step_kernel(step, recv_ref, inc_ref, sinv_ref, lag_ref, own_ref, a_ref, b_ref, c_ref, obs_ref, coup_ref, *rest):
    past_refs, (send_ref, amp_ref) = rest[:-2], rest[-2:]
    amp = amplitude_of(step, recv_ref, inc_ref, sinv_ref)
    amp_ref[...] = amp
    driven = (
        own_ref[step + 1]
        + a_ref[step].astype(F32)
        + b_ref[step].astype(F32)
        + c_ref[step].astype(F32)
    )
    for lag, past in enumerate([amp] + [r[...] for r in past_refs]):
        driven = driven + dot_f32(lag_ref[lag], past, ((0,), (0,)))
    field_of(driven, obs_ref, coup_ref, send_ref)


def last_kernel(recv_ref, inc_ref, sinv_ref, amp_ref):
    amp_ref[...] = amplitude_of(STEPS - 1, recv_ref, inc_ref, sinv_ref)


def call(kernel, name, outs, args):
    vmem = pl.BlockSpec(memory_space=pltpu.VMEM)
    return pl.pallas_call(
        kernel,
        name=name,
        out_shape=outs,
        in_specs=[vmem] * len(args),
        out_specs=jax.tree.map(lambda _: vmem, outs),
        compiler_params=pltpu.CompilerParams(vmem_limit_bytes=24 * 2**20),
    )(*args)


def on_device(history, interp_weights, pair_table, coupling, self_inverse, incident):
    patches, slab_len, src = history.shape
    pairs = pair_table.shape[1]
    local = coupling.shape[1]
    slabs = lax.axis_size("slab")
    blocks = lax.axis_size("patch")
    slab_id = lax.axis_index("slab")
    rows = patches * local

    def rolled(x):
        return lax.dynamic_slice_in_dim(jnp.concatenate([x, x], axis=1), slab_id * local, pairs, 1)

    table = rolled(pair_table)
    observer, first, band = table[..., 0], table[..., 1], table[..., 2]
    taps = jnp.arange(WMAX, dtype=jnp.int32)
    weights = jnp.where(taps < band[..., None], rolled(interp_weights).astype(F32), 0.0)
    steps = jnp.arange(STEPS, dtype=jnp.int32)
    start = first[:, None, :] - 1 - slab_id * slab_len - steps[:, None]
    start = start.reshape(patches, 1, STEPS * pairs).astype(F32)
    spread = jnp.tile(weights.transpose(0, 2, 1), (1, 1, STEPS))
    table_rows = jnp.concatenate([start, spread, jnp.zeros((patches, 3, STEPS * pairs), F32)], axis=1)
    obs = observer[:, :local].reshape(1, rows)
    lags = jnp.arange(1, STEPS, dtype=jnp.int32)
    hit = lags[:, None, None, None] - first[None, :, :local, None] == taps
    lag_w = jnp.sum(jnp.where(hit, weights[None, :, :local], 0.0), axis=-1)
    same = jnp.arange(patches)[:, None] == jnp.arange(rows)[None, :] // local
    lag_table = jnp.where(same[None], lag_w.reshape(LAGS, 1, rows), 0.0).astype(BF16)
    inc = incident.transpose(1, 0, 2)

    shape = jax.ShapeDtypeStruct
    outs = (
        [shape((STEPS, rows, src), F32)]
        + [shape((1, rows, src), BF16)] * (slabs - 1)
        + [shape((STEPS - 1, rows, src), BF16)] * (slabs - 1)
    )
    own, *sends = call(history_kernel, "history", outs, [table_rows, history])

    def moved(x, s):
        return lax.ppermute(x, "slab", [(z, (z + s) % slabs) for z in range(slabs)])

    now = [moved(x, s + 1) for s, x in enumerate(sends[: slabs - 1])]
    later = [moved(x, s + 1) for s, x in enumerate(sends[slabs - 1 :])]

    send_shape = shape((blocks, slabs, patches, src), BF16)
    send = call(first_kernel, "field0", send_shape, [own, *now, obs, coupling])
    amps = []
    for step in range(STEPS):
        recv = lax.all_to_all(
            send.reshape(blocks * slabs, patches, src), ("patch", "slab"), 0, 0, tiled=True
        )
        if step == STEPS - 1:
            amps.append(
                call(last_kernel, "last", shape((patches, src), BF16), [recv, inc, self_inverse])
            )
            break

        def body(*refs, step=step):
            step_kernel(step, *refs)

        send, amp = call(
            body,
            f"step{step}",
            [send_shape, shape((patches, src), BF16)],
            [recv, inc, self_inverse, lag_table, own, *later, obs, coupling, *amps[::-1]],
        )
        amps.append(amp)
    return jnp.stack(amps, axis=1)


def solution(mesh):
    in_specs = (
        P("patch", "slab", None),
        P("patch", None, None),
        P("patch", None, None),
        P("patch", "slab", None, None),
        P("patch", None, None),
        P("patch", None, None),
    )
    out_specs = P("patch", None, None)
    return jax.shard_map(
        on_device, mesh=mesh, in_specs=in_specs, out_specs=out_specs, check_vma=False
    )
```

time: 456 us -> 107 us (0.23)
  waiting for transfers between devices: 364 us -> 13.7 us
  matrix products: 31.8 us -> 0 us
  starting transfers between devices: 0.3 us -> 20.3 us
  blocking collectives: 36.2 us -> 53.6 us
  between operations: 13.7 us -> 0.2 us
  Pallas kernels: 0 us -> 8.62 us
    reduce_scatter x8 -> x0, waiting for transfers between devices: 364 us -> none  [the longest x4 304 us: on_device(): lax.psum_scatter(jnp.dot(field_onehot, contrib, precision=lax.Precision.H...]
    all_to_all x0 -> x3, blocking collectives: none -> 53.6 us  [on_device(): lax.all_to_all(send.reshape(blocks * slabs, patches, src), ('patch', 'sla...]
    psum x4 -> x0, blocking collectives: 36.2 us -> none  [on_device(): scattered = lax.psum(field_share, 'slab')]
    dot_general x20 -> x0, matrix products: 31.8 us -> none  [the longest x4 17.7 us: on_device(): jnp.einsum('pkij,kpj->pki', coupling, driven, preferred_element_type=jnp....]
    all_to_all x0 -> x1, waiting for transfers between devices: none -> 13.7 us  [on_device(): lax.all_to_all(send.reshape(blocks * slabs, patches, src), ('patch', 'sla...]
    all_to_all x0 -> x1, starting transfers between devices: none -> 10.5 us  [on_device(): lax.all_to_all(send.reshape(blocks * slabs, patches, src), ('patch', 'sla...]
    ppermute x0 -> x6, starting transfers between devices: none -> 9.77 us  [moved(): return lax.ppermute(x, 'slab', [(z, (z + s) % slabs) for z in range(slabs)])]
    pallas_call x0 -> x6, Pallas kernels: none -> 8.62 us  [call(): pl.pallas_call(kernel, name=name, out_shape=outs, in_specs=[vmem] * len(a...]
  transfers between devices with their start and end apart: 8 -> 7, of which waited for: 8 -> 1; matrix products, arithmetic and copies ran while one was open for 1% -> 1% of each run, Pallas kernels for 0% -> 2%
where the time goes in v1:
time: 107 us; the launch traced here: 106 us
  blocking collectives  53.6 us (50%)
  starting transfers between devices  20.3 us (19%)
  waiting for transfers between devices  13.7 us (13%)
  Pallas kernels  8.62 us (8%)
  local copies, waits for them, and re-layouts  6.79 us (6%)
  other arithmetic  2.96 us (3%)
    all_to_all x3, blocking collectives, on_device(): lax.all_to_all(send.reshape(blocks * slabs, patches, src), ('patch', 'sla...  53.6 us
    all_to_all x1, waiting for transfers between devices, on_device(): lax.all_to_all(send.reshape(blocks * slabs, patches, src), ('patch', 'sla...  13.7 us
    all_to_all x1, starting transfers between devices, on_device(): lax.all_to_all(send.reshape(blocks * slabs, patches, src), ('patch', 'sla...  10.5 us
    ppermute x6, starting transfers between devices, moved(): return lax.ppermute(x, 'slab', [(z, (z + s) % slabs) for z in range(slabs)])  9.77 us
    pallas_call x6, Pallas kernels, call(): pl.pallas_call(kernel, name=name, out_shape=outs, in_specs=[vmem] * len(a...  8.62 us
    unnamed x11, local copies, waits for them, and re-layouts  5.34 us
  transfers between devices with their start and end apart: 7, of which 1 were waited for; matrix products, arithmetic and copies ran while one was open for 1% of the time, Pallas kernels for 2%

profile of v1, /device:TPU:1, one launch (start us, length us, event | category | flops | bytes accessed | tf_op | source)
XLA Modules:
  0.0 106.1 jit_solution(18271583304288249572)
XLA Ops:
  0.0 0.0 copy-start.4
  0.0 0.0 copy-start.2
  0.0 0.1 sub.72
  0.1 0.9 dynamic-slice_add_fusion
  1.0 0.1 sub.70
  1.1 0.9 fusion
  2.1 0.1 tile.10
  2.2 0.1 pad.6.clone
  2.3 0.1 maximum_maximum_fusion.rows_ref
  2.4 0.0 copy-start.3
  2.4 0.9 copy-done.3
  3.3 0.4 history.1
  3.7 2.5 %collective-permute-start = (bf16[1,128,128]{2,1,0:T(8,128)(2,1)S(1)}, bf16[1,128,128]{2,1,0:T(8,128)(2,1)S(1)}, u32[]{:S(2)}, u32[]{:S(2)}) collective-permute-start(bf16[1,128,128]{2,1,0:T(8,128)(2,1)S(1)} %get-tuple-element.19), channel_id=1, source_target_pairs={{0,1},{1,2},{2,3},{3,0},{4,5},{5,6},{6,7},{7,4},{8,9},{9,10},{10,1... | collective-permute-start | bytes 98312 | tf_op jit(solution)/shard_map/ppermute | solution.py:157
  6.2 3.3 %collective-permute-start.1 = (bf16[1,128,128]{2,1,0:T(8,128)(2,1)S(1)}, bf16[1,128,128]{2,1,0:T(8,128)(2,1)S(1)}, u32[]{:S(2)}, u32[]{:S(2)}) collective-permute-start(bf16[1,128,128]{2,1,0:T(8,128)(2,1)S(1)} %get-tuple-element.20), channel_id=1, source_target_pairs={{0,2},{1,3},{2,0},{3,1},{4,6},{5,7},{6,4},{7,5},{8,10},{9,11},{10,... | collective-permute-start | bytes 98312 | tf_op jit(solution)/shard_map/ppermute | solution.py:157
  9.5 0.7 collective-permute-start.2
  10.3 0.7 collective-permute-start.3
  11.0 0.4 collective-permute-start.4
  11.5 0.9 convert_select_fusion
  12.4 0.1 copy.14
  12.4 0.1 copy.15
  12.5 0.1 broadcast_subtract_fusion
  12.6 0.1 reshape.145.obs_ref.refs_8_
  12.7 0.1 copy.16
  12.8 0.1 broadcast_in_dim.54
  12.9 0.0 collective-permute-done.a_ref
  12.9 2.0 %collective-permute-start.5 = (bf16[3,128,128]{2,1,0:T(8,128)(2,1)S(1)}, bf16[3,128,128]{2,1,0:T(8,128)(2,1)S(1)}, u32[]{:S(2)}, u32[]{:S(2)}) collective-permute-start(bf16[3,128,128]{2,1,0:T(8,128)(2,1)S(1)} %get-tuple-element.24), channel_id=1, source_target_pairs={{0,3},{1,0},{2,1},{3,2},{4,7},{5,4},{6,5},{7,6},{8,11},{9,8},{10,9... | collective-permute-start | bytes 294920 | tf_op jit(solution)/shard_map/ppermute | solution.py:157
  14.9 0.0 collective-permute-done.1.b_ref
  14.9 0.0 collective-permute-done.2.c_ref
  14.9 0.0 copy-start
  14.9 2.2 %copy-done = bf16[16,8,128,128]{3,2,1,0:T(8,128)(2,1)S(1)} copy-done((bf16[16,8,128,128]{3,2,1,0:T(8,128)(2,1)S(1)}, bf16[16,8,128,128]{3,2,1,0:T(8,128)(2,1)}, u32[]{:S(2)}) %copy-start) | copy-done | bytes 4194328
  17.1 2.2 %field0.1 = bf16[32,4,16,128]{3,2,1,0:T(8,128)(2,1)} custom-call(f32[4,128,128]{2,1,0:T(8,128)S(1)} %get-tuple-element.18.own_ref.refs_4_, bf16[1,128,128]{2,1,0:T(8,128)(2,1)S(1)} %collective-permute-done.a_ref, bf16[1,128,128]{2,1,0:T(8,128)(2,1)S(1)} %collective-permute-done.1.b_ref, bf16[1,128,128]{2,1,0:T(8,128)(2,1)S(1)} %collective-permute-done.2.c_ref, ...), custom_call_target="tpu_custom_call" | custom-call | tf_op jit(solution)/shard_map/field0/pallas_call | solution.py:109
  19.3 10.5 %all-to-all-start = ((bf16[128,16,128]{2,1,0:T(8,128)(2,1)}), bf16[128,16,128]{2,1,0:T(8,128)(2,1)S(1)}, u32[]{:S(2)}, u32[]{:S(2)}) async-start(bf16[128,16,128]{2,1,0:T(8,128)(2,1)} %bitcast.4), calls=%async_computation | async-start | bytes 1048576 | tf_op jit(solution)/shard_map/all_to_all | solution.py:166
  29.9 0.0 copy-done.4
  29.9 0.0 collective-permute-done.3.refs_5_
  29.9 0.0 collective-permute-done.4.refs_6_
  29.9 0.0 collective-permute-done.5.refs_7_
  29.9 13.7 %all-to-all-done.refs_0_ = bf16[128,16,128]{2,1,0:T(8,128)(2,1)S(1)} async-done(((bf16[128,16,128]{2,1,0:T(8,128)(2,1)}), bf16[128,16,128]{2,1,0:T(8,128)(2,1)S(1)}, u32[]{:S(2)}, u32[]{:S(2)}) %all-to-all-start) | async-done | bytes 524320 | tf_op jit(solution)/shard_map/all_to_all | solution.py:166
  43.6 0.0 copy-done.2
  43.6 0.0 copy-start.1
  43.6 2.2 %copy-done.1 = bf16[16,8,128,128]{3,2,1,0:T(8,128)(2,1)S(1)} copy-done((bf16[16,8,128,128]{3,2,1,0:T(8,128)(2,1)S(1)}, bf16[16,8,128,128]{3,2,1,0:T(8,128)(2,1)}, u32[]{:S(2)}) %copy-start.1) | copy-done | bytes 4194328
  45.8 1.9 %step0.1 = (bf16[32,4,16,128]{3,2,1,0:T(8,128)(2,1)S(1)}, bf16[16,128]{1,0:T(8,128)(2,1)S(1)}) custom-call(bf16[128,16,128]{2,1,0:T(8,128)(2,1)S(1)} %all-to-all-done.refs_0_, f32[4,16,128]{2,1,0:T(8,128)S(1)} %bitcast.24, bf16[16,128,128]{2,1,0:T(8,128)(2,1)S(1)} %copy-done.2, bf16[3,16,128]{2,1,0:T(8,128)(2,1)S(1)} %select_convert_fusion.refs_3_, ...), custom_call_target="tpu_custom_call" | custom-call | tf_op jit(solution)/shard_map/step0/pallas_call | solution.py:109
  47.7 17.9 %all_to_all.20.refs_0_ = bf16[128,16,128]{2,1,0:T(8,128)(2,1)S(1)} all-to-all(bf16[128,16,128]{2,1,0:T(8,128)(2,1)S(1)} %bitcast.29), channel_id=1, replica_groups=mesh['patch'=32,'slab'=4] {'patch','slab'}, dimensions={0} | all-to-all | bytes 1048576 | tf_op jit(solution)/shard_map/all_to_all | solution.py:166
  65.5 1.9 %step1.1 = (bf16[32,4,16,128]{3,2,1,0:T(8,128)(2,1)S(1)}, bf16[16,128]{1,0:T(8,128)(2,1)S(1)}) custom-call(bf16[128,16,128]{2,1,0:T(8,128)(2,1)S(1)} %all_to_all.20.refs_0_, f32[4,16,128]{2,1,0:T(8,128)S(1)} %bitcast.25, bf16[16,128,128]{2,1,0:T(8,128)(2,1)S(1)} %copy-done.2, bf16[3,16,128]{2,1,0:T(8,128)(2,1)S(1)} %select_convert_fusion.refs_3_, ...), custom_call_target="tpu_custom_call" | custom-call | tf_op jit(solution)/shard_map/step1/pallas_call | solution.py:109
  67.4 17.9 %all_to_all.21.refs_0_ = bf16[128,16,128]{2,1,0:T(8,128)(2,1)S(1)} all-to-all(bf16[128,16,128]{2,1,0:T(8,128)(2,1)S(1)} %bitcast.30), channel_id=1, replica_groups=mesh['patch'=32,'slab'=4] {'patch','slab'}, dimensions={0} | all-to-all | bytes 1048576 | tf_op jit(solution)/shard_map/all_to_all | solution.py:166
  85.3 1.9 %step2.1 = (bf16[32,4,16,128]{3,2,1,0:T(8,128)(2,1)S(1)}, bf16[16,128]{1,0:T(8,128)(2,1)S(1)}) custom-call(bf16[128,16,128]{2,1,0:T(8,128)(2,1)S(1)} %all_to_all.21.refs_0_, f32[4,16,128]{2,1,0:T(8,128)S(1)} %bitcast.26, bf16[16,128,128]{2,1,0:T(8,128)(2,1)S(1)} %copy-done.2, bf16[3,16,128]{2,1,0:T(8,128)(2,1)S(1)} %select_convert_fusion.refs_3_, ...), custom_call_target="tpu_custom_call" | custom-call | tf_op jit(solution)/shard_map/step2/pallas_call | solution.py:109
  87.2 17.9 %all_to_all.22.recv_ref = bf16[128,16,128]{2,1,0:T(8,128)(2,1)S(1)} all-to-all(bf16[128,16,128]{2,1,0:T(8,128)(2,1)S(1)} %bitcast.28), channel_id=1, replica_groups=mesh['patch'=32,'slab'=4] {'patch','slab'}, dimensions={0} | all-to-all | bytes 1048576 | tf_op jit(solution)/shard_map/all_to_all | solution.py:166
  105.1 0.3 last.1
  105.4 0.1 pad_maximum_fusion
  105.5 0.6 copy.17
  (13 shorter events, 0.1 us)
Async XLA Ops:
  0.0 29.9 %copy-start.4 = (f32[16,4,128]{2,1,0:T(4,128)S(1)}, f32[16,4,128]{2,1,0:T(4,128)}, u32[]{:S(2)}) copy-start(f32[16,4,128]{2,1,0:T(4,128)} %param.11) | copy-start | bytes 98308
  0.0 43.6 %copy-start.2 = (bf16[16,128,128]{2,1,0:T(8,128)(2,1)S(1)}, bf16[16,128,128]{2,1,0:T(8,128)(2,1)}, u32[]{:S(2)}) copy-start(bf16[16,128,128]{2,1,0:T(8,128)(2,1)} %sinv_ref.1) | copy-start | bytes 1572868
  2.4 1.0 copy-start.3
  3.7 9.2 %collective-permute-start = (bf16[1,128,128]{2,1,0:T(8,128)(2,1)S(1)}, bf16[1,128,128]{2,1,0:T(8,128)(2,1)S(1)}, u32[]{:S(2)}, u32[]{:S(2)}) collective-permute-start(bf16[1,128,128]{2,1,0:T(8,128)(2,1)S(1)} %get-tuple-element.19), channel_id=1, source_target_pairs={{0,1},{1,2},{2,3},{3,0},{4,5},{5,6},{6,7},{7,4},{8,9},{9,10},{10,1... | collective-permute-start | bytes 98312 | tf_op jit(solution)/shard_map/ppermute | solution.py:157
  6.2 8.7 %collective-permute-start.1 = (bf16[1,128,128]{2,1,0:T(8,128)(2,1)S(1)}, bf16[1,128,128]{2,1,0:T(8,128)(2,1)S(1)}, u32[]{:S(2)}, u32[]{:S(2)}) collective-permute-start(bf16[1,128,128]{2,1,0:T(8,128)(2,1)S(1)} %get-tuple-element.20), channel_id=1, source_target_pairs={{0,2},{1,3},{2,0},{3,1},{4,6},{5,7},{6,4},{7,5},{8,10},{9,11},{10,... | collective-permute-start | bytes 98312 | tf_op jit(solution)/shard_map/ppermute | solution.py:157
  9.5 5.4 %collective-permute-start.2 = (bf16[1,128,128]{2,1,0:T(8,128)(2,1)S(1)}, bf16[1,128,128]{2,1,0:T(8,128)(2,1)S(1)}, u32[]{:S(2)}, u32[]{:S(2)}) collective-permute-start(bf16[1,128,128]{2,1,0:T(8,128)(2,1)S(1)} %get-tuple-element.21), channel_id=1, source_target_pairs={{0,3},{1,0},{2,1},{3,2},{4,7},{5,4},{6,5},{7,6},{8,11},{9,8},{10,9... | collective-permute-start | bytes 98312 | tf_op jit(solution)/shard_map/ppermute | solution.py:157
  10.3 19.6 %collective-permute-start.3 = (bf16[3,128,128]{2,1,0:T(8,128)(2,1)S(1)}, bf16[3,128,128]{2,1,0:T(8,128)(2,1)S(1)}, u32[]{:S(2)}, u32[]{:S(2)}) collective-permute-start(bf16[3,128,128]{2,1,0:T(8,128)(2,1)S(1)} %get-tuple-element.22), channel_id=1, source_target_pairs={{0,1},{1,2},{2,3},{3,0},{4,5},{5,6},{6,7},{7,4},{8,9},{9,10},{10,1... | collective-permute-start | bytes 294920 | tf_op jit(solution)/shard_map/ppermute | solution.py:157
  11.0 18.9 %collective-permute-start.4 = (bf16[3,128,128]{2,1,0:T(8,128)(2,1)S(1)}, bf16[3,128,128]{2,1,0:T(8,128)(2,1)S(1)}, u32[]{:S(2)}, u32[]{:S(2)}) collective-permute-start(bf16[3,128,128]{2,1,0:T(8,128)(2,1)S(1)} %get-tuple-element.23), channel_id=1, source_target_pairs={{0,2},{1,3},{2,0},{3,1},{4,6},{5,7},{6,4},{7,5},{8,10},{9,11},{10,... | collective-permute-start | bytes 294920 | tf_op jit(solution)/shard_map/ppermute | solution.py:157
  12.9 17.0 %collective-permute-start.5 = (bf16[3,128,128]{2,1,0:T(8,128)(2,1)S(1)}, bf16[3,128,128]{2,1,0:T(8,128)(2,1)S(1)}, u32[]{:S(2)}, u32[]{:S(2)}) collective-permute-start(bf16[3,128,128]{2,1,0:T(8,128)(2,1)S(1)} %get-tuple-element.24), channel_id=1, source_target_pairs={{0,3},{1,0},{2,1},{3,2},{4,7},{5,4},{6,5},{7,6},{8,11},{9,8},{10,9... | collective-permute-start | bytes 294920 | tf_op jit(solution)/shard_map/ppermute | solution.py:157
  14.9 2.2 %copy-start = (bf16[16,8,128,128]{3,2,1,0:T(8,128)(2,1)S(1)}, bf16[16,8,128,128]{3,2,1,0:T(8,128)(2,1)}, u32[]{:S(2)}) copy-start(bf16[16,8,128,128]{3,2,1,0:T(8,128)(2,1)} %refs_9_.5) | copy-start | bytes 12582916
  19.3 24.3 %all-to-all-start = ((bf16[128,16,128]{2,1,0:T(8,128)(2,1)}), bf16[128,16,128]{2,1,0:T(8,128)(2,1)S(1)}, u32[]{:S(2)}, u32[]{:S(2)}) async-start(bf16[128,16,128]{2,1,0:T(8,128)(2,1)} %bitcast.4), calls=%async_computation | async-start | bytes 1048576 | tf_op jit(solution)/shard_map/all_to_all | solution.py:166
  43.6 2.2 %copy-start.1 = (bf16[16,8,128,128]{3,2,1,0:T(8,128)(2,1)S(1)}, bf16[16,8,128,128]{3,2,1,0:T(8,128)(2,1)}, u32[]{:S(2)}) copy-start(bf16[16,8,128,128]{3,2,1,0:T(8,128)(2,1)} %refs_9_.5) | copy-start | bytes 12582916

commit v2 on v1

v2 whole, which is shorter than its diff:
```python
import jax
import jax.numpy as jnp
from jax import lax
from jax.experimental import pallas as pl
from jax.experimental.pallas import tpu as pltpu
from jax.sharding import PartitionSpec as P

WMAX = 4
STEPS = 4
LAGS = STEPS - 1

BF16 = jnp.bfloat16
F32 = jnp.float32


def dot_f32(a, b, contract):
    return lax.dot_general(a, b, (contract, ((), ())), preferred_element_type=F32)


def spread(values, group, keep):
    out = jnp.where(keep, values, 0.0)
    lanes = out.shape[1]
    step = group
    while step < lanes:
        out = out + pltpu.roll(out, step, 1)
        step *= 2
    return out


def tapped(at, weights):
    found = jnp.where(at == 0, weights[0], 0.0)
    for tap in range(1, WMAX):
        found = jnp.where(at == tap, weights[tap], found)
    return found


def history_kernel(table_hbm, weight_hbm, hist_hbm, own_ref, *rest):
    send_refs, (table_ref, weight_ref, hist_ref, sems) = rest[:-4], rest[-4:]
    copies = [
        pltpu.make_async_copy(src, dst, sems.at[i])
        for i, (src, dst) in enumerate(
            [(table_hbm, table_ref), (weight_hbm, weight_ref), (hist_hbm, hist_ref)]
        )
    ]
    for copy in copies:
        copy.start()
    patches, pairs = table_ref.shape[1:]
    _, slab_len, src = hist_ref.shape
    slabs = len(send_refs) + 1
    local = pairs // slabs
    slab_id = lax.axis_index("slab")
    lane = lax.broadcasted_iota(jnp.int32, (patches, src), 1)
    turn = lax.rem(src - slab_id * local, src)

    def widen(x):
        return pltpu.roll(jnp.concatenate([x.astype(F32)] * STEPS, axis=1), turn, 1)

    copies[0].wait()
    copies[1].wait()
    first, band = widen(table_ref[1]), widen(table_ref[2])
    wide = weight_ref[...].astype(F32)
    weights = [jnp.where(band > tap, widen(wide[:, tap, :]), 0.0) for tap in range(WMAX)]
    start = first - (lane // pairs + 1 + slab_id * slab_len).astype(F32)
    h = lax.broadcasted_iota(jnp.int32, (slab_len, src), 0).astype(F32)
    copies[2].wait()
    for p in range(0, patches, 2):
        parts = []
        for q in (p, p + 1):
            table = tapped(h - start[q : q + 1], [w[q : q + 1] for w in weights])
            parts.append(dot_f32(table.astype(BF16), hist_ref[q], ((0,), (0,))))
        at = pl.ds(p * local, 2 * local)
        for n in range(STEPS):
            for s in range(slabs):
                lo = n * pairs + s * local
                both = jnp.concatenate([part[lo : lo + local] for part in parts], axis=0)
                if s == 0:
                    own_ref[n, at, :] = both
                else:
                    send_refs[s - 1][n, at, :] = both.astype(BF16)


def prepare_kernel(table_ref, weight_ref, coup_ref, lag_ref, obs_ref, out_ref, sems):
    copies = [
        pltpu.make_async_copy(coup_ref.at[p], out_ref.at[p], sems.at[p])
        for p in range(coup_ref.shape[0])
    ]
    for copy in copies:
        copy.start()
    patches, pairs = table_ref.shape[1:]
    local, src = coup_ref.shape[1:3]
    slab_id = lax.axis_index("slab")
    core = lax.rem(lax.axis_index("patch"), 2)
    lane = lax.broadcasted_iota(jnp.int32, (patches, src), 1)
    row = lax.broadcasted_iota(jnp.int32, (patches, src), 0)
    mine = lane // local == slab_id
    blank = jnp.zeros((patches, src - pairs), F32)

    def widen(x):
        return spread(jnp.concatenate([x.astype(F32), blank], axis=1), local, mine)

    first, band = widen(table_ref[1]), widen(table_ref[2])
    obs = table_ref[0]
    obs = (obs // patches % 2 ^ core) * (patches * (lax.axis_size("patch") // 2)) + (
        obs // (2 * patches) * patches + obs % patches
    )
    diagonal = lane // local == row
    obs = jnp.sum(jnp.where(diagonal, widen(obs), 0.0), axis=0, keepdims=True)
    obs_ref[...] = jnp.broadcast_to(obs, obs_ref.shape).astype(jnp.int32)
    wide = weight_ref[...].astype(F32)
    weights = [jnp.where(band > tap, widen(wide[:, tap, :]), 0.0) for tap in range(WMAX)]
    lags = [jnp.where(diagonal, tapped(lag - first, weights), 0.0) for lag in range(1, STEPS)]
    lag_ref[...] = jnp.concatenate(lags, axis=0).astype(BF16)
    for copy in copies:
        copy.wait()


def field_of(driven, obs_ref, coup_ref, keep_ref, give_ref):
    rows, src = driven.shape
    patches = coup_ref.shape[0]
    local = rows // patches
    row_id = lax.broadcasted_iota(jnp.int32, (local, src), 0)
    coupled = []
    for p in range(patches):
        mine = driven[p * local : (p + 1) * local].astype(BF16)
        full = dot_f32(mine, coup_ref[p].reshape(local * src, src), ((1,), (1,)))
        out = full[:, :src]
        for k in range(1, local):
            out = jnp.where(row_id == k, full[:, k * src : (k + 1) * src], out)
        coupled.append(out)
    coupled = jnp.concatenate(coupled, axis=0).astype(BF16)
    half = keep_ref.shape[0]
    targets = lax.broadcasted_iota(jnp.int32, (2 * half, rows), 0)
    onehot = jnp.where(targets == obs_ref[0:1, :], 1.0, 0.0).astype(BF16)
    field = dot_f32(onehot, coupled, ((1,), (0,)))
    keep_ref[...] = field[:half]
    give_ref[...] = field[half:].astype(BF16)


def first_kernel(own_ref, a_ref, b_ref, c_ref, obs_ref, coup_ref, keep_ref, give_ref):
    driven = own_ref[0] + a_ref[0].astype(F32) + b_ref[0].astype(F32) + c_ref[0].astype(F32)
    field_of(driven, obs_ref, coup_ref, keep_ref, give_ref)


def join_kernel(keep_ref, got_ref, send_ref):
    blocks, slabs, patches, src = send_ref.shape
    total = (keep_ref[...] + got_ref[...].astype(F32)).astype(BF16).reshape(blocks, patches, src)
    for s in range(slabs):
        send_ref[:, s] = total


def amplitude_of(step, recv_ref, inc_ref, sinv_ref):
    sources, patches, src = recv_ref.shape
    total = jnp.sum(recv_ref[...].astype(F32), axis=0)
    drive = (inc_ref[:, step, :] - total).astype(BF16)
    row_id = lax.broadcasted_iota(jnp.int32, (patches, src), 0)
    amp = jnp.zeros((patches, src), F32)
    full = dot_f32(drive, sinv_ref[...].reshape(patches * src, src), ((1,), (1,)))
    for p in range(patches):
        amp = jnp.where(row_id == p, full[:, p * src : (p + 1) * src], amp)
    return amp.astype(BF16)


def step_kernel(step, recv_ref, inc_ref, sinv_ref, lag_ref, own_ref, a_ref, b_ref, c_ref, obs_ref, coup_ref, *rest):
    past_refs, (keep_ref, give_ref, amp_ref) = rest[:-3], rest[-3:]
    amp = amplitude_of(step, recv_ref, inc_ref, sinv_ref)
    amp_ref[...] = amp
    past = jnp.concatenate([amp] + [r[...] for r in past_refs], axis=0)
    driven = (
        own_ref[step + 1]
        + a_ref[step + 1].astype(F32)
        + b_ref[step + 1].astype(F32)
        + c_ref[step + 1].astype(F32)
        + dot_f32(lag_ref[: past.shape[0], :], past, ((0,), (0,)))
    )
    field_of(driven, obs_ref, coup_ref, keep_ref, give_ref)


def last_kernel(recv_ref, inc_ref, sinv_ref, *rest):
    past_refs, out_ref = rest[:-1], rest[-1]
    amp = amplitude_of(STEPS - 1, recv_ref, inc_ref, sinv_ref)
    for step, value in enumerate([r[...] for r in past_refs] + [amp]):
        out_ref[:, step, :] = value


def call(kernel, name, outs, args, spaces=None, scratch=(), cost=None):
    vmem = pl.BlockSpec(memory_space=pltpu.VMEM)
    spaces = spaces or [pltpu.VMEM] * len(args)
    return pl.pallas_call(
        kernel,
        name=name,
        out_shape=outs,
        in_specs=[pl.BlockSpec(memory_space=space) for space in spaces],
        out_specs=jax.tree.map(lambda _: vmem, outs),
        scratch_shapes=scratch,
        cost_estimate=cost,
        compiler_params=pltpu.CompilerParams(vmem_limit_bytes=24 * 2**20),
    )(*args)


def on_device(history, interp_weights, pair_table, coupling, self_inverse, incident):
    patches, slab_len, src = history.shape
    local = coupling.shape[1]
    slabs = lax.axis_size("slab")
    blocks = lax.axis_size("patch") // 2
    rows = patches * local
    half = blocks * patches
    cores = [(i, i ^ 1) for i in range(2 * blocks)]
    groups = [
        [(2 * b + core) * slabs + z for b in range(blocks) for z in range(slabs)] for core in range(2)
    ]

    def exchange(keep, give):
        got = lax.ppermute(give, "patch", cores)
        send = call(join_kernel, "join", shape((blocks, slabs, patches, src), BF16), [keep, got])
        send = send.reshape(blocks * slabs, patches, src)
        return lax.all_to_all(
            send, ("patch", "slab"), 0, 0, axis_index_groups=groups, tiled=True
        )

    shape = jax.ShapeDtypeStruct
    field = [shape((half, src), F32), shape((half, src), BF16)]
    table = pair_table.transpose(2, 0, 1)
    weight = interp_weights.transpose(0, 2, 1)
    own, *sends = call(
        history_kernel,
        "history",
        [shape((STEPS, rows, src), F32)] + [shape((STEPS, rows, src), BF16)] * (slabs - 1),
        [table, weight, history],
        spaces=[pltpu.HBM] * 3,
        scratch=[
            pltpu.VMEM(table.shape, jnp.int32),
            pltpu.VMEM(weight.shape, BF16),
            pltpu.VMEM(history.shape, BF16),
            pltpu.SemaphoreType.DMA((3,)),
        ],
    )
    parts = [
        lax.ppermute(x, "slab", [(z, (z + s + 1) % slabs) for z in range(slabs)])
        for s, x in enumerate(sends)
    ]
    lag_table, obs, near = call(
        prepare_kernel,
        "prepare",
        [
            shape((LAGS * patches, rows), BF16),
            shape((8, rows), jnp.int32),
            shape(coupling.shape, BF16),
        ],
        [table, weight, coupling],
        spaces=[pltpu.VMEM, pltpu.VMEM, pltpu.HBM],
        scratch=[pltpu.SemaphoreType.DMA((patches,))],
        cost=pl.CostEstimate(flops=0, bytes_accessed=4 * coupling.size, transcendentals=0),
    )
    keep, give = call(first_kernel, "first", field, [own, *parts, obs, near])
    amps = []
    for step in range(STEPS):
        recv = exchange(keep, give)
        if step == STEPS - 1:
            return call(
                last_kernel,
                "last",
                shape((patches, STEPS, src), BF16),
                [recv, incident, self_inverse, *amps],
            )

        def body(*refs, step=step):
            step_kernel(step, *refs)

        keep, give, amp = call(
            body,
            f"step{step}",
            field + [shape((patches, src), BF16)],
            [recv, incident, self_inverse, lag_table, own, *parts, obs, coupling, *amps[::-1]],
        )
        amps.append(amp)


def solution(mesh):
    in_specs = (
        P("patch", "slab", None),
        P("patch", None, None),
        P("patch", None, None),
        P("patch", "slab", None, None),
        P("patch", None, None),
        P("patch", None, None),
    )
    out_specs = P("patch", None, None)
    return jax.shard_map(
        on_device, mesh=mesh, in_specs=in_specs, out_specs=out_specs, check_vma=False
    )
```

time: 107 us -> 95.5 us (0.89)
  blocking collectives: 53.6 us -> 62.1 us
  waiting for transfers between devices: 13.7 us -> 5.59 us
  starting transfers between devices: 20.3 us -> 13.2 us
  other arithmetic: 2.96 us -> 0 us
  local copies, waits for them, and re-layouts: 6.79 us -> 4.6 us
    all_to_all x1 -> x0, waiting for transfers between devices: 13.7 us -> none  [on_device(): lax.all_to_all(send.reshape(blocks * slabs, patches, src), ('patch', 'sla...]
    all_to_all x1 -> x0, starting transfers between devices: 10.5 us -> none  [on_device(): lax.all_to_all(send.reshape(blocks * slabs, patches, src), ('patch', 'sla...]
    all_to_all x3 -> x4, blocking collectives: 53.6 us -> 62.1 us  [exchange(): lax.all_to_all(send, ('patch', 'slab'), 0, 0, axis_index_groups=groups, t...]
    ppermute x6 -> x7, waiting for transfers between devices: 0.02 us -> 5.59 us  [the longest x4 3.61 us: exchange(): got = lax.ppermute(give, 'patch', cores)]
    ppermute x6 -> x7, starting transfers between devices: 9.77 us -> 13.2 us  [the longest x4 6.64 us: exchange(): got = lax.ppermute(give, 'patch', cores)]
    pallas_call x6 -> x11, Pallas kernels: 8.62 us -> 9.36 us  [call(): pl.pallas_call(kernel, name=name, out_shape=outs, in_specs=[pl.BlockSpec(...]
    unnamed x11 -> x14, local copies, waits for them, and re-layouts: 5.34 us -> 4.6 us
  transfers between devices with their start and end apart: 7 -> 7, of which waited for: 1 -> 5; matrix products, arithmetic and copies ran while one was open for 1% -> 0% of each run, Pallas kernels for 2% -> 1%
where the time goes in v2:
time: 95.5 us; the launch traced here: 94.9 us
  blocking collectives  62.1 us (65%)
  starting transfers between devices  13.2 us (14%)
  Pallas kernels  9.36 us (10%)
  waiting for transfers between devices  5.59 us (6%)
  local copies, waits for them, and re-layouts  4.6 us (5%)
    all_to_all x4, blocking collectives, exchange(): lax.all_to_all(send, ('patch', 'slab'), 0, 0, axis_index_groups=groups, t...  62.1 us
    pallas_call x11, Pallas kernels, call(): pl.pallas_call(kernel, name=name, out_shape=outs, in_specs=[pl.BlockSpec(...  9.36 us
    ppermute x4, starting transfers between devices, exchange(): got = lax.ppermute(give, 'patch', cores)  6.64 us
    ppermute x3, starting transfers between devices, on_device(): lax.ppermute(x, 'slab', [(z, (z + s + 1) % slabs) for z in range(slabs)])  6.56 us
    unnamed x14, local copies, waits for them, and re-layouts  4.6 us
    ppermute x4, waiting for transfers between devices, exchange(): got = lax.ppermute(give, 'patch', cores)  3.61 us
    ppermute x3, waiting for transfers between devices, on_device(): lax.ppermute(x, 'slab', [(z, (z + s + 1) % slabs) for z in range(slabs)])  1.98 us
  transfers between devices with their start and end apart: 7, of which 5 were waited for; matrix products, arithmetic and copies ran while one was open for 0% of the time, Pallas kernels for 1%

profile of v2, /device:TPU:1, one launch (start us, length us, event | category | flops | bytes accessed | tf_op | source)
XLA Modules:
  0.0 94.9 jit_solution(30690125196591665)
XLA Ops:
  0.0 0.0 copy-start.4
  0.0 0.9 copy-done.4
  1.0 0.0 copy-start.5
  1.0 0.7 copy-done.5
  1.7 0.0 copy-start.6
  1.7 0.7 copy-done.6
  2.4 0.7 history.1
  3.1 2.5 %collective-permute-start = (bf16[4,128,128]{2,1,0:T(8,128)(2,1)S(1)}, bf16[4,128,128]{2,1,0:T(8,128)(2,1)S(1)}, u32[]{:S(2)}, u32[]{:S(2)}) collective-permute-start(bf16[4,128,128]{2,1,0:T(8,128)(2,1)S(1)} %get-tuple-element.24), channel_id=1, source_target_pairs={{0,1},{1,2},{2,3},{3,0},{4,5},{5,6},{6,7},{7,4},{8,9},{9,10},{10,1... | collective-permute-start | bytes 393224 | tf_op jit(solution)/shard_map/ppermute | solution.py:238
  5.6 3.3 %collective-permute-start.1 = (bf16[4,128,128]{2,1,0:T(8,128)(2,1)S(1)}, bf16[4,128,128]{2,1,0:T(8,128)(2,1)S(1)}, u32[]{:S(2)}, u32[]{:S(2)}) collective-permute-start(bf16[4,128,128]{2,1,0:T(8,128)(2,1)S(1)} %get-tuple-element.25), channel_id=1, source_target_pairs={{0,2},{1,3},{2,0},{3,1},{4,6},{5,7},{6,4},{7,5},{8,10},{9,11},{10,... | collective-permute-start | bytes 393224 | tf_op jit(solution)/shard_map/ppermute | solution.py:238
  8.9 0.7 collective-permute-start.2
  9.6 0.0 copy-start
  9.6 2.2 %copy-done = bf16[16,8,128,128]{3,2,1,0:T(8,128)(2,1)S(1)} copy-done((bf16[16,8,128,128]{3,2,1,0:T(8,128)(2,1)S(1)}, bf16[16,8,128,128]{3,2,1,0:T(8,128)(2,1)}, u32[]{:S(2)}) %copy-start) | copy-done | bytes 4194328
  11.8 0.0 copy-start.1
  11.8 0.0 copy-start.2
  11.8 0.0 copy-start.3
  11.8 0.8 prepare.1
  12.6 0.0 collective-permute-done.a_ref.refs_5_
  12.7 2.0 %collective-permute-done.1.b_ref.refs_6_ = bf16[4,128,128]{2,1,0:T(8,128)(2,1)S(1)} collective-permute-done((bf16[4,128,128]{2,1,0:T(8,128)(2,1)S(1)}, bf16[4,128,128]{2,1,0:T(8,128)(2,1)S(1)}, u32[]{:S(2)}, u32[]{:S(2)}) %collective-permute-start.1) | collective-permute-done | bytes 131104 | tf_op jit(solution)/shard_map/ppermute | solution.py:238
  14.6 0.0 collective-permute-done.2.c_ref.refs_7_
  14.6 1.4 %first.1 = (f32[256,128]{1,0:T(8,128)S(1)}, bf16[256,128]{1,0:T(8,128)(2,1)S(1)}) custom-call(f32[4,128,128]{2,1,0:T(8,128)S(1)} %get-tuple-element.23.own_ref.refs_4_, bf16[4,128,128]{2,1,0:T(8,128)(2,1)S(1)} %collective-permute-done.a_ref.refs_5_, bf16[4,128,128]{2,1,0:T(8,128)(2,1)S(1)} %collective-permute-done.1.b_ref.refs_6_, ...), custom_call_target="tpu_custom_call" | custom-call | tf_op jit(solution)/shard_map/first/pallas_call | solution.py:188
  16.1 1.6 %collective-permute-start.3 = (bf16[256,128]{1,0:T(8,128)(2,1)S(1)}, bf16[256,128]{1,0:T(8,128)(2,1)S(1)}, u32[]{:S(2)}, u32[]{:S(2)}) collective-permute-start(bf16[256,128]{1,0:T(8,128)(2,1)S(1)} %get-tuple-element.30), channel_id=1, source_target_pairs={{0,4},{4,0},{8,12},{12,8},{16,20},{20,16},{24,28},{28,24},{32,36},... | collective-permute-start | bytes 196616 | tf_op jit(solution)/shard_map/ppermute | solution.py:213
  17.7 0.9 collective-permute-done.3.got_ref
  18.6 19.0 %all_to_all.20.refs_0_ = bf16[64,16,128]{2,1,0:T(8,128)(2,1)S(1)} all-to-all(bf16[64,16,128]{2,1,0:T(8,128)(2,1)S(1)} %bitcast.6), channel_id=1, replica_groups={{0,1,2,3,8,9,10,11,16,17,18,19,24,25,26,27,32,33,34,35,40,41,42,43,48,4..., dimensions={0} | all-to-all | bytes 524288 | tf_op jit(solution)/shard_map/all_to_all | solution.py:216
  37.7 0.0 copy-done.1
  37.7 0.0 copy-done.2
  37.7 0.0 copy-done.3
  37.7 1.8 %step0.1 = (f32[256,128]{1,0:T(8,128)S(1)}, bf16[256,128]{1,0:T(8,128)(2,1)S(1)}, bf16[16,128]{1,0:T(8,128)(2,1)S(1)}) custom-call(bf16[64,16,128]{2,1,0:T(8,128)(2,1)S(1)} %all_to_all.20.refs_0_, f32[16,4,128]{2,1,0:T(4,128)S(1)} %copy-done.3, bf16[16,128,128]{2,1,0:T(8,128)(2,1)S(1)} %copy-done.2, bf16[48,128]{1,0:T(8,128)(2,1)S(1)} %get-tuple-element.31.refs_3_, ...), custom_call_target="tpu_custom_call" | custom-call | tf_op jit(solution)/shard_map/step0/pallas_call | solution.py:188
  39.5 1.7 %collective-permute-start.4 = (bf16[256,128]{1,0:T(8,128)(2,1)S(1)}, bf16[256,128]{1,0:T(8,128)(2,1)S(1)}, u32[]{:S(2)}, u32[]{:S(2)}) collective-permute-start(bf16[256,128]{1,0:T(8,128)(2,1)S(1)} %get-tuple-element.33), channel_id=1, source_target_pairs={{0,4},{4,0},{8,12},{12,8},{16,20},{20,16},{24,28},{28,24},{32,36},... | collective-permute-start | bytes 196616 | tf_op jit(solution)/shard_map/ppermute | solution.py:213
  41.2 0.9 collective-permute-done.4.got_ref
  42.1 14.3 %all_to_all.21.refs_0_ = bf16[64,16,128]{2,1,0:T(8,128)(2,1)S(1)} all-to-all(bf16[64,16,128]{2,1,0:T(8,128)(2,1)S(1)} %bitcast.7), channel_id=1, replica_groups={{0,1,2,3,8,9,10,11,16,17,18,19,24,25,26,27,32,33,34,35,40,41,42,43,48,4..., dimensions={0} | all-to-all | bytes 524288 | tf_op jit(solution)/shard_map/all_to_all | solution.py:216
  56.4 1.8 %step1.1 = (f32[256,128]{1,0:T(8,128)S(1)}, bf16[256,128]{1,0:T(8,128)(2,1)S(1)}, bf16[16,128]{1,0:T(8,128)(2,1)S(1)}) custom-call(bf16[64,16,128]{2,1,0:T(8,128)(2,1)S(1)} %all_to_all.21.refs_0_, f32[16,4,128]{2,1,0:T(4,128)S(1)} %copy-done.3, bf16[16,128,128]{2,1,0:T(8,128)(2,1)S(1)} %copy-done.2, bf16[48,128]{1,0:T(8,128)(2,1)S(1)} %get-tuple-element.31.refs_3_, ...), custom_call_target="tpu_custom_call" | custom-call | tf_op jit(solution)/shard_map/step1/pallas_call | solution.py:188
  58.3 1.7 %collective-permute-start.5 = (bf16[256,128]{1,0:T(8,128)(2,1)S(1)}, bf16[256,128]{1,0:T(8,128)(2,1)S(1)}, u32[]{:S(2)}, u32[]{:S(2)}) collective-permute-start(bf16[256,128]{1,0:T(8,128)(2,1)S(1)} %get-tuple-element.36), channel_id=1, source_target_pairs={{0,4},{4,0},{8,12},{12,8},{16,20},{20,16},{24,28},{28,24},{32,36},... | collective-permute-start | bytes 196616 | tf_op jit(solution)/shard_map/ppermute | solution.py:213
  59.9 0.9 collective-permute-done.5.got_ref
  60.9 14.3 %all_to_all.22.refs_0_ = bf16[64,16,128]{2,1,0:T(8,128)(2,1)S(1)} all-to-all(bf16[64,16,128]{2,1,0:T(8,128)(2,1)S(1)} %bitcast.8), channel_id=1, replica_groups={{0,1,2,3,8,9,10,11,16,17,18,19,24,25,26,27,32,33,34,35,40,41,42,43,48,4..., dimensions={0} | all-to-all | bytes 524288 | tf_op jit(solution)/shard_map/all_to_all | solution.py:216
  75.2 1.8 %step2.1 = (f32[256,128]{1,0:T(8,128)S(1)}, bf16[256,128]{1,0:T(8,128)(2,1)S(1)}, bf16[16,128]{1,0:T(8,128)(2,1)S(1)}) custom-call(bf16[64,16,128]{2,1,0:T(8,128)(2,1)S(1)} %all_to_all.22.refs_0_, f32[16,4,128]{2,1,0:T(4,128)S(1)} %copy-done.3, bf16[16,128,128]{2,1,0:T(8,128)(2,1)S(1)} %copy-done.2, bf16[48,128]{1,0:T(8,128)(2,1)S(1)} %get-tuple-element.31.refs_3_, ...), custom_call_target="tpu_custom_call" | custom-call | tf_op jit(solution)/shard_map/step2/pallas_call | solution.py:188
  77.0 1.7 %collective-permute-start.6 = (bf16[256,128]{1,0:T(8,128)(2,1)S(1)}, bf16[256,128]{1,0:T(8,128)(2,1)S(1)}, u32[]{:S(2)}, u32[]{:S(2)}) collective-permute-start(bf16[256,128]{1,0:T(8,128)(2,1)S(1)} %get-tuple-element.39), channel_id=1, source_target_pairs={{0,4},{4,0},{8,12},{12,8},{16,20},{20,16},{24,28},{28,24},{32,36},... | collective-permute-start | bytes 196616 | tf_op jit(solution)/shard_map/ppermute | solution.py:213
  78.7 0.9 collective-permute-done.6.got_ref
  79.6 14.3 %all_to_all.23.recv_ref = bf16[64,16,128]{2,1,0:T(8,128)(2,1)S(1)} all-to-all(bf16[64,16,128]{2,1,0:T(8,128)(2,1)S(1)} %bitcast.9), channel_id=1, replica_groups={{0,1,2,3,8,9,10,11,16,17,18,19,24,25,26,27,32,33,34,35,40,41,42,43,48,4..., dimensions={0} | all-to-all | bytes 524288 | tf_op jit(solution)/shard_map/all_to_all | solution.py:216
  94.0 0.9 last.1
  (4 shorter events, 0.1 us)
Async XLA Ops:
  0.0 0.9 %copy-start.4 = (bf16[16,64,128]{2,1,0:T(8,128)(2,1)S(1)}, bf16[16,64,128]{2,1,0:T(8,128)(2,1)}, u32[]{:S(2)}) copy-start(bf16[16,64,128]{2,1,0:T(8,128)(2,1)} %hist_hbm.1) | copy-start | bytes 786436
  1.0 0.7 copy-start.5
  1.7 0.7 copy-start.6
  3.1 9.6 %collective-permute-start = (bf16[4,128,128]{2,1,0:T(8,128)(2,1)S(1)}, bf16[4,128,128]{2,1,0:T(8,128)(2,1)S(1)}, u32[]{:S(2)}, u32[]{:S(2)}) collective-permute-start(bf16[4,128,128]{2,1,0:T(8,128)(2,1)S(1)} %get-tuple-element.24), channel_id=1, source_target_pairs={{0,1},{1,2},{2,3},{3,0},{4,5},{5,6},{6,7},{7,4},{8,9},{9,10},{10,1... | collective-permute-start | bytes 393224 | tf_op jit(solution)/shard_map/ppermute | solution.py:238
  5.6 9.0 %collective-permute-start.1 = (bf16[4,128,128]{2,1,0:T(8,128)(2,1)S(1)}, bf16[4,128,128]{2,1,0:T(8,128)(2,1)S(1)}, u32[]{:S(2)}, u32[]{:S(2)}) collective-permute-start(bf16[4,128,128]{2,1,0:T(8,128)(2,1)S(1)} %get-tuple-element.25), channel_id=1, source_target_pairs={{0,2},{1,3},{2,0},{3,1},{4,6},{5,7},{6,4},{7,5},{8,10},{9,11},{10,... | collective-permute-start | bytes 393224 | tf_op jit(solution)/shard_map/ppermute | solution.py:238
  8.9 5.7 %collective-permute-start.2 = (bf16[4,128,128]{2,1,0:T(8,128)(2,1)S(1)}, bf16[4,128,128]{2,1,0:T(8,128)(2,1)S(1)}, u32[]{:S(2)}, u32[]{:S(2)}) collective-permute-start(bf16[4,128,128]{2,1,0:T(8,128)(2,1)S(1)} %get-tuple-element.26), channel_id=1, source_target_pairs={{0,3},{1,0},{2,1},{3,2},{4,7},{5,4},{6,5},{7,6},{8,11},{9,8},{10,9... | collective-permute-start | bytes 393224 | tf_op jit(solution)/shard_map/ppermute | solution.py:238
  9.6 2.2 %copy-start = (bf16[16,8,128,128]{3,2,1,0:T(8,128)(2,1)S(1)}, bf16[16,8,128,128]{3,2,1,0:T(8,128)(2,1)}, u32[]{:S(2)}) copy-start(bf16[16,8,128,128]{3,2,1,0:T(8,128)(2,1)} %refs_9_.5) | copy-start | bytes 12582916
  11.8 25.8 %copy-start.1 = (bf16[16,8,128,128]{3,2,1,0:T(8,128)(2,1)S(1)}, bf16[16,8,128,128]{3,2,1,0:T(8,128)(2,1)}, u32[]{:S(2)}) copy-start(bf16[16,8,128,128]{3,2,1,0:T(8,128)(2,1)} %refs_9_.5) | copy-start | bytes 12582916
  11.8 25.8 %copy-start.2 = (bf16[16,128,128]{2,1,0:T(8,128)(2,1)S(1)}, bf16[16,128,128]{2,1,0:T(8,128)(2,1)}, u32[]{:S(2)}) copy-start(bf16[16,128,128]{2,1,0:T(8,128)(2,1)} %sinv_ref.1) | copy-start | bytes 1572868
  11.8 25.8 %copy-start.3 = (f32[16,4,128]{2,1,0:T(4,128)S(1)}, f32[16,4,128]{2,1,0:T(4,128)}, u32[]{:S(2)}) copy-start(f32[16,4,128]{2,1,0:T(4,128)} %inc_ref.1) | copy-start | bytes 98308
  16.1 2.5 %collective-permute-start.3 = (bf16[256,128]{1,0:T(8,128)(2,1)S(1)}, bf16[256,128]{1,0:T(8,128)(2,1)S(1)}, u32[]{:S(2)}, u32[]{:S(2)}) collective-permute-start(bf16[256,128]{1,0:T(8,128)(2,1)S(1)} %get-tuple-element.30), channel_id=1, source_target_pairs={{0,4},{4,0},{8,12},{12,8},{16,20},{20,16},{24,28},{28,24},{32,36},... | collective-permute-start | bytes 196616 | tf_op jit(solution)/shard_map/ppermute | solution.py:213
  39.5 2.6 %collective-permute-start.4 = (bf16[256,128]{1,0:T(8,128)(2,1)S(1)}, bf16[256,128]{1,0:T(8,128)(2,1)S(1)}, u32[]{:S(2)}, u32[]{:S(2)}) collective-permute-start(bf16[256,128]{1,0:T(8,128)(2,1)S(1)} %get-tuple-element.33), channel_id=1, source_target_pairs={{0,4},{4,0},{8,12},{12,8},{16,20},{20,16},{24,28},{28,24},{32,36},... | collective-permute-start | bytes 196616 | tf_op jit(solution)/shard_map/ppermute | solution.py:213
  58.3 2.6 %collective-permute-start.5 = (bf16[256,128]{1,0:T(8,128)(2,1)S(1)}, bf16[256,128]{1,0:T(8,128)(2,1)S(1)}, u32[]{:S(2)}, u32[]{:S(2)}) collective-permute-start(bf16[256,128]{1,0:T(8,128)(2,1)S(1)} %get-tuple-element.36), channel_id=1, source_target_pairs={{0,4},{4,0},{8,12},{12,8},{16,20},{20,16},{24,28},{28,24},{32,36},... | collective-permute-start | bytes 196616 | tf_op jit(solution)/shard_map/ppermute | solution.py:213
  77.0 2.6 %collective-permute-start.6 = (bf16[256,128]{1,0:T(8,128)(2,1)S(1)}, bf16[256,128]{1,0:T(8,128)(2,1)S(1)}, u32[]{:S(2)}, u32[]{:S(2)}) collective-permute-start(bf16[256,128]{1,0:T(8,128)(2,1)S(1)} %get-tuple-element.39), channel_id=1, source_target_pairs={{0,4},{4,0},{8,12},{12,8},{16,20},{20,16},{24,28},{28,24},{32,36},... | collective-permute-start | bytes 196616 | tf_op jit(solution)/shard_map/ppermute | solution.py:213

commit v3 on v2

--- a/solution.py
+++ b/solution.py
@@ -1,3 +1,5 @@
+import functools
+
 import jax
 import jax.numpy as jnp
 from jax import lax
@@ -34,16 +36,18 @@
     return found
 
 
+def start_copies(pairs, sems):
+    copies = [pltpu.make_async_copy(src, dst, sems.at[i]) for i, (src, dst) in enumerate(pairs)]
+    for copy in copies:
+        copy.start()
+    return copies
+
+
 def history_kernel(table_hbm, weight_hbm, hist_hbm, own_ref, *rest):
     send_refs, (table_ref, weight_ref, hist_ref, sems) = rest[:-4], rest[-4:]
-    copies = [
-        pltpu.make_async_copy(src, dst, sems.at[i])
-        for i, (src, dst) in enumerate(
-            [(table_hbm, table_ref), (weight_hbm, weight_ref), (hist_hbm, hist_ref)]
-        )
-    ]
-    for copy in copies:
-        copy.start()
+    copies = start_copies(
+        [(table_hbm, table_ref), (weight_hbm, weight_ref), (hist_hbm, hist_ref)], sems
+    )
     patches, pairs = table_ref.shape[1:]
     _, slab_len, src = hist_ref.shape
     slabs = len(send_refs) + 1
@@ -79,13 +83,16 @@
                     send_refs[s - 1][n, at, :] = both.astype(BF16)
 
 
-def prepare_kernel(table_ref, weight_ref, coup_ref, lag_ref, obs_ref, out_ref, sems):
-    copies = [
-        pltpu.make_async_copy(coup_ref.at[p], out_ref.at[p], sems.at[p])
-        for p in range(coup_ref.shape[0])
-    ]
-    for copy in copies:
-        copy.start()
+def prepare_kernel(
+    table_hbm, weight_hbm, coup_ref, lag_ref, obs_ref, out_ref, table_ref, weight_ref, sems
+):
+    copies = start_copies(
+        [(table_hbm, table_ref), (weight_hbm, weight_ref)]
+        + [(coup_ref.at[p], out_ref.at[p]) for p in range(coup_ref.shape[0])],
+        sems,
+    )
+    copies[0].wait()
+    copies[1].wait()
     patches, pairs = table_ref.shape[1:]
     local, src = coup_ref.shape[1:3]
     slab_id = lax.axis_index("slab")
@@ -110,7 +117,7 @@
     weights = [jnp.where(band > tap, widen(wide[:, tap, :]), 0.0) for tap in range(WMAX)]
     lags = [jnp.where(diagonal, tapped(lag - first, weights), 0.0) for lag in range(1, STEPS)]
     lag_ref[...] = jnp.concatenate(lags, axis=0).astype(BF16)
-    for copy in copies:
+    for copy in copies[2:]:
         copy.wait()
 
 
@@ -141,11 +148,12 @@
     field_of(driven, obs_ref, coup_ref, keep_ref, give_ref)
 
 
-def join_kernel(keep_ref, got_ref, send_ref):
-    blocks, slabs, patches, src = send_ref.shape
-    total = (keep_ref[...] + got_ref[...].astype(F32)).astype(BF16).reshape(blocks, patches, src)
-    for s in range(slabs):
-        send_ref[:, s] = total
+def join_kernel(orders, keep_ref, got_ref, send_ref, total_ref):
+    total = (keep_ref[...] + got_ref[...].astype(F32)).astype(BF16)
+    total_ref[...] = total.reshape(total_ref.shape)
+    core = lax.rem(lax.axis_index("patch"), 2)
+    for i, (even, odd) in enumerate(zip(*orders)):
+        send_ref[i] = total_ref[jnp.where(core == 0, even, odd)]
 
 
 def amplitude_of(step, recv_ref, inc_ref, sinv_ref):
@@ -182,19 +190,25 @@
         out_ref[:, step, :] = value
 
 
-def call(kernel, name, outs, args, spaces=None, scratch=(), cost=None):
+def call(kernel, name, outs, args, in_hbm=False, scratch=(), cost=None):
     vmem = pl.BlockSpec(memory_space=pltpu.VMEM)
-    spaces = spaces or [pltpu.VMEM] * len(args)
+    space = pltpu.HBM if in_hbm else pltpu.VMEM
+    if in_hbm:
+        args = [pltpu.with_memory_space_constraint(x, pltpu.HBM) for x in args]
     return pl.pallas_call(
         kernel,
         name=name,
         out_shape=outs,
-        in_specs=[pl.BlockSpec(memory_space=space) for space in spaces],
+        in_specs=[pl.BlockSpec(memory_space=space)] * len(args),
         out_specs=jax.tree.map(lambda _: vmem, outs),
         scratch_shapes=scratch,
         cost_estimate=cost,
         compiler_params=pltpu.CompilerParams(vmem_limit_bytes=24 * 2**20),
     )(*args)
+
+
+def around(n):
+    return [i ^ (i >> 1) for i in range(n)]
 
 
 def on_device(history, interp_weights, pair_table, coupling, self_inverse, incident):
@@ -205,14 +219,23 @@
     rows = patches * local
     half = blocks * patches
     cores = [(i, i ^ 1) for i in range(2 * blocks)]
-    groups = [
-        [(2 * b + core) * slabs + z for b in range(blocks) for z in range(slabs)] for core in range(2)
+    wide = next(n for n in range(1, blocks + 1) if n * n >= blocks)
+    chips = [
+        [(y * wide + x, z) for y in around(blocks // wide) for x in around(wide) for z in around(slabs)],
+        [(y * wide + x, z) for x in around(wide) for z in around(slabs) for y in around(blocks // wide)],
     ]
+    groups = [[(2 * b + core) * slabs + z for b, z in chips[core]] for core in range(2)]
+    orders = [[b for b, _ in chips[core]] for core in range(2)]
 
     def exchange(keep, give):
         got = lax.ppermute(give, "patch", cores)
-        send = call(join_kernel, "join", shape((blocks, slabs, patches, src), BF16), [keep, got])
-        send = send.reshape(blocks * slabs, patches, src)
+        send = call(
+            functools.partial(join_kernel, orders),
+            "join",
+            shape((blocks * slabs, patches, src), BF16),
+            [keep, got],
+            scratch=[pltpu.VMEM((blocks, patches, src), BF16)],
+        )
         return lax.all_to_all(
             send, ("patch", "slab"), 0, 0, axis_index_groups=groups, tiled=True
         )
@@ -226,7 +249,7 @@
         "history",
         [shape((STEPS, rows, src), F32)] + [shape((STEPS, rows, src), BF16)] * (slabs - 1),
         [table, weight, history],
-        spaces=[pltpu.HBM] * 3,
+        in_hbm=True,
         scratch=[
             pltpu.VMEM(table.shape, jnp.int32),
             pltpu.VMEM(weight.shape, BF16),
@@ -247,8 +270,12 @@
             shape(coupling.shape, BF16),
         ],
         [table, weight, coupling],
-        spaces=[pltpu.VMEM, pltpu.VMEM, pltpu.HBM],
-        scratch=[pltpu.SemaphoreType.DMA((patches,))],
+        in_hbm=True,
+        scratch=[
+            pltpu.VMEM(table.shape, jnp.int32),
+            pltpu.VMEM(weight.shape, BF16),
+            pltpu.SemaphoreType.DMA((2 + patches,)),
+        ],
         cost=pl.CostEstimate(flops=0, bytes_accessed=4 * coupling.size, transcendentals=0),
     )
     keep, give = call(first_kernel, "first", field, [own, *parts, obs, near])

time: 95.5 us -> 92.2 us (0.965)
  local copies, waits for them, and re-layouts: 4.6 us -> 0.01 us
  blocking collectives: 62.1 us -> 59.1 us
  Pallas kernels: 9.36 us -> 12.2 us
    unnamed x14 -> x6, local copies, waits for them, and re-layouts: 4.6 us -> 0.01 us
    all_to_all x4, blocking collectives: 62.1 us -> 59.1 us  [exchange(): lax.all_to_all(send, ('patch', 'slab'), 0, 0, axis_index_groups=groups, t...]
    pallas_call x11, Pallas kernels: 9.36 us -> 12.2 us  [call(): pl.pallas_call(kernel, name=name, out_shape=outs, in_specs=[pl.BlockSpec(...]
  transfers between devices with their start and end apart: 7 -> 7, of which waited for: 5 -> 5; matrix products, arithmetic and copies ran while one was open for 0% -> 0% of each run, Pallas kernels for 1% -> 3%
where the time goes in v3:
time: 92.2 us; the launch traced here: 91.4 us
  blocking collectives  59.1 us (64%)
  starting transfers between devices  14.1 us (15%)
  Pallas kernels  12.2 us (13%)
  waiting for transfers between devices  5.88 us (6%)
    all_to_all x4, blocking collectives, exchange(): lax.all_to_all(send, ('patch', 'slab'), 0, 0, axis_index_groups=groups, t...  59.1 us
    pallas_call x11, Pallas kernels, call(): pl.pallas_call(kernel, name=name, out_shape=outs, in_specs=[pl.BlockSpec(...  12.2 us
    ppermute x4, starting transfers between devices, exchange(): got = lax.ppermute(give, 'patch', cores)  7.52 us
    ppermute x3, starting transfers between devices, on_device(): lax.ppermute(x, 'slab', [(z, (z + s + 1) % slabs) for z in range(slabs)])  6.58 us
    ppermute x4, waiting for transfers between devices, exchange(): got = lax.ppermute(give, 'patch', cores)  3.61 us
    ppermute x3, waiting for transfers between devices, on_device(): lax.ppermute(x, 'slab', [(z, (z + s + 1) % slabs) for z in range(slabs)])  2.27 us
  transfers between devices with their start and end apart: 7, of which 5 were waited for; matrix products, arithmetic and copies ran while one was open for 0% of the time, Pallas kernels for 3%

profile of v3, /device:TPU:1, one launch (start us, length us, event | category | flops | bytes accessed | tf_op | source)
XLA Modules:
  0.0 91.4 jit_solution(6672680159434895927)
XLA Ops:
  0.0 1.4 %history.1 = (f32[4,128,128]{2,1,0:T(8,128)S(1)}, bf16[4,128,128]{2,1,0:T(8,128)(2,1)S(1)}, bf16[4,128,128]{2,1,0:T(8,128)(2,1)S(1)}, bf16[4,128,128]{2,1,0:T(8,128)(2,1)S(1)}) custom-call(s32[3,16,32]{2,1,0:T(8,128)} %bitcast.2, bf16[16,4,32]{2,1,0:T(4,128)(2,1)} %bitcast.4, bf16[16,64,128]{2,1,0:T(8,128)(2,1)} %hist_hbm.1), custom_call_target="tpu_custom_call" | custom-call | tf_op jit(solution)/shard_map/history/pallas_call | solution.py:198
  1.4 2.5 %collective-permute-start = (bf16[4,128,128]{2,1,0:T(8,128)(2,1)S(1)}, bf16[4,128,128]{2,1,0:T(8,128)(2,1)S(1)}, u32[]{:S(2)}, u32[]{:S(2)}) collective-permute-start(bf16[4,128,128]{2,1,0:T(8,128)(2,1)S(1)} %get-tuple-element.24), channel_id=1, source_target_pairs={{0,1},{1,2},{2,3},{3,0},{4,5},{5,6},{6,7},{7,4},{8,9},{9,10},{10,1... | collective-permute-start | bytes 393224 | tf_op jit(solution)/shard_map/ppermute | solution.py:261
  3.9 3.3 %collective-permute-start.1 = (bf16[4,128,128]{2,1,0:T(8,128)(2,1)S(1)}, bf16[4,128,128]{2,1,0:T(8,128)(2,1)S(1)}, u32[]{:S(2)}, u32[]{:S(2)}) collective-permute-start(bf16[4,128,128]{2,1,0:T(8,128)(2,1)S(1)} %get-tuple-element.25), channel_id=1, source_target_pairs={{0,2},{1,3},{2,0},{3,1},{4,6},{5,7},{6,4},{7,5},{8,10},{9,11},{10,... | collective-permute-start | bytes 393224 | tf_op jit(solution)/shard_map/ppermute | solution.py:261
  7.2 0.0 copy-start
  7.2 0.0 copy-start.1
  7.2 0.0 copy-start.2
  7.2 0.7 collective-permute-start.2
  8.0 2.7 %prepare.1 = (bf16[48,128]{1,0:T(8,128)(2,1)S(1)}, s32[8,128]{1,0:T(8,128)S(1)}, bf16[16,8,128,128]{3,2,1,0:T(8,128)(2,1)S(1)}) custom-call(s32[3,16,32]{2,1,0:T(8,128)} %bitcast.3, bf16[16,4,32]{2,1,0:T(4,128)(2,1)} %bitcast.5, bf16[16,8,128,128]{3,2,1,0:T(8,128)(2,1)} %refs_9_.5), custom_call_target="tpu_custom_call" | custom-call | bytes 8388608 | tf_op jit(solution)/shard_map/prepare/pallas_call | solution.py:198
  10.7 0.0 collective-permute-done.a_ref.refs_5_
  10.7 2.3 %collective-permute-done.1.b_ref.refs_6_ = bf16[4,128,128]{2,1,0:T(8,128)(2,1)S(1)} collective-permute-done((bf16[4,128,128]{2,1,0:T(8,128)(2,1)S(1)}, bf16[4,128,128]{2,1,0:T(8,128)(2,1)S(1)}, u32[]{:S(2)}, u32[]{:S(2)}) %collective-permute-start.1) | collective-permute-done | bytes 131104 | tf_op jit(solution)/shard_map/ppermute | solution.py:261
  12.9 0.0 collective-permute-done.2.c_ref.refs_7_
  13.0 1.4 %first.1 = (f32[256,128]{1,0:T(8,128)S(1)}, bf16[256,128]{1,0:T(8,128)(2,1)S(1)}) custom-call(f32[4,128,128]{2,1,0:T(8,128)S(1)} %get-tuple-element.23.own_ref.refs_4_, bf16[4,128,128]{2,1,0:T(8,128)(2,1)S(1)} %collective-permute-done.a_ref.refs_5_, bf16[4,128,128]{2,1,0:T(8,128)(2,1)S(1)} %collective-permute-done.1.b_ref.refs_6_, ...), custom_call_target="tpu_custom_call" | custom-call | tf_op jit(solution)/shard_map/first/pallas_call | solution.py:198
  14.4 1.6 %collective-permute-start.3 = (bf16[256,128]{1,0:T(8,128)(2,1)S(1)}, bf16[256,128]{1,0:T(8,128)(2,1)S(1)}, u32[]{:S(2)}, u32[]{:S(2)}) collective-permute-start(bf16[256,128]{1,0:T(8,128)(2,1)S(1)} %get-tuple-element.30), channel_id=1, source_target_pairs={{0,4},{4,0},{8,12},{12,8},{16,20},{20,16},{24,28},{28,24},{32,36},... | collective-permute-start | bytes 196616 | tf_op jit(solution)/shard_map/ppermute | solution.py:231
  16.0 0.9 collective-permute-done.3.got_ref
  16.9 0.1 join.4
  17.0 18.7 %all_to_all.20.refs_0_ = bf16[64,16,128]{2,1,0:T(8,128)(2,1)S(1)} all-to-all(bf16[64,16,128]{2,1,0:T(8,128)(2,1)S(1)} %join.4), channel_id=1, replica_groups={{0,1,3,2,8,9,11,10,24,25,27,26,16,17,19,18,32,33,35,34,40,41,43,42,56,5..., dimensions={0} | all-to-all | bytes 524288 | tf_op jit(solution)/shard_map/all_to_all | solution.py:239
  35.7 0.0 copy-done
  35.7 0.0 copy-done.1
  35.7 0.0 copy-done.2
  35.7 1.8 %step0.1 = (f32[256,128]{1,0:T(8,128)S(1)}, bf16[256,128]{1,0:T(8,128)(2,1)S(1)}, bf16[16,128]{1,0:T(8,128)(2,1)S(1)}) custom-call(bf16[64,16,128]{2,1,0:T(8,128)(2,1)S(1)} %all_to_all.20.refs_0_, f32[16,4,128]{2,1,0:T(4,128)S(1)} %copy-done.2, bf16[16,128,128]{2,1,0:T(8,128)(2,1)S(1)} %copy-done.1, bf16[48,128]{1,0:T(8,128)(2,1)S(1)} %get-tuple-element.31.refs_3_, ...), custom_call_target="tpu_custom_call" | custom-call | tf_op jit(solution)/shard_map/step0/pallas_call | solution.py:198
  37.5 2.0 %collective-permute-start.4 = (bf16[256,128]{1,0:T(8,128)(2,1)S(1)}, bf16[256,128]{1,0:T(8,128)(2,1)S(1)}, u32[]{:S(2)}, u32[]{:S(2)}) collective-permute-start(bf16[256,128]{1,0:T(8,128)(2,1)S(1)} %get-tuple-element.33), channel_id=1, source_target_pairs={{0,4},{4,0},{8,12},{12,8},{16,20},{20,16},{24,28},{28,24},{32,36},... | collective-permute-start | bytes 196616 | tf_op jit(solution)/shard_map/ppermute | solution.py:231
  39.5 0.9 collective-permute-done.4.got_ref
  40.4 0.1 join.5
  40.5 13.5 %all_to_all.21.refs_0_ = bf16[64,16,128]{2,1,0:T(8,128)(2,1)S(1)} all-to-all(bf16[64,16,128]{2,1,0:T(8,128)(2,1)S(1)} %join.5), channel_id=1, replica_groups={{0,1,3,2,8,9,11,10,24,25,27,26,16,17,19,18,32,33,35,34,40,41,43,42,56,5..., dimensions={0} | all-to-all | bytes 524288 | tf_op jit(solution)/shard_map/all_to_all | solution.py:239
  54.0 1.8 %step1.1 = (f32[256,128]{1,0:T(8,128)S(1)}, bf16[256,128]{1,0:T(8,128)(2,1)S(1)}, bf16[16,128]{1,0:T(8,128)(2,1)S(1)}) custom-call(bf16[64,16,128]{2,1,0:T(8,128)(2,1)S(1)} %all_to_all.21.refs_0_, f32[16,4,128]{2,1,0:T(4,128)S(1)} %copy-done.2, bf16[16,128,128]{2,1,0:T(8,128)(2,1)S(1)} %copy-done.1, bf16[48,128]{1,0:T(8,128)(2,1)S(1)} %get-tuple-element.31.refs_3_, ...), custom_call_target="tpu_custom_call" | custom-call | tf_op jit(solution)/shard_map/step1/pallas_call | solution.py:198
  55.8 2.0 %collective-permute-start.5 = (bf16[256,128]{1,0:T(8,128)(2,1)S(1)}, bf16[256,128]{1,0:T(8,128)(2,1)S(1)}, u32[]{:S(2)}, u32[]{:S(2)}) collective-permute-start(bf16[256,128]{1,0:T(8,128)(2,1)S(1)} %get-tuple-element.36), channel_id=1, source_target_pairs={{0,4},{4,0},{8,12},{12,8},{16,20},{20,16},{24,28},{28,24},{32,36},... | collective-permute-start | bytes 196616 | tf_op jit(solution)/shard_map/ppermute | solution.py:231
  57.8 0.9 collective-permute-done.5.got_ref
  58.7 0.1 join.6
  58.8 13.5 %all_to_all.22.refs_0_ = bf16[64,16,128]{2,1,0:T(8,128)(2,1)S(1)} all-to-all(bf16[64,16,128]{2,1,0:T(8,128)(2,1)S(1)} %join.6), channel_id=1, replica_groups={{0,1,3,2,8,9,11,10,24,25,27,26,16,17,19,18,32,33,35,34,40,41,43,42,56,5..., dimensions={0} | all-to-all | bytes 524288 | tf_op jit(solution)/shard_map/all_to_all | solution.py:239
  72.2 1.8 %step2.1 = (f32[256,128]{1,0:T(8,128)S(1)}, bf16[256,128]{1,0:T(8,128)(2,1)S(1)}, bf16[16,128]{1,0:T(8,128)(2,1)S(1)}) custom-call(bf16[64,16,128]{2,1,0:T(8,128)(2,1)S(1)} %all_to_all.22.refs_0_, f32[16,4,128]{2,1,0:T(4,128)S(1)} %copy-done.2, bf16[16,128,128]{2,1,0:T(8,128)(2,1)S(1)} %copy-done.1, bf16[48,128]{1,0:T(8,128)(2,1)S(1)} %get-tuple-element.31.refs_3_, ...), custom_call_target="tpu_custom_call" | custom-call | tf_op jit(solution)/shard_map/step2/pallas_call | solution.py:198
  74.1 2.0 %collective-permute-start.6 = (bf16[256,128]{1,0:T(8,128)(2,1)S(1)}, bf16[256,128]{1,0:T(8,128)(2,1)S(1)}, u32[]{:S(2)}, u32[]{:S(2)}) collective-permute-start(bf16[256,128]{1,0:T(8,128)(2,1)S(1)} %get-tuple-element.39), channel_id=1, source_target_pairs={{0,4},{4,0},{8,12},{12,8},{16,20},{20,16},{24,28},{28,24},{32,36},... | collective-permute-start | bytes 196616 | tf_op jit(solution)/shard_map/ppermute | solution.py:231
  76.0 0.9 collective-permute-done.6.got_ref
  76.9 0.1 join.7
  77.0 13.5 %all_to_all.23.recv_ref = bf16[64,16,128]{2,1,0:T(8,128)(2,1)S(1)} all-to-all(bf16[64,16,128]{2,1,0:T(8,128)(2,1)S(1)} %join.7), channel_id=1, replica_groups={{0,1,3,2,8,9,11,10,24,25,27,26,16,17,19,18,32,33,35,34,40,41,43,42,56,5..., dimensions={0} | all-to-all | bytes 524288 | tf_op jit(solution)/shard_map/all_to_all | solution.py:239
  90.5 0.9 %last.1 = bf16[16,4,128]{2,1,0:T(4,128)(2,1)} custom-call(bf16[64,16,128]{2,1,0:T(8,128)(2,1)S(1)} %all_to_all.23.recv_ref, f32[16,4,128]{2,1,0:T(4,128)S(1)} %copy-done.2, bf16[16,128,128]{2,1,0:T(8,128)(2,1)S(1)} %copy-done.1, bf16[16,128]{1,0:T(8,128)(2,1)S(1)} %get-tuple-element.34.refs_10_.refs_11_.rest_0_, ...), custom_call_target="tpu_custom_call" | custom-call | tf_op jit(solution)/shard_map/last/pallas_call | solution.py:198
Async XLA Ops:
  1.4 9.3 %collective-permute-start = (bf16[4,128,128]{2,1,0:T(8,128)(2,1)S(1)}, bf16[4,128,128]{2,1,0:T(8,128)(2,1)S(1)}, u32[]{:S(2)}, u32[]{:S(2)}) collective-permute-start(bf16[4,128,128]{2,1,0:T(8,128)(2,1)S(1)} %get-tuple-element.24), channel_id=1, source_target_pairs={{0,1},{1,2},{2,3},{3,0},{4,5},{5,6},{6,7},{7,4},{8,9},{9,10},{10,1... | collective-permute-start | bytes 393224 | tf_op jit(solution)/shard_map/ppermute | solution.py:261
  3.9 9.0 %collective-permute-start.1 = (bf16[4,128,128]{2,1,0:T(8,128)(2,1)S(1)}, bf16[4,128,128]{2,1,0:T(8,128)(2,1)S(1)}, u32[]{:S(2)}, u32[]{:S(2)}) collective-permute-start(bf16[4,128,128]{2,1,0:T(8,128)(2,1)S(1)} %get-tuple-element.25), channel_id=1, source_target_pairs={{0,2},{1,3},{2,0},{3,1},{4,6},{5,7},{6,4},{7,5},{8,10},{9,11},{10,... | collective-permute-start | bytes 393224 | tf_op jit(solution)/shard_map/ppermute | solution.py:261
  7.2 28.5 %copy-start = (bf16[16,8,128,128]{3,2,1,0:T(8,128)(2,1)S(1)}, bf16[16,8,128,128]{3,2,1,0:T(8,128)(2,1)}, u32[]{:S(2)}) copy-start(bf16[16,8,128,128]{3,2,1,0:T(8,128)(2,1)} %refs_9_.5) | copy-start | bytes 12582916
  7.2 28.5 %copy-start.1 = (bf16[16,128,128]{2,1,0:T(8,128)(2,1)S(1)}, bf16[16,128,128]{2,1,0:T(8,128)(2,1)}, u32[]{:S(2)}) copy-start(bf16[16,128,128]{2,1,0:T(8,128)(2,1)} %sinv_ref.1) | copy-start | bytes 1572868
  7.2 28.5 %copy-start.2 = (f32[16,4,128]{2,1,0:T(4,128)S(1)}, f32[16,4,128]{2,1,0:T(4,128)}, u32[]{:S(2)}) copy-start(f32[16,4,128]{2,1,0:T(4,128)} %inc_ref.1) | copy-start | bytes 98308
  7.2 5.7 %collective-permute-start.2 = (bf16[4,128,128]{2,1,0:T(8,128)(2,1)S(1)}, bf16[4,128,128]{2,1,0:T(8,128)(2,1)S(1)}, u32[]{:S(2)}, u32[]{:S(2)}) collective-permute-start(bf16[4,128,128]{2,1,0:T(8,128)(2,1)S(1)} %get-tuple-element.26), channel_id=1, source_target_pairs={{0,3},{1,0},{2,1},{3,2},{4,7},{5,4},{6,5},{7,6},{8,11},{9,8},{10,9... | collective-permute-start | bytes 393224 | tf_op jit(solution)/shard_map/ppermute | solution.py:261
  14.4 2.5 %collective-permute-start.3 = (bf16[256,128]{1,0:T(8,128)(2,1)S(1)}, bf16[256,128]{1,0:T(8,128)(2,1)S(1)}, u32[]{:S(2)}, u32[]{:S(2)}) collective-permute-start(bf16[256,128]{1,0:T(8,128)(2,1)S(1)} %get-tuple-element.30), channel_id=1, source_target_pairs={{0,4},{4,0},{8,12},{12,8},{16,20},{20,16},{24,28},{28,24},{32,36},... | collective-permute-start | bytes 196616 | tf_op jit(solution)/shard_map/ppermute | solution.py:231
  37.5 2.9 %collective-permute-start.4 = (bf16[256,128]{1,0:T(8,128)(2,1)S(1)}, bf16[256,128]{1,0:T(8,128)(2,1)S(1)}, u32[]{:S(2)}, u32[]{:S(2)}) collective-permute-start(bf16[256,128]{1,0:T(8,128)(2,1)S(1)} %get-tuple-element.33), channel_id=1, source_target_pairs={{0,4},{4,0},{8,12},{12,8},{16,20},{20,16},{24,28},{28,24},{32,36},... | collective-permute-start | bytes 196616 | tf_op jit(solution)/shard_map/ppermute | solution.py:231
  55.8 2.9 %collective-permute-start.5 = (bf16[256,128]{1,0:T(8,128)(2,1)S(1)}, bf16[256,128]{1,0:T(8,128)(2,1)S(1)}, u32[]{:S(2)}, u32[]{:S(2)}) collective-permute-start(bf16[256,128]{1,0:T(8,128)(2,1)S(1)} %get-tuple-element.36), channel_id=1, source_target_pairs={{0,4},{4,0},{8,12},{12,8},{16,20},{20,16},{24,28},{28,24},{32,36},... | collective-permute-start | bytes 196616 | tf_op jit(solution)/shard_map/ppermute | solution.py:231
  74.1 2.9 %collective-permute-start.6 = (bf16[256,128]{1,0:T(8,128)(2,1)S(1)}, bf16[256,128]{1,0:T(8,128)(2,1)S(1)}, u32[]{:S(2)}, u32[]{:S(2)}) collective-permute-start(bf16[256,128]{1,0:T(8,128)(2,1)S(1)} %get-tuple-element.39), channel_id=1, source_target_pairs={{0,4},{4,0},{8,12},{12,8},{16,20},{20,16},{24,28},{28,24},{32,36},... | collective-permute-start | bytes 196616 | tf_op jit(solution)/shard_map/ppermute | solution.py:231

commit v4 on v3

v4 whole, which is shorter than its diff:
```python
import functools
import math

import jax
import jax.numpy as jnp
from jax import lax
from jax.experimental import pallas as pl
from jax.experimental.pallas import tpu as pltpu
from jax.sharding import PartitionSpec as P

WMAX = 4
STEPS = 4
LAGS = STEPS - 1
STRIDE = 37

BF16 = jnp.bfloat16
F32 = jnp.float32


def dot_f32(a, b, contract):
    return lax.dot_general(a, b, (contract, ((), ())), preferred_element_type=F32)


def spread(values, group, keep):
    out = jnp.where(keep, values, 0.0)
    lanes = out.shape[1]
    step = group
    while step < lanes:
        out = out + pltpu.roll(out, step, 1)
        step *= 2
    return out


def tapped(at, weights):
    found = jnp.where(at == 0, weights[0], 0.0)
    for tap in range(1, WMAX):
        found = jnp.where(at == tap, weights[tap], found)
    return found


def start_copies(pairs, sems):
    copies = [pltpu.make_async_copy(src, dst, sems.at[i]) for i, (src, dst) in enumerate(pairs)]
    for copy in copies:
        copy.start()
    return copies


def history_kernel(plan, table_hbm, weight_hbm, hist_hbm, own_ref, *rest):
    send_refs, (table_ref, weight_ref, hist_ref, sems) = rest[:-4], rest[-4:]
    copies = start_copies(
        [(table_hbm, table_ref), (weight_hbm, weight_ref), (hist_hbm, hist_ref)], sems
    )
    patches, pairs = table_ref.shape[1:]
    _, slab_len, src = hist_ref.shape
    local = own_ref.shape[1] // patches
    slab_id = lax.axis_index("slab")
    lane = lax.broadcasted_iota(jnp.int32, (patches, src), 1)
    turn = lax.rem(src - slab_id * local, src)

    def widen(x):
        return pltpu.roll(jnp.concatenate([x.astype(F32)] * STEPS, axis=1), turn, 1)

    copies[0].wait()
    copies[1].wait()
    first, band = widen(table_ref[1]), widen(table_ref[2])
    wide = weight_ref[...].astype(F32)
    weights = [jnp.where(band > tap, widen(wide[:, tap, :]), 0.0) for tap in range(WMAX)]
    start = first - (lane // pairs + 1 + slab_id * slab_len).astype(F32)

    h = lax.broadcasted_iota(jnp.int32, (slab_len, src), 0).astype(F32)
    copies[2].wait()
    for p in range(0, patches, 2):
        parts = []
        for q in (p, p + 1):
            table = tapped(h - start[q : q + 1], [w[q : q + 1] for w in weights])
            parts.append(dot_f32(table.astype(BF16), hist_ref[q], ((0,), (0,))))
        at = pl.ds(p * local, 2 * local)
        for n in range(STEPS):
            for (s, steps), out_ref in zip(((0, range(STEPS)),) + plan, (own_ref,) + send_refs):
                if n in steps:
                    lo = n * pairs + s * local
                    both = jnp.concatenate([part[lo : lo + local] for part in parts], axis=0)
                    out_ref[n - steps[0], at, :] = both.astype(out_ref.dtype)


def tables_kernel(local, table_hbm, weight_hbm, lag_ref, onehot_ref, table_ref, weight_ref, sems):
    copies = start_copies([(table_hbm, table_ref), (weight_hbm, weight_ref)], sems)
    patches, pairs = table_ref.shape[1:]
    rows = onehot_ref.shape[1]
    slab_id = lax.axis_index("slab")
    core = lax.rem(lax.axis_index("patch"), 2)
    lane = lax.broadcasted_iota(jnp.int32, (patches, rows), 1)
    row = lax.broadcasted_iota(jnp.int32, (patches, rows), 0)
    mine = lane // local == slab_id
    diagonal = lane // local == row
    blank = jnp.zeros((patches, rows - pairs), F32)

    def widen(x):
        return spread(jnp.concatenate([x.astype(F32), blank], axis=1), local, mine)

    for copy in copies:
        copy.wait()
    first, band = widen(table_ref[1]), widen(table_ref[2])
    wide = weight_ref[...].astype(F32)
    weights = [jnp.where(band > tap, widen(wide[:, tap, :]), 0.0) for tap in range(WMAX)]
    lags = [jnp.where(diagonal, tapped(lag - first, weights), 0.0) for lag in range(1, STEPS)]
    lag_ref[...] = jnp.concatenate(lags, axis=0).astype(BF16)
    obs = table_ref[0]
    obs = (obs // patches % 2 ^ core) * (patches * (lax.axis_size("patch") // 2)) + (
        obs // (2 * patches) * patches + obs % patches
    )
    obs = jnp.sum(jnp.where(diagonal, widen(obs), 0.0), axis=0, keepdims=True).astype(jnp.int32)
    targets = lax.broadcasted_iota(jnp.int32, onehot_ref.shape, 0)
    onehot_ref[...] = jnp.where(targets == obs, 1.0, 0.0).astype(BF16)


def field_of(driven, onehot_ref, coup_ref, coupled_ref, give_ref):
    rows, src = driven.shape
    patches = coup_ref.shape[0]
    local = rows // patches
    row_id = lax.broadcasted_iota(jnp.int32, (local, src), 0)
    coupled = []
    for p in range(patches):
        mine = driven[p * local : (p + 1) * local].astype(BF16)
        full = dot_f32(mine, coup_ref[p].reshape(local * src, src), ((1,), (1,)))
        out = full[:, :src]
        for k in range(1, local):
            out = jnp.where(row_id == k, full[:, k * src : (k + 1) * src], out)
        coupled.append(out)
    coupled = jnp.concatenate(coupled, axis=0).astype(BF16)
    coupled_ref[...] = coupled
    give_ref[...] = dot_f32(onehot_ref[give_ref.shape[0] :], coupled, ((1,), (0,))).astype(BF16)


def keep_kernel(onehot_ref, coupled_ref, keep_ref):
    keep_ref[...] = dot_f32(onehot_ref[: keep_ref.shape[0]], coupled_ref[...], ((1,), (0,)))


def first_kernel(own_ref, *rest):
    part_refs, tail = rest[:-4], rest[-4:]
    driven = own_ref[0]
    for part in part_refs:
        driven = driven + part[0].astype(F32)
    field_of(driven, *tail)


def add_kernel(orders, plan, keep_ref, got_ref, own_ref, *rest):
    part_refs, (send_ref, stored_ref, total_ref) = rest[:-3], rest[-3:]
    join_kernel(orders, keep_ref, got_ref, send_ref, total_ref)
    for n in range(1, STEPS):
        stored = own_ref[n]
        for (_, steps), part in zip(plan, part_refs):
            if n in steps:
                stored = stored + part[n - steps[0]].astype(F32)
        stored_ref[n - 1] = stored


def join_kernel(orders, keep_ref, got_ref, send_ref, total_ref):
    total = (keep_ref[...] + got_ref[...].astype(F32)).astype(BF16)
    total_ref[...] = total.reshape(total_ref.shape)
    core = lax.rem(lax.axis_index("patch"), 2)
    for which, order in enumerate(orders):

        @pl.when(core == which)
        def _(order=order):
            for i, block in enumerate(order):
                send_ref[i] = total_ref[block]


def amplitude_of(step, recv_ref, inc_ref, sinv_ref):
    sources, patches, src = recv_ref.shape
    total = jnp.sum(recv_ref[...].astype(F32), axis=0)
    drive = (inc_ref[:, step, :] - total).astype(BF16)
    row_id = lax.broadcasted_iota(jnp.int32, (patches, src), 0)
    amp = jnp.zeros((patches, src), F32)
    full = dot_f32(drive, sinv_ref[...].reshape(patches * src, src), ((1,), (1,)))
    for p in range(patches):
        amp = jnp.where(row_id == p, full[:, p * src : (p + 1) * src], amp)
    return amp.astype(BF16)


def step_kernel(step, recv_ref, inc_ref, sinv_ref, lag_ref, stored_ref, onehot_ref, coup_ref, *rest):
    past_refs, (coupled_ref, give_ref, amp_ref) = rest[:-3], rest[-3:]
    amp = amplitude_of(step, recv_ref, inc_ref, sinv_ref)
    amp_ref[...] = amp
    past = jnp.concatenate([amp] + [r[...] for r in past_refs], axis=0)
    driven = stored_ref[step] + dot_f32(lag_ref[: past.shape[0], :], past, ((0,), (0,)))
    field_of(driven, onehot_ref, coup_ref, coupled_ref, give_ref)


def last_kernel(recv_ref, inc_ref, sinv_ref, *rest):
    past_refs, out_ref = rest[:-1], rest[-1]
    amp = amplitude_of(STEPS - 1, recv_ref, inc_ref, sinv_ref)
    for step, value in enumerate([r[...] for r in past_refs] + [amp]):
        out_ref[:, step, :] = value


def call(kernel, name, outs, args, in_hbm=False, scratch=(), cost=None):
    vmem = pl.BlockSpec(memory_space=pltpu.VMEM)
    space = pltpu.HBM if in_hbm else pltpu.VMEM
    if in_hbm:
        args = [pltpu.with_memory_space_constraint(x, pltpu.HBM) for x in args]
    return pl.pallas_call(
        kernel,
        name=name,
        out_shape=outs,
        in_specs=[pl.BlockSpec(memory_space=space)] * len(args),
        out_specs=jax.tree.map(lambda _: vmem, outs),
        scratch_shapes=scratch,
        cost_estimate=cost,
        compiler_params=pltpu.CompilerParams(vmem_limit_bytes=24 * 2**20),
    )(*args)


def around(n):
    return [i ^ (i >> 1) for i in range(n)]


def on_device(history, interp_weights, pair_table, coupling, self_inverse, incident):
    patches, slab_len, src = history.shape
    local = coupling.shape[1]
    slabs = lax.axis_size("slab")
    blocks = lax.axis_size("patch") // 2
    rows = patches * local
    half = blocks * patches
    cores = [(i, i ^ 1) for i in range(2 * blocks)]
    wide = next(n for n in range(1, blocks + 1) if n * n >= blocks)
    chips = [
        [(y * wide + x, z) for y in around(blocks // wide) for x in around(wide) for z in around(slabs)],
        [(y * wide + x, z) for x in around(wide) for z in around(slabs) for y in around(blocks // wide)],
    ]
    count = len(chips[0])
    chips[0] = [chips[0][i * STRIDE % count] for i in range(count)] if math.gcd(STRIDE, count) == 1 else chips[0]
    groups = [[(2 * b + core) * slabs + z for b, z in chips[core]] for core in range(2)]
    orders = [[b for b, _ in chips[core]] for core in range(2)]

    def exchange(coupled, give, history=None):
        got = lax.ppermute(give, "patch", cores)
        keep = call(keep_kernel, "keep", shape((half, src), F32), [onehot, coupled])
        out = shape((blocks * slabs, patches, src), BF16)
        scratch = [pltpu.VMEM((blocks, patches, src), BF16)]
        if history:
            kernel = functools.partial(add_kernel, orders, plan)
            outs = [out, shape((STEPS - 1, rows, src), F32)]
            send, *stored = call(kernel, "add", outs, [keep, got, *history], scratch=scratch)
        else:
            kernel, stored = functools.partial(join_kernel, orders), []
            send = call(kernel, "join", out, [keep, got], scratch=scratch)
        recv = lax.all_to_all(send, ("patch", "slab"), 0, 0, axis_index_groups=groups, tiled=True)
        return recv, *stored

    shape = jax.ShapeDtypeStruct
    field = [shape((rows, src), BF16), shape((half, src), BF16)]
    table = pair_table.transpose(2, 0, 1)
    weight = interp_weights.transpose(0, 2, 1)
    far = slabs // 2
    order = [far] + [s for s in range(slabs - 1, 0, -1) if s != far]
    plan = tuple((s, range(STEPS)) for s in order)
    own, *sends = call(
        functools.partial(history_kernel, plan),
        "history",
        [
            shape((STEPS, rows, src), F32),
            *(shape((len(steps), rows, src), BF16) for _, steps in plan),
        ],
        [table, weight, history],
        in_hbm=True,
        scratch=[
            pltpu.VMEM(table.shape, jnp.int32),
            pltpu.VMEM(weight.shape, BF16),
            pltpu.VMEM(history.shape, BF16),
            pltpu.SemaphoreType.DMA((3,)),
        ],
        cost=pl.CostEstimate(flops=10**10, bytes_accessed=10**7, transcendentals=0),
    )
    parts = [
        lax.ppermute(x, "slab", [(z, (z + s) % slabs) for z in range(slabs)])
        for (s, _), x in zip(plan, sends)
    ]
    lag_table, onehot = call(
        functools.partial(tables_kernel, local),
        "tables",
        [shape((LAGS * patches, rows), BF16), shape((2 * half, rows), BF16)],
        [table, weight],
        in_hbm=True,
        scratch=[
            pltpu.VMEM(table.shape, jnp.int32),
            pltpu.VMEM(weight.shape, BF16),
            pltpu.SemaphoreType.DMA((2,)),
        ],
    )
    coupled, give = call(first_kernel, "first", field, [own, *parts, onehot, coupling])
    amps = []
    for step in range(STEPS):
        if step == 0:
            recv, stored = exchange(coupled, give, [own, *parts])
        else:
            (recv,) = exchange(coupled, give)
        if step == STEPS - 1:
            return call(
                last_kernel,
                "last",
                shape((patches, STEPS, src), BF16),
                [recv, incident, self_inverse, *amps],
            )

        def body(*refs, step=step):
            step_kernel(step, *refs)

        coupled, give, amp = call(
            body,
            f"step{step}",
            field + [shape((patches, src), BF16)],
            [recv, incident, self_inverse, lag_table, stored, onehot, coupling, *amps[::-1]],
        )
        amps.append(amp)


def solution(mesh):
    in_specs = (
        P("patch", "slab", None),
        P("patch", None, None),
        P("patch", None, None),
        P("patch", "slab", None, None),
        P("patch", None, None),
        P("patch", None, None),
    )
    out_specs = P("patch", None, None)
    return jax.shard_map(
        on_device, mesh=mesh, in_specs=in_specs, out_specs=out_specs, check_vma=False
    )
```

time: 92.2 us -> 91.4 us (level)
  starting transfers between devices: 14.1 us -> 11.2 us
  blocking collectives: 59.1 us -> 61.8 us
  Pallas kernels: 12.2 us -> 11 us
  waiting for transfers between devices: 5.88 us -> 6.97 us
    all_to_all x4, blocking collectives: 59.1 us -> 61.8 us  [exchange(): lax.all_to_all(send, ('patch', 'slab'), 0, 0, axis_index_groups=groups, t...]
    ppermute x4, starting transfers between devices: 7.52 us -> 5.23 us  [exchange(): got = lax.ppermute(give, 'patch', cores)]
    ppermute x3, waiting for transfers between devices: 2.27 us -> 3.94 us  [on_device(): lax.ppermute(x, 'slab', [(z, (z + s) % slabs) for z in range(slabs)])]
    pallas_call x11 -> x15, Pallas kernels: 12.2 us -> 11 us  [call(): pl.pallas_call(kernel, name=name, out_shape=outs, in_specs=[pl.BlockSpec(...]
  transfers between devices with their start and end apart: 7 -> 7, of which waited for: 5 -> 6; matrix products, arithmetic and copies ran while one was open for 0% -> 0% of each run, Pallas kernels for 3% -> 2%
where the time goes in v4:
time: 91.4 us; the launch traced here: 91.1 us
  blocking collectives  61.8 us (68%)
  starting transfers between devices  11.2 us (12%)
  Pallas kernels  11 us (12%)
  waiting for transfers between devices  6.97 us (8%)
    all_to_all x4, blocking collectives, exchange(): lax.all_to_all(send, ('patch', 'slab'), 0, 0, axis_index_groups=groups, t...  61.8 us
    pallas_call x15, Pallas kernels, call(): pl.pallas_call(kernel, name=name, out_shape=outs, in_specs=[pl.BlockSpec(...  11 us
    ppermute x3, starting transfers between devices, on_device(): lax.ppermute(x, 'slab', [(z, (z + s) % slabs) for z in range(slabs)])  5.97 us
    ppermute x4, starting transfers between devices, exchange(): got = lax.ppermute(give, 'patch', cores)  5.23 us
    ppermute x3, waiting for transfers between devices, on_device(): lax.ppermute(x, 'slab', [(z, (z + s) % slabs) for z in range(slabs)])  3.94 us
    ppermute x4, waiting for transfers between devices, exchange(): got = lax.ppermute(give, 'patch', cores)  3.03 us
  transfers between devices with their start and end apart: 7, of which 6 were waited for; matrix products, arithmetic and copies ran while one was open for 0% of the time, Pallas kernels for 2%

profile of v4, /device:TPU:1, one launch (start us, length us, event | category | flops | bytes accessed | tf_op | source)
XLA Modules:
  0.0 91.1 jit_solution(12820900031169395844)
XLA Ops:
  0.0 0.0 copy-start
  0.0 1.5 %history.1 = (f32[4,128,128]{2,1,0:T(8,128)S(1)}, bf16[4,128,128]{2,1,0:T(8,128)(2,1)S(1)}, bf16[4,128,128]{2,1,0:T(8,128)(2,1)S(1)}, bf16[4,128,128]{2,1,0:T(8,128)(2,1)S(1)}) custom-call(s32[3,16,32]{2,1,0:T(8,128)} %bitcast.2, bf16[16,4,32]{2,1,0:T(4,128)(2,1)} %bitcast.4, bf16[16,64,128]{2,1,0:T(8,128)(2,1)} %hist_hbm.1), custom_call_target="tpu_custom_call" | custom-call | flops 10000000000 | bytes 10000000 | tf_op jit(solution)/shard_map/history/pallas_call | solution.py:203
  1.6 0.0 copy-start.1
  1.6 0.0 copy-start.2
  1.6 4.5 %collective-permute-start = (bf16[4,128,128]{2,1,0:T(8,128)(2,1)S(1)}, bf16[4,128,128]{2,1,0:T(8,128)(2,1)S(1)}, u32[]{:S(2)}, u32[]{:S(2)}) collective-permute-start(bf16[4,128,128]{2,1,0:T(8,128)(2,1)S(1)} %get-tuple-element.26), channel_id=1, source_target_pairs={{0,2},{1,3},{2,0},{3,1},{4,6},{5,7},{6,4},{7,5},{8,10},{9,11},{10,... | collective-permute-start | bytes 393224 | tf_op jit(solution)/shard_map/ppermute | solution.py:277
  6.1 0.4 collective-permute-start.1
  6.5 1.0 %collective-permute-start.2 = (bf16[4,128,128]{2,1,0:T(8,128)(2,1)S(1)}, bf16[4,128,128]{2,1,0:T(8,128)(2,1)S(1)}, u32[]{:S(2)}, u32[]{:S(2)}) collective-permute-start(bf16[4,128,128]{2,1,0:T(8,128)(2,1)S(1)} %get-tuple-element.28), channel_id=1, source_target_pairs={{0,1},{1,2},{2,3},{3,0},{4,5},{5,6},{6,7},{7,4},{8,9},{9,10},{10,1... | collective-permute-start | bytes 393224 | tf_op jit(solution)/shard_map/ppermute | solution.py:277
  7.5 1.1 %tables.1 = (bf16[48,128]{1,0:T(8,128)(2,1)S(1)}, bf16[512,128]{1,0:T(8,128)(2,1)S(1)}) custom-call(s32[3,16,32]{2,1,0:T(8,128)} %bitcast.3, bf16[16,4,32]{2,1,0:T(4,128)(2,1)} %bitcast.5), custom_call_target="tpu_custom_call" | custom-call | tf_op jit(solution)/shard_map/tables/pallas_call | solution.py:203
  8.7 0.6 collective-permute-done.rest_0_
  9.3 3.3 %collective-permute-done.1.rest_1_ = bf16[4,128,128]{2,1,0:T(8,128)(2,1)S(1)} collective-permute-done((bf16[4,128,128]{2,1,0:T(8,128)(2,1)S(1)}, bf16[4,128,128]{2,1,0:T(8,128)(2,1)S(1)}, u32[]{:S(2)}, u32[]{:S(2)}) %collective-permute-start.1) | collective-permute-done | bytes 131104 | tf_op jit(solution)/shard_map/ppermute | solution.py:277
  12.6 0.0 collective-permute-done.2.rest_2_
  12.6 0.0 copy-done
  12.6 1.3 %first.1 = (bf16[128,128]{1,0:T(8,128)(2,1)S(1)}, bf16[256,128]{1,0:T(8,128)(2,1)S(1)}) custom-call(f32[4,128,128]{2,1,0:T(8,128)S(1)} %get-tuple-element.25.own_ref, bf16[4,128,128]{2,1,0:T(8,128)(2,1)S(1)} %collective-permute-done.rest_0_, bf16[4,128,128]{2,1,0:T(8,128)(2,1)S(1)} %collective-permute-done.1.rest_1_, ...), custom_call_target="tpu_custom_call" | custom-call | tf_op jit(solution)/shard_map/first/pallas_call | solution.py:203
  14.0 1.6 %collective-permute-start.3 = (bf16[256,128]{1,0:T(8,128)(2,1)S(1)}, bf16[256,128]{1,0:T(8,128)(2,1)S(1)}, u32[]{:S(2)}, u32[]{:S(2)}) collective-permute-start(bf16[256,128]{1,0:T(8,128)(2,1)S(1)} %get-tuple-element.30), channel_id=1, source_target_pairs={{0,4},{4,0},{8,12},{12,8},{16,20},{20,16},{24,28},{28,24},{32,36},... | collective-permute-start | bytes 196616 | tf_op jit(solution)/shard_map/ppermute | solution.py:238
  15.6 0.1 keep.4.keep_ref
  15.7 0.8 collective-permute-done.3.got_ref
  16.5 0.1 add.1
  16.6 19.4 %all_to_all.20.refs_0_ = bf16[64,16,128]{2,1,0:T(8,128)(2,1)S(1)} all-to-all(bf16[64,16,128]{2,1,0:T(8,128)(2,1)S(1)} %get-tuple-element.31), channel_id=1, replica_groups={{0,105,27,114,40,89,51,2,120,17,67,42,80,97,11,122,32,73,59,82,104,25,1..., dimensions={0} | all-to-all | bytes 524288 | tf_op jit(solution)/shard_map/all_to_all | solution.py:249
  36.0 0.0 copy-done.1
  36.0 0.0 copy-done.2
  36.0 1.7 %step0.1 = (bf16[128,128]{1,0:T(8,128)(2,1)S(1)}, bf16[256,128]{1,0:T(8,128)(2,1)S(1)}, bf16[16,128]{1,0:T(8,128)(2,1)S(1)}) custom-call(bf16[64,16,128]{2,1,0:T(8,128)(2,1)S(1)} %all_to_all.20.refs_0_, f32[16,4,128]{2,1,0:T(4,128)S(1)} %copy-done.2, bf16[16,128,128]{2,1,0:T(8,128)(2,1)S(1)} %copy-done.1, bf16[48,128]{1,0:T(8,128)(2,1)S(1)} %get-tuple-element.32.refs_3_, ...), custom_call_target="tpu_custom_call" | custom-call | tf_op jit(solution)/shard_map/step0/pallas_call | solution.py:203
  37.7 1.2 %collective-permute-start.4 = (bf16[256,128]{1,0:T(8,128)(2,1)S(1)}, bf16[256,128]{1,0:T(8,128)(2,1)S(1)}, u32[]{:S(2)}, u32[]{:S(2)}) collective-permute-start(bf16[256,128]{1,0:T(8,128)(2,1)S(1)} %get-tuple-element.35), channel_id=1, source_target_pairs={{0,4},{4,0},{8,12},{12,8},{16,20},{20,16},{24,28},{28,24},{32,36},... | collective-permute-start | bytes 196616 | tf_op jit(solution)/shard_map/ppermute | solution.py:238
  38.9 0.1 keep.5.keep_ref
  39.1 0.8 collective-permute-done.4.got_ref
  39.8 0.1 join.3
  39.9 14.1 %all_to_all.21.refs_0_ = bf16[64,16,128]{2,1,0:T(8,128)(2,1)S(1)} all-to-all(bf16[64,16,128]{2,1,0:T(8,128)(2,1)S(1)} %join.3), channel_id=1, replica_groups={{0,105,27,114,40,89,51,2,120,17,67,42,80,97,11,122,32,73,59,82,104,25,1..., dimensions={0} | all-to-all | bytes 524288 | tf_op jit(solution)/shard_map/all_to_all | solution.py:249
  54.0 1.7 %step1.1 = (bf16[128,128]{1,0:T(8,128)(2,1)S(1)}, bf16[256,128]{1,0:T(8,128)(2,1)S(1)}, bf16[16,128]{1,0:T(8,128)(2,1)S(1)}) custom-call(bf16[64,16,128]{2,1,0:T(8,128)(2,1)S(1)} %all_to_all.21.refs_0_, f32[16,4,128]{2,1,0:T(4,128)S(1)} %copy-done.2, bf16[16,128,128]{2,1,0:T(8,128)(2,1)S(1)} %copy-done.1, bf16[48,128]{1,0:T(8,128)(2,1)S(1)} %get-tuple-element.32.refs_3_, ...), custom_call_target="tpu_custom_call" | custom-call | tf_op jit(solution)/shard_map/step1/pallas_call | solution.py:203
  55.8 1.2 %collective-permute-start.5 = (bf16[256,128]{1,0:T(8,128)(2,1)S(1)}, bf16[256,128]{1,0:T(8,128)(2,1)S(1)}, u32[]{:S(2)}, u32[]{:S(2)}) collective-permute-start(bf16[256,128]{1,0:T(8,128)(2,1)S(1)} %get-tuple-element.38), channel_id=1, source_target_pairs={{0,4},{4,0},{8,12},{12,8},{16,20},{20,16},{24,28},{28,24},{32,36},... | collective-permute-start | bytes 196616 | tf_op jit(solution)/shard_map/ppermute | solution.py:238
  57.0 0.1 keep.6.keep_ref
  57.1 0.8 collective-permute-done.5.got_ref
  57.9 0.1 join.4
  57.9 14.1 %all_to_all.22.refs_0_ = bf16[64,16,128]{2,1,0:T(8,128)(2,1)S(1)} all-to-all(bf16[64,16,128]{2,1,0:T(8,128)(2,1)S(1)} %join.4), channel_id=1, replica_groups={{0,105,27,114,40,89,51,2,120,17,67,42,80,97,11,122,32,73,59,82,104,25,1..., dimensions={0} | all-to-all | bytes 524288 | tf_op jit(solution)/shard_map/all_to_all | solution.py:249
  72.1 1.7 %step2.1 = (bf16[128,128]{1,0:T(8,128)(2,1)S(1)}, bf16[256,128]{1,0:T(8,128)(2,1)S(1)}, bf16[16,128]{1,0:T(8,128)(2,1)S(1)}) custom-call(bf16[64,16,128]{2,1,0:T(8,128)(2,1)S(1)} %all_to_all.22.refs_0_, f32[16,4,128]{2,1,0:T(4,128)S(1)} %copy-done.2, bf16[16,128,128]{2,1,0:T(8,128)(2,1)S(1)} %copy-done.1, bf16[48,128]{1,0:T(8,128)(2,1)S(1)} %get-tuple-element.32.refs_3_, ...), custom_call_target="tpu_custom_call" | custom-call | tf_op jit(solution)/shard_map/step2/pallas_call | solution.py:203
  73.8 1.2 %collective-permute-start.6 = (bf16[256,128]{1,0:T(8,128)(2,1)S(1)}, bf16[256,128]{1,0:T(8,128)(2,1)S(1)}, u32[]{:S(2)}, u32[]{:S(2)}) collective-permute-start(bf16[256,128]{1,0:T(8,128)(2,1)S(1)} %get-tuple-element.41), channel_id=1, source_target_pairs={{0,4},{4,0},{8,12},{12,8},{16,20},{20,16},{24,28},{28,24},{32,36},... | collective-permute-start | bytes 196616 | tf_op jit(solution)/shard_map/ppermute | solution.py:238
  75.0 0.1 keep.7.keep_ref
  75.2 0.8 collective-permute-done.6.got_ref
  75.9 0.1 join.5
  76.0 14.1 %all_to_all.23.recv_ref = bf16[64,16,128]{2,1,0:T(8,128)(2,1)S(1)} all-to-all(bf16[64,16,128]{2,1,0:T(8,128)(2,1)S(1)} %join.5), channel_id=1, replica_groups={{0,105,27,114,40,89,51,2,120,17,67,42,80,97,11,122,32,73,59,82,104,25,1..., dimensions={0} | all-to-all | bytes 524288 | tf_op jit(solution)/shard_map/all_to_all | solution.py:249
  90.1 0.9 %last.1 = bf16[16,4,128]{2,1,0:T(4,128)(2,1)} custom-call(bf16[64,16,128]{2,1,0:T(8,128)(2,1)S(1)} %all_to_all.23.recv_ref, f32[16,4,128]{2,1,0:T(4,128)S(1)} %copy-done.2, bf16[16,128,128]{2,1,0:T(8,128)(2,1)S(1)} %copy-done.1, bf16[16,128]{1,0:T(8,128)(2,1)S(1)} %get-tuple-element.36.refs_7_.refs_8_.rest_0_, ...), custom_call_target="tpu_custom_call" | custom-call | tf_op jit(solution)/shard_map/last/pallas_call | solution.py:203
Async XLA Ops:
  0.0 12.6 %copy-start = (bf16[16,8,128,128]{3,2,1,0:T(8,128)(2,1)S(1)}, bf16[16,8,128,128]{3,2,1,0:T(8,128)(2,1)}, u32[]{:S(2)}) copy-start(bf16[16,8,128,128]{3,2,1,0:T(8,128)(2,1)} %refs_6_.5) | copy-start | bytes 12582916
  1.6 34.4 %copy-start.1 = (bf16[16,128,128]{2,1,0:T(8,128)(2,1)S(1)}, bf16[16,128,128]{2,1,0:T(8,128)(2,1)}, u32[]{:S(2)}) copy-start(bf16[16,128,128]{2,1,0:T(8,128)(2,1)} %sinv_ref.1) | copy-start | bytes 1572868
  1.6 34.4 %copy-start.2 = (f32[16,4,128]{2,1,0:T(4,128)S(1)}, f32[16,4,128]{2,1,0:T(4,128)}, u32[]{:S(2)}) copy-start(f32[16,4,128]{2,1,0:T(4,128)} %inc_ref.1) | copy-start | bytes 98308
  1.6 7.7 %collective-permute-start = (bf16[4,128,128]{2,1,0:T(8,128)(2,1)S(1)}, bf16[4,128,128]{2,1,0:T(8,128)(2,1)S(1)}, u32[]{:S(2)}, u32[]{:S(2)}) collective-permute-start(bf16[4,128,128]{2,1,0:T(8,128)(2,1)S(1)} %get-tuple-element.26), channel_id=1, source_target_pairs={{0,2},{1,3},{2,0},{3,1},{4,6},{5,7},{6,4},{7,5},{8,10},{9,11},{10,... | collective-permute-start | bytes 393224 | tf_op jit(solution)/shard_map/ppermute | solution.py:277
  6.1 6.5 %collective-permute-start.1 = (bf16[4,128,128]{2,1,0:T(8,128)(2,1)S(1)}, bf16[4,128,128]{2,1,0:T(8,128)(2,1)S(1)}, u32[]{:S(2)}, u32[]{:S(2)}) collective-permute-start(bf16[4,128,128]{2,1,0:T(8,128)(2,1)S(1)} %get-tuple-element.27), channel_id=1, source_target_pairs={{0,3},{1,0},{2,1},{3,2},{4,7},{5,4},{6,5},{7,6},{8,11},{9,8},{10,9... | collective-permute-start | bytes 393224 | tf_op jit(solution)/shard_map/ppermute | solution.py:277
  6.5 6.1 %collective-permute-start.2 = (bf16[4,128,128]{2,1,0:T(8,128)(2,1)S(1)}, bf16[4,128,128]{2,1,0:T(8,128)(2,1)S(1)}, u32[]{:S(2)}, u32[]{:S(2)}) collective-permute-start(bf16[4,128,128]{2,1,0:T(8,128)(2,1)S(1)} %get-tuple-element.28), channel_id=1, source_target_pairs={{0,1},{1,2},{2,3},{3,0},{4,5},{5,6},{6,7},{7,4},{8,9},{9,10},{10,1... | collective-permute-start | bytes 393224 | tf_op jit(solution)/shard_map/ppermute | solution.py:277
  14.0 2.5 %collective-permute-start.3 = (bf16[256,128]{1,0:T(8,128)(2,1)S(1)}, bf16[256,128]{1,0:T(8,128)(2,1)S(1)}, u32[]{:S(2)}, u32[]{:S(2)}) collective-permute-start(bf16[256,128]{1,0:T(8,128)(2,1)S(1)} %get-tuple-element.30), channel_id=1, source_target_pairs={{0,4},{4,0},{8,12},{12,8},{16,20},{20,16},{24,28},{28,24},{32,36},... | collective-permute-start | bytes 196616 | tf_op jit(solution)/shard_map/ppermute | solution.py:238
  37.7 2.1 %collective-permute-start.4 = (bf16[256,128]{1,0:T(8,128)(2,1)S(1)}, bf16[256,128]{1,0:T(8,128)(2,1)S(1)}, u32[]{:S(2)}, u32[]{:S(2)}) collective-permute-start(bf16[256,128]{1,0:T(8,128)(2,1)S(1)} %get-tuple-element.35), channel_id=1, source_target_pairs={{0,4},{4,0},{8,12},{12,8},{16,20},{20,16},{24,28},{28,24},{32,36},... | collective-permute-start | bytes 196616 | tf_op jit(solution)/shard_map/ppermute | solution.py:238
  55.8 2.1 %collective-permute-start.5 = (bf16[256,128]{1,0:T(8,128)(2,1)S(1)}, bf16[256,128]{1,0:T(8,128)(2,1)S(1)}, u32[]{:S(2)}, u32[]{:S(2)}) collective-permute-start(bf16[256,128]{1,0:T(8,128)(2,1)S(1)} %get-tuple-element.38), channel_id=1, source_target_pairs={{0,4},{4,0},{8,12},{12,8},{16,20},{20,16},{24,28},{28,24},{32,36},... | collective-permute-start | bytes 196616 | tf_op jit(solution)/shard_map/ppermute | solution.py:238
  73.8 2.1 %collective-permute-start.6 = (bf16[256,128]{1,0:T(8,128)(2,1)S(1)}, bf16[256,128]{1,0:T(8,128)(2,1)S(1)}, u32[]{:S(2)}, u32[]{:S(2)}) collective-permute-start(bf16[256,128]{1,0:T(8,128)(2,1)S(1)} %get-tuple-element.41), channel_id=1, source_target_pairs={{0,4},{4,0},{8,12},{12,8},{16,20},{20,16},{24,28},{28,24},{32,36},... | collective-permute-start | bytes 196616 | tf_op jit(solution)/shard_map/ppermute | solution.py:238

commit v5 on v4

--- a/solution.py
+++ b/solution.py
@@ -12,6 +12,7 @@
 STEPS = 4
 LAGS = STEPS - 1
 STRIDE = 37
+TURNED = 2
 
 BF16 = jnp.bfloat16
 F32 = jnp.float32
@@ -104,7 +105,8 @@
     wide = weight_ref[...].astype(F32)
     weights = [jnp.where(band > tap, widen(wide[:, tap, :]), 0.0) for tap in range(WMAX)]
     lags = [jnp.where(diagonal, tapped(lag - first, weights), 0.0) for lag in range(1, STEPS)]
-    lag_ref[...] = jnp.concatenate(lags, axis=0).astype(BF16)
+    rest = jnp.zeros((rows - LAGS * patches, rows), F32)
+    lag_ref[...] = jnp.concatenate(lags + [rest], axis=0).T.astype(BF16)
     obs = table_ref[0]
     obs = (obs // patches % 2 ^ core) * (patches * (lax.axis_size("patch") // 2)) + (
         obs // (2 * patches) * patches + obs % patches
@@ -114,18 +116,32 @@
     onehot_ref[...] = jnp.where(targets == obs, 1.0, 0.0).astype(BF16)
 
 
-def field_of(driven, onehot_ref, coup_ref, coupled_ref, give_ref):
+def turn_kernel(coup_ref, turned_ref):
+    patches, count = turned_ref.shape[:2]
+    skip = coup_ref.shape[1] - count
+    for p in range(patches):
+        for i in range(count):
+            turned_ref[p, i] = coup_ref[p, skip + i].astype(F32).T.astype(BF16)
+
+
+def field_of(driven, onehot_ref, coup_ref, turned_ref, coupled_ref, give_ref):
     rows, src = driven.shape
-    patches = coup_ref.shape[0]
-    local = rows // patches
+    patches, local = coup_ref.shape[:2]
+    direct = local - turned_ref.shape[1]
     row_id = lax.broadcasted_iota(jnp.int32, (local, src), 0)
+    driven = driven.astype(BF16).astype(F32)
+    columns = driven.T
     coupled = []
     for p in range(patches):
         mine = driven[p * local : (p + 1) * local].astype(BF16)
-        full = dot_f32(mine, coup_ref[p].reshape(local * src, src), ((1,), (1,)))
+        full = dot_f32(mine, coup_ref[p, :direct].reshape(direct * src, src), ((1,), (1,)))
         out = full[:, :src]
-        for k in range(1, local):
+        for k in range(1, direct):
             out = jnp.where(row_id == k, full[:, k * src : (k + 1) * src], out)
+        for k in range(direct, local):
+            r = p * local + k
+            terms = turned_ref[p, k - direct].astype(F32) * columns[:, r : r + 1]
+            out = jnp.where(row_id == k, jnp.sum(terms, axis=0, keepdims=True), out)
         coupled.append(out)
     coupled = jnp.concatenate(coupled, axis=0).astype(BF16)
     coupled_ref[...] = coupled
@@ -137,7 +153,7 @@
 
 
 def first_kernel(own_ref, *rest):
-    part_refs, tail = rest[:-4], rest[-4:]
+    part_refs, tail = rest[:-5], rest[-5:]
     driven = own_ref[0]
     for part in part_refs:
         driven = driven + part[0].astype(F32)
@@ -170,22 +186,28 @@
 def amplitude_of(step, recv_ref, inc_ref, sinv_ref):
     sources, patches, src = recv_ref.shape
     total = jnp.sum(recv_ref[...].astype(F32), axis=0)
-    drive = (inc_ref[:, step, :] - total).astype(BF16)
-    row_id = lax.broadcasted_iota(jnp.int32, (patches, src), 0)
-    amp = jnp.zeros((patches, src), F32)
-    full = dot_f32(drive, sinv_ref[...].reshape(patches * src, src), ((1,), (1,)))
-    for p in range(patches):
-        amp = jnp.where(row_id == p, full[:, p * src : (p + 1) * src], amp)
+    drive = inc_ref[:, step, :] - total
+    halves = []
+    group = 8
+    row_id = lax.broadcasted_iota(jnp.int32, (group, src), 0)
+    for p in range(0, patches, group):
+        matrices = sinv_ref[p : p + group].reshape(group * src, src)
+        full = dot_f32(drive[p : p + group].astype(BF16), matrices, ((1,), (1,)))
+        amp = full[:, :src]
+        for i in range(1, group):
+            amp = jnp.where(row_id == i, full[:, i * src : (i + 1) * src], amp)
+        halves.append(amp)
+    amp = jnp.concatenate(halves, axis=0)
     return amp.astype(BF16)
 
 
-def step_kernel(step, recv_ref, inc_ref, sinv_ref, lag_ref, stored_ref, onehot_ref, coup_ref, *rest):
+def step_kernel(step, recv_ref, inc_ref, sinv_ref, lag_ref, stored_ref, onehot_ref, coup_ref, turned_ref, *rest):
     past_refs, (coupled_ref, give_ref, amp_ref) = rest[:-3], rest[-3:]
     amp = amplitude_of(step, recv_ref, inc_ref, sinv_ref)
     amp_ref[...] = amp
     past = jnp.concatenate([amp] + [r[...] for r in past_refs], axis=0)
-    driven = stored_ref[step] + dot_f32(lag_ref[: past.shape[0], :], past, ((0,), (0,)))
-    field_of(driven, onehot_ref, coup_ref, coupled_ref, give_ref)
+    driven = stored_ref[step] + dot_f32(lag_ref[:, : past.shape[0]], past, ((1,), (0,)))
+    field_of(driven, onehot_ref, coup_ref, turned_ref, coupled_ref, give_ref)
 
 
 def last_kernel(recv_ref, inc_ref, sinv_ref, *rest):
@@ -280,7 +302,7 @@
     lag_table, onehot = call(
         functools.partial(tables_kernel, local),
         "tables",
-        [shape((LAGS * patches, rows), BF16), shape((2 * half, rows), BF16)],
+        [shape((rows, rows), BF16), shape((2 * half, rows), BF16)],
         [table, weight],
         in_hbm=True,
         scratch=[
@@ -289,7 +311,8 @@
             pltpu.SemaphoreType.DMA((2,)),
         ],
     )
-    coupled, give = call(first_kernel, "first", field, [own, *parts, onehot, coupling])
+    turned = call(turn_kernel, "turn", shape((patches, TURNED, src, src), BF16), [coupling])
+    coupled, give = call(first_kernel, "first", field, [own, *parts, onehot, coupling, turned])
     amps = []
     for step in range(STEPS):
         if step == 0:
@@ -311,7 +334,7 @@
             body,
             f"step{step}",
             field + [shape((patches, src), BF16)],
-            [recv, incident, self_inverse, lag_table, stored, onehot, coupling, *amps[::-1]],
+            [recv, incident, self_inverse, lag_table, stored, onehot, coupling, turned, *amps[::-1]],
         )
         amps.append(amp)
 

time: 91.4 us -> 90.4 us (0.989)
    pallas_call x15 -> x16, Pallas kernels: 11 us -> 10.4 us  [call(): pl.pallas_call(kernel, name=name, out_shape=outs, in_specs=[pl.BlockSpec(...]
where the time goes in v5:
time: 90.4 us; the launch traced here: 90 us
  blocking collectives  61.8 us (68%)
  starting transfers between devices  11.2 us (12%)
  Pallas kernels  10.4 us (12%)
  waiting for transfers between devices  6.53 us (7%)
    all_to_all x4, blocking collectives, exchange(): lax.all_to_all(send, ('patch', 'slab'), 0, 0, axis_index_groups=groups, t...  61.8 us
    pallas_call x16, Pallas kernels, call(): pl.pallas_call(kernel, name=name, out_shape=outs, in_specs=[pl.BlockSpec(...  10.4 us
    ppermute x3, starting transfers between devices, on_device(): lax.ppermute(x, 'slab', [(z, (z + s) % slabs) for z in range(slabs)])  5.97 us
    ppermute x4, starting transfers between devices, exchange(): got = lax.ppermute(give, 'patch', cores)  5.23 us
    ppermute x3, waiting for transfers between devices, on_device(): lax.ppermute(x, 'slab', [(z, (z + s) % slabs) for z in range(slabs)])  3.5 us
    ppermute x4, waiting for transfers between devices, exchange(): got = lax.ppermute(give, 'patch', cores)  3.03 us
  transfers between devices with their start and end apart: 7, of which 6 were waited for; matrix products, arithmetic and copies ran while one was open for 0% of the time, Pallas kernels for 2%

profile of v5, /device:TPU:1, one launch (start us, length us, event | category | flops | bytes accessed | tf_op | source)
XLA Modules:
  0.0 90.0 jit_solution(8508137778503334336)
XLA Ops:
  0.0 0.0 copy-start
  0.0 1.5 %history.1 = (f32[4,128,128]{2,1,0:T(8,128)S(1)}, bf16[4,128,128]{2,1,0:T(8,128)(2,1)S(1)}, bf16[4,128,128]{2,1,0:T(8,128)(2,1)S(1)}, bf16[4,128,128]{2,1,0:T(8,128)(2,1)S(1)}) custom-call(s32[3,16,32]{2,1,0:T(8,128)} %bitcast.2, bf16[16,4,32]{2,1,0:T(4,128)(2,1)} %bitcast.4, bf16[16,64,128]{2,1,0:T(8,128)(2,1)} %hist_hbm.1), custom_call_target="tpu_custom_call" | custom-call | flops 10000000000 | bytes 10000000 | tf_op jit(solution)/shard_map/history/pallas_call | solution.py:225
  1.6 4.5 %collective-permute-start = (bf16[4,128,128]{2,1,0:T(8,128)(2,1)S(1)}, bf16[4,128,128]{2,1,0:T(8,128)(2,1)S(1)}, u32[]{:S(2)}, u32[]{:S(2)}) collective-permute-start(bf16[4,128,128]{2,1,0:T(8,128)(2,1)S(1)} %get-tuple-element.26), channel_id=1, source_target_pairs={{0,2},{1,3},{2,0},{3,1},{4,6},{5,7},{6,4},{7,5},{8,10},{9,11},{10,... | collective-permute-start | bytes 393224 | tf_op jit(solution)/shard_map/ppermute | solution.py:299
  6.1 0.4 collective-permute-start.1
  6.5 1.0 %collective-permute-start.2 = (bf16[4,128,128]{2,1,0:T(8,128)(2,1)S(1)}, bf16[4,128,128]{2,1,0:T(8,128)(2,1)S(1)}, u32[]{:S(2)}, u32[]{:S(2)}) collective-permute-start(bf16[4,128,128]{2,1,0:T(8,128)(2,1)S(1)} %get-tuple-element.28), channel_id=1, source_target_pairs={{0,1},{1,2},{2,3},{3,0},{4,5},{5,6},{6,7},{7,4},{8,9},{9,10},{10,1... | collective-permute-start | bytes 393224 | tf_op jit(solution)/shard_map/ppermute | solution.py:299
  7.5 1.2 %tables.1 = (bf16[128,128]{1,0:T(8,128)(2,1)S(1)}, bf16[512,128]{1,0:T(8,128)(2,1)S(1)}) custom-call(s32[3,16,32]{2,1,0:T(8,128)} %bitcast.3, bf16[16,4,32]{2,1,0:T(4,128)(2,1)} %bitcast.5), custom_call_target="tpu_custom_call" | custom-call | tf_op jit(solution)/shard_map/tables/pallas_call | solution.py:225
  8.7 0.0 copy-done
  8.7 0.3 turn.1.rest_5_.refs_7_
  9.1 0.0 copy-start.1
  9.1 0.0 copy-start.2
  9.1 0.2 collective-permute-done.rest_0_
  9.3 3.3 %collective-permute-done.1.rest_1_ = bf16[4,128,128]{2,1,0:T(8,128)(2,1)S(1)} collective-permute-done((bf16[4,128,128]{2,1,0:T(8,128)(2,1)S(1)}, bf16[4,128,128]{2,1,0:T(8,128)(2,1)S(1)}, u32[]{:S(2)}, u32[]{:S(2)}) %collective-permute-start.1) | collective-permute-done | bytes 131104 | tf_op jit(solution)/shard_map/ppermute | solution.py:299
  12.6 0.0 collective-permute-done.2.rest_2_
  12.6 1.1 %first.1 = (bf16[128,128]{1,0:T(8,128)(2,1)S(1)}, bf16[256,128]{1,0:T(8,128)(2,1)S(1)}) custom-call(f32[4,128,128]{2,1,0:T(8,128)S(1)} %get-tuple-element.25.own_ref, bf16[4,128,128]{2,1,0:T(8,128)(2,1)S(1)} %collective-permute-done.rest_0_, bf16[4,128,128]{2,1,0:T(8,128)(2,1)S(1)} %collective-permute-done.1.rest_1_, ...), custom_call_target="tpu_custom_call" | custom-call | tf_op jit(solution)/shard_map/first/pallas_call | solution.py:225
  13.7 1.6 %collective-permute-start.3 = (bf16[256,128]{1,0:T(8,128)(2,1)S(1)}, bf16[256,128]{1,0:T(8,128)(2,1)S(1)}, u32[]{:S(2)}, u32[]{:S(2)}) collective-permute-start(bf16[256,128]{1,0:T(8,128)(2,1)S(1)} %get-tuple-element.30), channel_id=1, source_target_pairs={{0,4},{4,0},{8,12},{12,8},{16,20},{20,16},{24,28},{28,24},{32,36},... | collective-permute-start | bytes 196616 | tf_op jit(solution)/shard_map/ppermute | solution.py:260
  15.3 0.1 keep.4.keep_ref
  15.4 0.8 collective-permute-done.3.got_ref
  16.2 0.1 add.1
  16.3 19.4 %all_to_all.20.refs_0_ = bf16[64,16,128]{2,1,0:T(8,128)(2,1)S(1)} all-to-all(bf16[64,16,128]{2,1,0:T(8,128)(2,1)S(1)} %get-tuple-element.31), channel_id=1, replica_groups={{0,105,27,114,40,89,51,2,120,17,67,42,80,97,11,122,32,73,59,82,104,25,1..., dimensions={0} | all-to-all | bytes 524288 | tf_op jit(solution)/shard_map/all_to_all | solution.py:271
  35.7 0.0 copy-done.1
  35.7 0.0 copy-done.2
  35.7 1.5 %step0.1 = (bf16[128,128]{1,0:T(8,128)(2,1)S(1)}, bf16[256,128]{1,0:T(8,128)(2,1)S(1)}, bf16[16,128]{1,0:T(8,128)(2,1)S(1)}) custom-call(bf16[64,16,128]{2,1,0:T(8,128)(2,1)S(1)} %all_to_all.20.refs_0_, f32[16,4,128]{2,1,0:T(4,128)S(1)} %copy-done.2, bf16[16,128,128]{2,1,0:T(8,128)(2,1)S(1)} %copy-done.1, bf16[128,128]{1,0:T(8,128)(2,1)S(1)} %get-tuple-element.32.refs_3_, ...), custom_call_target="tpu_custom_call" | custom-call | tf_op jit(solution)/shard_map/step0/pallas_call | solution.py:225
  37.2 1.2 %collective-permute-start.4 = (bf16[256,128]{1,0:T(8,128)(2,1)S(1)}, bf16[256,128]{1,0:T(8,128)(2,1)S(1)}, u32[]{:S(2)}, u32[]{:S(2)}) collective-permute-start(bf16[256,128]{1,0:T(8,128)(2,1)S(1)} %get-tuple-element.35), channel_id=1, source_target_pairs={{0,4},{4,0},{8,12},{12,8},{16,20},{20,16},{24,28},{28,24},{32,36},... | collective-permute-start | bytes 196616 | tf_op jit(solution)/shard_map/ppermute | solution.py:260
  38.4 0.1 keep.5.keep_ref
  38.5 0.8 collective-permute-done.4.got_ref
  39.3 0.1 join.3
  39.3 14.1 %all_to_all.21.refs_0_ = bf16[64,16,128]{2,1,0:T(8,128)(2,1)S(1)} all-to-all(bf16[64,16,128]{2,1,0:T(8,128)(2,1)S(1)} %join.3), channel_id=1, replica_groups={{0,105,27,114,40,89,51,2,120,17,67,42,80,97,11,122,32,73,59,82,104,25,1..., dimensions={0} | all-to-all | bytes 524288 | tf_op jit(solution)/shard_map/all_to_all | solution.py:271
  53.5 1.5 %step1.1 = (bf16[128,128]{1,0:T(8,128)(2,1)S(1)}, bf16[256,128]{1,0:T(8,128)(2,1)S(1)}, bf16[16,128]{1,0:T(8,128)(2,1)S(1)}) custom-call(bf16[64,16,128]{2,1,0:T(8,128)(2,1)S(1)} %all_to_all.21.refs_0_, f32[16,4,128]{2,1,0:T(4,128)S(1)} %copy-done.2, bf16[16,128,128]{2,1,0:T(8,128)(2,1)S(1)} %copy-done.1, bf16[128,128]{1,0:T(8,128)(2,1)S(1)} %get-tuple-element.32.refs_3_, ...), custom_call_target="tpu_custom_call" | custom-call | tf_op jit(solution)/shard_map/step1/pallas_call | solution.py:225
  55.0 1.2 %collective-permute-start.5 = (bf16[256,128]{1,0:T(8,128)(2,1)S(1)}, bf16[256,128]{1,0:T(8,128)(2,1)S(1)}, u32[]{:S(2)}, u32[]{:S(2)}) collective-permute-start(bf16[256,128]{1,0:T(8,128)(2,1)S(1)} %get-tuple-element.38), channel_id=1, source_target_pairs={{0,4},{4,0},{8,12},{12,8},{16,20},{20,16},{24,28},{28,24},{32,36},... | collective-permute-start | bytes 196616 | tf_op jit(solution)/shard_map/ppermute | solution.py:260
  56.2 0.1 keep.6.keep_ref
  56.4 0.8 collective-permute-done.5.got_ref
  57.1 0.1 join.4
  57.2 14.1 %all_to_all.22.refs_0_ = bf16[64,16,128]{2,1,0:T(8,128)(2,1)S(1)} all-to-all(bf16[64,16,128]{2,1,0:T(8,128)(2,1)S(1)} %join.4), channel_id=1, replica_groups={{0,105,27,114,40,89,51,2,120,17,67,42,80,97,11,122,32,73,59,82,104,25,1..., dimensions={0} | all-to-all | bytes 524288 | tf_op jit(solution)/shard_map/all_to_all | solution.py:271
  71.3 1.5 %step2.1 = (bf16[128,128]{1,0:T(8,128)(2,1)S(1)}, bf16[256,128]{1,0:T(8,128)(2,1)S(1)}, bf16[16,128]{1,0:T(8,128)(2,1)S(1)}) custom-call(bf16[64,16,128]{2,1,0:T(8,128)(2,1)S(1)} %all_to_all.22.refs_0_, f32[16,4,128]{2,1,0:T(4,128)S(1)} %copy-done.2, bf16[16,128,128]{2,1,0:T(8,128)(2,1)S(1)} %copy-done.1, bf16[128,128]{1,0:T(8,128)(2,1)S(1)} %get-tuple-element.32.refs_3_, ...), custom_call_target="tpu_custom_call" | custom-call | tf_op jit(solution)/shard_map/step2/pallas_call | solution.py:225
  72.8 1.2 %collective-permute-start.6 = (bf16[256,128]{1,0:T(8,128)(2,1)S(1)}, bf16[256,128]{1,0:T(8,128)(2,1)S(1)}, u32[]{:S(2)}, u32[]{:S(2)}) collective-permute-start(bf16[256,128]{1,0:T(8,128)(2,1)S(1)} %get-tuple-element.41), channel_id=1, source_target_pairs={{0,4},{4,0},{8,12},{12,8},{16,20},{20,16},{24,28},{28,24},{32,36},... | collective-permute-start | bytes 196616 | tf_op jit(solution)/shard_map/ppermute | solution.py:260
  74.0 0.1 keep.7.keep_ref
  74.2 0.8 collective-permute-done.6.got_ref
  74.9 0.1 join.5
  75.0 14.1 %all_to_all.23.recv_ref = bf16[64,16,128]{2,1,0:T(8,128)(2,1)S(1)} all-to-all(bf16[64,16,128]{2,1,0:T(8,128)(2,1)S(1)} %join.5), channel_id=1, replica_groups={{0,105,27,114,40,89,51,2,120,17,67,42,80,97,11,122,32,73,59,82,104,25,1..., dimensions={0} | all-to-all | bytes 524288 | tf_op jit(solution)/shard_map/all_to_all | solution.py:271
  89.1 0.9 %last.1 = bf16[16,4,128]{2,1,0:T(4,128)(2,1)} custom-call(bf16[64,16,128]{2,1,0:T(8,128)(2,1)S(1)} %all_to_all.23.recv_ref, f32[16,4,128]{2,1,0:T(4,128)S(1)} %copy-done.2, bf16[16,128,128]{2,1,0:T(8,128)(2,1)S(1)} %copy-done.1, bf16[16,128]{1,0:T(8,128)(2,1)S(1)} %get-tuple-element.36.refs_8_.refs_9_.rest_0_, ...), custom_call_target="tpu_custom_call" | custom-call | tf_op jit(solution)/shard_map/last/pallas_call | solution.py:225
Async XLA Ops:
  0.0 8.7 %copy-start = (bf16[16,8,128,128]{3,2,1,0:T(8,128)(2,1)S(1)}, bf16[16,8,128,128]{3,2,1,0:T(8,128)(2,1)}, u32[]{:S(2)}) copy-start(bf16[16,8,128,128]{3,2,1,0:T(8,128)(2,1)} %refs_6_.5) | copy-start | bytes 12582916
  1.6 7.7 %collective-permute-start = (bf16[4,128,128]{2,1,0:T(8,128)(2,1)S(1)}, bf16[4,128,128]{2,1,0:T(8,128)(2,1)S(1)}, u32[]{:S(2)}, u32[]{:S(2)}) collective-permute-start(bf16[4,128,128]{2,1,0:T(8,128)(2,1)S(1)} %get-tuple-element.26), channel_id=1, source_target_pairs={{0,2},{1,3},{2,0},{3,1},{4,6},{5,7},{6,4},{7,5},{8,10},{9,11},{10,... | collective-permute-start | bytes 393224 | tf_op jit(solution)/shard_map/ppermute | solution.py:299
  6.1 6.5 %collective-permute-start.1 = (bf16[4,128,128]{2,1,0:T(8,128)(2,1)S(1)}, bf16[4,128,128]{2,1,0:T(8,128)(2,1)S(1)}, u32[]{:S(2)}, u32[]{:S(2)}) collective-permute-start(bf16[4,128,128]{2,1,0:T(8,128)(2,1)S(1)} %get-tuple-element.27), channel_id=1, source_target_pairs={{0,3},{1,0},{2,1},{3,2},{4,7},{5,4},{6,5},{7,6},{8,11},{9,8},{10,9... | collective-permute-start | bytes 393224 | tf_op jit(solution)/shard_map/ppermute | solution.py:299
  6.5 6.1 %collective-permute-start.2 = (bf16[4,128,128]{2,1,0:T(8,128)(2,1)S(1)}, bf16[4,128,128]{2,1,0:T(8,128)(2,1)S(1)}, u32[]{:S(2)}, u32[]{:S(2)}) collective-permute-start(bf16[4,128,128]{2,1,0:T(8,128)(2,1)S(1)} %get-tuple-element.28), channel_id=1, source_target_pairs={{0,1},{1,2},{2,3},{3,0},{4,5},{5,6},{6,7},{7,4},{8,9},{9,10},{10,1... | collective-permute-start | bytes 393224 | tf_op jit(solution)/shard_map/ppermute | solution.py:299
  9.1 26.6 %copy-start.1 = (bf16[16,128,128]{2,1,0:T(8,128)(2,1)S(1)}, bf16[16,128,128]{2,1,0:T(8,128)(2,1)}, u32[]{:S(2)}) copy-start(bf16[16,128,128]{2,1,0:T(8,128)(2,1)} %sinv_ref.1) | copy-start | bytes 1572868
  9.1 26.6 %copy-start.2 = (f32[16,4,128]{2,1,0:T(4,128)S(1)}, f32[16,4,128]{2,1,0:T(4,128)}, u32[]{:S(2)}) copy-start(f32[16,4,128]{2,1,0:T(4,128)} %inc_ref.1) | copy-start | bytes 98308
  13.7 2.5 %collective-permute-start.3 = (bf16[256,128]{1,0:T(8,128)(2,1)S(1)}, bf16[256,128]{1,0:T(8,128)(2,1)S(1)}, u32[]{:S(2)}, u32[]{:S(2)}) collective-permute-start(bf16[256,128]{1,0:T(8,128)(2,1)S(1)} %get-tuple-element.30), channel_id=1, source_target_pairs={{0,4},{4,0},{8,12},{12,8},{16,20},{20,16},{24,28},{28,24},{32,36},... | collective-permute-start | bytes 196616 | tf_op jit(solution)/shard_map/ppermute | solution.py:260
  37.2 2.1 %collective-permute-start.4 = (bf16[256,128]{1,0:T(8,128)(2,1)S(1)}, bf16[256,128]{1,0:T(8,128)(2,1)S(1)}, u32[]{:S(2)}, u32[]{:S(2)}) collective-permute-start(bf16[256,128]{1,0:T(8,128)(2,1)S(1)} %get-tuple-element.35), channel_id=1, source_target_pairs={{0,4},{4,0},{8,12},{12,8},{16,20},{20,16},{24,28},{28,24},{32,36},... | collective-permute-start | bytes 196616 | tf_op jit(solution)/shard_map/ppermute | solution.py:260
  55.0 2.1 %collective-permute-start.5 = (bf16[256,128]{1,0:T(8,128)(2,1)S(1)}, bf16[256,128]{1,0:T(8,128)(2,1)S(1)}, u32[]{:S(2)}, u32[]{:S(2)}) collective-permute-start(bf16[256,128]{1,0:T(8,128)(2,1)S(1)} %get-tuple-element.38), channel_id=1, source_target_pairs={{0,4},{4,0},{8,12},{12,8},{16,20},{20,16},{24,28},{28,24},{32,36},... | collective-permute-start | bytes 196616 | tf_op jit(solution)/shard_map/ppermute | solution.py:260
  72.8 2.1 %collective-permute-start.6 = (bf16[256,128]{1,0:T(8,128)(2,1)S(1)}, bf16[256,128]{1,0:T(8,128)(2,1)S(1)}, u32[]{:S(2)}, u32[]{:S(2)}) collective-permute-start(bf16[256,128]{1,0:T(8,128)(2,1)S(1)} %get-tuple-element.41), channel_id=1, source_target_pairs={{0,4},{4,0},{8,12},{12,8},{16,20},{20,16},{24,28},{28,24},{32,36},... | collective-permute-start | bytes 196616 | tf_op jit(solution)/shard_map/ppermute | solution.py:260

commit v6 on v5

--- a/solution.py
+++ b/solution.py
@@ -105,8 +105,9 @@
     wide = weight_ref[...].astype(F32)
     weights = [jnp.where(band > tap, widen(wide[:, tap, :]), 0.0) for tap in range(WMAX)]
     lags = [jnp.where(diagonal, tapped(lag - first, weights), 0.0) for lag in range(1, STEPS)]
-    rest = jnp.zeros((rows - LAGS * patches, rows), F32)
-    lag_ref[...] = jnp.concatenate(lags + [rest], axis=0).T.astype(BF16)
+    for i, lag in enumerate(lags):
+        line = jnp.sum(lag, axis=0, keepdims=True)
+        lag_ref[i] = jnp.broadcast_to(line, (rows, rows)).T
     obs = table_ref[0]
     obs = (obs // patches % 2 ^ core) * (patches * (lax.axis_size("patch") // 2)) + (
         obs // (2 * patches) * patches + obs % patches
@@ -185,7 +186,9 @@
 
 def amplitude_of(step, recv_ref, inc_ref, sinv_ref):
     sources, patches, src = recv_ref.shape
-    total = jnp.sum(recv_ref[...].astype(F32), axis=0)
+    group = sources // 4
+    total = [jnp.sum(recv_ref[i : i + group].astype(F32), axis=0) for i in range(0, sources, group)]
+    total = (total[0] + total[1]) + (total[2] + total[3])
     drive = inc_ref[:, step, :] - total
     halves = []
     group = 8
@@ -205,8 +208,13 @@
     past_refs, (coupled_ref, give_ref, amp_ref) = rest[:-3], rest[-3:]
     amp = amplitude_of(step, recv_ref, inc_ref, sinv_ref)
     amp_ref[...] = amp
-    past = jnp.concatenate([amp] + [r[...] for r in past_refs], axis=0)
-    driven = stored_ref[step] + dot_f32(lag_ref[:, : past.shape[0]], past, ((1,), (0,)))
+    rows, src = stored_ref.shape[1:]
+    patches = amp.shape[0]
+    driven = stored_ref[step]
+    for lag, past in reversed(list(enumerate([amp] + [r[...] for r in past_refs]))):
+        past = past.astype(F32)
+        each = [jnp.broadcast_to(past[p : p + 1], (rows // patches, src)) for p in range(patches)]
+        driven = driven + lag_ref[lag] * jnp.concatenate(each, axis=0)
     field_of(driven, onehot_ref, coup_ref, turned_ref, coupled_ref, give_ref)
 
 
@@ -302,7 +310,7 @@
     lag_table, onehot = call(
         functools.partial(tables_kernel, local),
         "tables",
-        [shape((rows, rows), BF16), shape((2 * half, rows), BF16)],
+        [shape((LAGS, rows, src), F32), shape((2 * half, rows), BF16)],
         [table, weight],
         in_hbm=True,
         scratch=[

time: 90.4 us -> 89.9 us (level)
  no operation moved by 1% of the time
where the time goes in v6:
time: 89.9 us; the launch traced here: 89.6 us
  blocking collectives  61.8 us (69%)
  starting transfers between devices  11.2 us (12%)
  Pallas kernels  9.93 us (11%)
  waiting for transfers between devices  6.49 us (7%)
    all_to_all x4, blocking collectives, exchange(): lax.all_to_all(send, ('patch', 'slab'), 0, 0, axis_index_groups=groups, t...  61.8 us
    pallas_call x16, Pallas kernels, call(): pl.pallas_call(kernel, name=name, out_shape=outs, in_specs=[pl.BlockSpec(...  9.93 us
    ppermute x3, starting transfers between devices, on_device(): lax.ppermute(x, 'slab', [(z, (z + s) % slabs) for z in range(slabs)])  5.97 us
    ppermute x4, starting transfers between devices, exchange(): got = lax.ppermute(give, 'patch', cores)  5.23 us
    ppermute x3, waiting for transfers between devices, on_device(): lax.ppermute(x, 'slab', [(z, (z + s) % slabs) for z in range(slabs)])  3.45 us
    ppermute x4, waiting for transfers between devices, exchange(): got = lax.ppermute(give, 'patch', cores)  3.03 us
  transfers between devices with their start and end apart: 7, of which 6 were waited for; matrix products, arithmetic and copies ran while one was open for 0% of the time, Pallas kernels for 2%

profile of v6, /device:TPU:1, one launch (start us, length us, event | category | flops | bytes accessed | tf_op | source)
XLA Modules:
  0.0 89.6 jit_solution(10824763382435261680)
XLA Ops:
  0.0 0.0 copy-start
  0.0 1.5 %history.1 = (f32[4,128,128]{2,1,0:T(8,128)S(1)}, bf16[4,128,128]{2,1,0:T(8,128)(2,1)S(1)}, bf16[4,128,128]{2,1,0:T(8,128)(2,1)S(1)}, bf16[4,128,128]{2,1,0:T(8,128)(2,1)S(1)}) custom-call(s32[3,16,32]{2,1,0:T(8,128)} %bitcast.2, bf16[16,4,32]{2,1,0:T(4,128)(2,1)} %bitcast.4, bf16[16,64,128]{2,1,0:T(8,128)(2,1)} %hist_hbm.1), custom_call_target="tpu_custom_call" | custom-call | flops 10000000000 | bytes 10000000 | tf_op jit(solution)/shard_map/history/pallas_call | solution.py:233
  1.6 4.5 %collective-permute-start = (bf16[4,128,128]{2,1,0:T(8,128)(2,1)S(1)}, bf16[4,128,128]{2,1,0:T(8,128)(2,1)S(1)}, u32[]{:S(2)}, u32[]{:S(2)}) collective-permute-start(bf16[4,128,128]{2,1,0:T(8,128)(2,1)S(1)} %get-tuple-element.26), channel_id=1, source_target_pairs={{0,2},{1,3},{2,0},{3,1},{4,6},{5,7},{6,4},{7,5},{8,10},{9,11},{10,... | collective-permute-start | bytes 393224 | tf_op jit(solution)/shard_map/ppermute | solution.py:307
  6.1 0.4 collective-permute-start.1
  6.5 1.0 %collective-permute-start.2 = (bf16[4,128,128]{2,1,0:T(8,128)(2,1)S(1)}, bf16[4,128,128]{2,1,0:T(8,128)(2,1)S(1)}, u32[]{:S(2)}, u32[]{:S(2)}) collective-permute-start(bf16[4,128,128]{2,1,0:T(8,128)(2,1)S(1)} %get-tuple-element.28), channel_id=1, source_target_pairs={{0,1},{1,2},{2,3},{3,0},{4,5},{5,6},{6,7},{7,4},{8,9},{9,10},{10,1... | collective-permute-start | bytes 393224 | tf_op jit(solution)/shard_map/ppermute | solution.py:307
  7.5 1.2 %tables.1 = (f32[3,128,128]{2,1,0:T(8,128)S(1)}, bf16[512,128]{1,0:T(8,128)(2,1)S(1)}) custom-call(s32[3,16,32]{2,1,0:T(8,128)} %bitcast.3, bf16[16,4,32]{2,1,0:T(4,128)(2,1)} %bitcast.5), custom_call_target="tpu_custom_call" | custom-call | tf_op jit(solution)/shard_map/tables/pallas_call | solution.py:233
  8.8 0.0 copy-done
  8.8 0.3 turn.1.rest_5_.refs_7_
  9.1 0.0 copy-start.1
  9.1 0.0 copy-start.2
  9.1 0.1 collective-permute-done.rest_0_
  9.3 3.3 %collective-permute-done.1.rest_1_ = bf16[4,128,128]{2,1,0:T(8,128)(2,1)S(1)} collective-permute-done((bf16[4,128,128]{2,1,0:T(8,128)(2,1)S(1)}, bf16[4,128,128]{2,1,0:T(8,128)(2,1)S(1)}, u32[]{:S(2)}, u32[]{:S(2)}) %collective-permute-start.1) | collective-permute-done | bytes 131104 | tf_op jit(solution)/shard_map/ppermute | solution.py:307
  12.6 0.0 collective-permute-done.2.rest_2_
  12.6 1.1 %first.1 = (bf16[128,128]{1,0:T(8,128)(2,1)S(1)}, bf16[256,128]{1,0:T(8,128)(2,1)S(1)}) custom-call(f32[4,128,128]{2,1,0:T(8,128)S(1)} %get-tuple-element.25.own_ref, bf16[4,128,128]{2,1,0:T(8,128)(2,1)S(1)} %collective-permute-done.rest_0_, bf16[4,128,128]{2,1,0:T(8,128)(2,1)S(1)} %collective-permute-done.1.rest_1_, ...), custom_call_target="tpu_custom_call" | custom-call | tf_op jit(solution)/shard_map/first/pallas_call | solution.py:233
  13.7 1.6 %collective-permute-start.3 = (bf16[256,128]{1,0:T(8,128)(2,1)S(1)}, bf16[256,128]{1,0:T(8,128)(2,1)S(1)}, u32[]{:S(2)}, u32[]{:S(2)}) collective-permute-start(bf16[256,128]{1,0:T(8,128)(2,1)S(1)} %get-tuple-element.30), channel_id=1, source_target_pairs={{0,4},{4,0},{8,12},{12,8},{16,20},{20,16},{24,28},{28,24},{32,36},... | collective-permute-start | bytes 196616 | tf_op jit(solution)/shard_map/ppermute | solution.py:268
  15.3 0.1 keep.4.keep_ref
  15.4 0.8 collective-permute-done.3.got_ref
  16.2 0.1 add.1
  16.3 19.4 %all_to_all.20.refs_0_ = bf16[64,16,128]{2,1,0:T(8,128)(2,1)S(1)} all-to-all(bf16[64,16,128]{2,1,0:T(8,128)(2,1)S(1)} %get-tuple-element.31), channel_id=1, replica_groups={{0,105,27,114,40,89,51,2,120,17,67,42,80,97,11,122,32,73,59,82,104,25,1..., dimensions={0} | all-to-all | bytes 524288 | tf_op jit(solution)/shard_map/all_to_all | solution.py:279
  35.7 0.0 copy-done.1
  35.7 0.0 copy-done.2
  35.7 1.3 %step0.1 = (bf16[128,128]{1,0:T(8,128)(2,1)S(1)}, bf16[256,128]{1,0:T(8,128)(2,1)S(1)}, bf16[16,128]{1,0:T(8,128)(2,1)S(1)}) custom-call(bf16[64,16,128]{2,1,0:T(8,128)(2,1)S(1)} %all_to_all.20.refs_0_, f32[16,4,128]{2,1,0:T(4,128)S(1)} %copy-done.2, bf16[16,128,128]{2,1,0:T(8,128)(2,1)S(1)} %copy-done.1, f32[3,128,128]{2,1,0:T(8,128)S(1)} %get-tuple-element.32.refs_3_, ...), custom_call_target="tpu_custom_call" | custom-call | tf_op jit(solution)/shard_map/step0/pallas_call | solution.py:233
  37.0 1.2 %collective-permute-start.4 = (bf16[256,128]{1,0:T(8,128)(2,1)S(1)}, bf16[256,128]{1,0:T(8,128)(2,1)S(1)}, u32[]{:S(2)}, u32[]{:S(2)}) collective-permute-start(bf16[256,128]{1,0:T(8,128)(2,1)S(1)} %get-tuple-element.35), channel_id=1, source_target_pairs={{0,4},{4,0},{8,12},{12,8},{16,20},{20,16},{24,28},{28,24},{32,36},... | collective-permute-start | bytes 196616 | tf_op jit(solution)/shard_map/ppermute | solution.py:268
  38.2 0.1 keep.5.keep_ref
  38.4 0.8 collective-permute-done.4.got_ref
  39.1 0.1 join.3
  39.2 14.1 %all_to_all.21.refs_0_ = bf16[64,16,128]{2,1,0:T(8,128)(2,1)S(1)} all-to-all(bf16[64,16,128]{2,1,0:T(8,128)(2,1)S(1)} %join.3), channel_id=1, replica_groups={{0,105,27,114,40,89,51,2,120,17,67,42,80,97,11,122,32,73,59,82,104,25,1..., dimensions={0} | all-to-all | bytes 524288 | tf_op jit(solution)/shard_map/all_to_all | solution.py:279
  53.3 1.3 %step1.1 = (bf16[128,128]{1,0:T(8,128)(2,1)S(1)}, bf16[256,128]{1,0:T(8,128)(2,1)S(1)}, bf16[16,128]{1,0:T(8,128)(2,1)S(1)}) custom-call(bf16[64,16,128]{2,1,0:T(8,128)(2,1)S(1)} %all_to_all.21.refs_0_, f32[16,4,128]{2,1,0:T(4,128)S(1)} %copy-done.2, bf16[16,128,128]{2,1,0:T(8,128)(2,1)S(1)} %copy-done.1, f32[3,128,128]{2,1,0:T(8,128)S(1)} %get-tuple-element.32.refs_3_, ...), custom_call_target="tpu_custom_call" | custom-call | tf_op jit(solution)/shard_map/step1/pallas_call | solution.py:233
  54.7 1.2 %collective-permute-start.5 = (bf16[256,128]{1,0:T(8,128)(2,1)S(1)}, bf16[256,128]{1,0:T(8,128)(2,1)S(1)}, u32[]{:S(2)}, u32[]{:S(2)}) collective-permute-start(bf16[256,128]{1,0:T(8,128)(2,1)S(1)} %get-tuple-element.38), channel_id=1, source_target_pairs={{0,4},{4,0},{8,12},{12,8},{16,20},{20,16},{24,28},{28,24},{32,36},... | collective-permute-start | bytes 196616 | tf_op jit(solution)/shard_map/ppermute | solution.py:268
  55.9 0.1 keep.6.keep_ref
  56.1 0.8 collective-permute-done.5.got_ref
  56.8 0.1 join.4
  56.9 14.1 %all_to_all.22.refs_0_ = bf16[64,16,128]{2,1,0:T(8,128)(2,1)S(1)} all-to-all(bf16[64,16,128]{2,1,0:T(8,128)(2,1)S(1)} %join.4), channel_id=1, replica_groups={{0,105,27,114,40,89,51,2,120,17,67,42,80,97,11,122,32,73,59,82,104,25,1..., dimensions={0} | all-to-all | bytes 524288 | tf_op jit(solution)/shard_map/all_to_all | solution.py:279
  71.0 1.3 %step2.1 = (bf16[128,128]{1,0:T(8,128)(2,1)S(1)}, bf16[256,128]{1,0:T(8,128)(2,1)S(1)}, bf16[16,128]{1,0:T(8,128)(2,1)S(1)}) custom-call(bf16[64,16,128]{2,1,0:T(8,128)(2,1)S(1)} %all_to_all.22.refs_0_, f32[16,4,128]{2,1,0:T(4,128)S(1)} %copy-done.2, bf16[16,128,128]{2,1,0:T(8,128)(2,1)S(1)} %copy-done.1, f32[3,128,128]{2,1,0:T(8,128)S(1)} %get-tuple-element.32.refs_3_, ...), custom_call_target="tpu_custom_call" | custom-call | tf_op jit(solution)/shard_map/step2/pallas_call | solution.py:233
  72.4 1.2 %collective-permute-start.6 = (bf16[256,128]{1,0:T(8,128)(2,1)S(1)}, bf16[256,128]{1,0:T(8,128)(2,1)S(1)}, u32[]{:S(2)}, u32[]{:S(2)}) collective-permute-start(bf16[256,128]{1,0:T(8,128)(2,1)S(1)} %get-tuple-element.41), channel_id=1, source_target_pairs={{0,4},{4,0},{8,12},{12,8},{16,20},{20,16},{24,28},{28,24},{32,36},... | collective-permute-start | bytes 196616 | tf_op jit(solution)/shard_map/ppermute | solution.py:268
  73.6 0.1 keep.7.keep_ref
  73.7 0.8 collective-permute-done.6.got_ref
  74.5 0.1 join.5
  74.5 14.1 %all_to_all.23.recv_ref = bf16[64,16,128]{2,1,0:T(8,128)(2,1)S(1)} all-to-all(bf16[64,16,128]{2,1,0:T(8,128)(2,1)S(1)} %join.5), channel_id=1, replica_groups={{0,105,27,114,40,89,51,2,120,17,67,42,80,97,11,122,32,73,59,82,104,25,1..., dimensions={0} | all-to-all | bytes 524288 | tf_op jit(solution)/shard_map/all_to_all | solution.py:279
  88.7 0.9 last.1
Async XLA Ops:
  0.0 8.8 %copy-start = (bf16[16,8,128,128]{3,2,1,0:T(8,128)(2,1)S(1)}, bf16[16,8,128,128]{3,2,1,0:T(8,128)(2,1)}, u32[]{:S(2)}) copy-start(bf16[16,8,128,128]{3,2,1,0:T(8,128)(2,1)} %refs_6_.5) | copy-start | bytes 12582916
  1.6 7.7 %collective-permute-start = (bf16[4,128,128]{2,1,0:T(8,128)(2,1)S(1)}, bf16[4,128,128]{2,1,0:T(8,128)(2,1)S(1)}, u32[]{:S(2)}, u32[]{:S(2)}) collective-permute-start(bf16[4,128,128]{2,1,0:T(8,128)(2,1)S(1)} %get-tuple-element.26), channel_id=1, source_target_pairs={{0,2},{1,3},{2,0},{3,1},{4,6},{5,7},{6,4},{7,5},{8,10},{9,11},{10,... | collective-permute-start | bytes 393224 | tf_op jit(solution)/shard_map/ppermute | solution.py:307
  6.1 6.5 %collective-permute-start.1 = (bf16[4,128,128]{2,1,0:T(8,128)(2,1)S(1)}, bf16[4,128,128]{2,1,0:T(8,128)(2,1)S(1)}, u32[]{:S(2)}, u32[]{:S(2)}) collective-permute-start(bf16[4,128,128]{2,1,0:T(8,128)(2,1)S(1)} %get-tuple-element.27), channel_id=1, source_target_pairs={{0,3},{1,0},{2,1},{3,2},{4,7},{5,4},{6,5},{7,6},{8,11},{9,8},{10,9... | collective-permute-start | bytes 393224 | tf_op jit(solution)/shard_map/ppermute | solution.py:307
  6.5 6.1 %collective-permute-start.2 = (bf16[4,128,128]{2,1,0:T(8,128)(2,1)S(1)}, bf16[4,128,128]{2,1,0:T(8,128)(2,1)S(1)}, u32[]{:S(2)}, u32[]{:S(2)}) collective-permute-start(bf16[4,128,128]{2,1,0:T(8,128)(2,1)S(1)} %get-tuple-element.28), channel_id=1, source_target_pairs={{0,1},{1,2},{2,3},{3,0},{4,5},{5,6},{6,7},{7,4},{8,9},{9,10},{10,1... | collective-permute-start | bytes 393224 | tf_op jit(solution)/shard_map/ppermute | solution.py:307
  9.1 26.6 %copy-start.1 = (bf16[16,128,128]{2,1,0:T(8,128)(2,1)S(1)}, bf16[16,128,128]{2,1,0:T(8,128)(2,1)}, u32[]{:S(2)}) copy-start(bf16[16,128,128]{2,1,0:T(8,128)(2,1)} %sinv_ref.1) | copy-start | bytes 1572868
  9.1 26.5 %copy-start.2 = (f32[16,4,128]{2,1,0:T(4,128)S(1)}, f32[16,4,128]{2,1,0:T(4,128)}, u32[]{:S(2)}) copy-start(f32[16,4,128]{2,1,0:T(4,128)} %inc_ref.1) | copy-start | bytes 98308
  13.7 2.5 %collective-permute-start.3 = (bf16[256,128]{1,0:T(8,128)(2,1)S(1)}, bf16[256,128]{1,0:T(8,128)(2,1)S(1)}, u32[]{:S(2)}, u32[]{:S(2)}) collective-permute-start(bf16[256,128]{1,0:T(8,128)(2,1)S(1)} %get-tuple-element.30), channel_id=1, source_target_pairs={{0,4},{4,0},{8,12},{12,8},{16,20},{20,16},{24,28},{28,24},{32,36},... | collective-permute-start | bytes 196616 | tf_op jit(solution)/shard_map/ppermute | solution.py:268
  37.0 2.1 %collective-permute-start.4 = (bf16[256,128]{1,0:T(8,128)(2,1)S(1)}, bf16[256,128]{1,0:T(8,128)(2,1)S(1)}, u32[]{:S(2)}, u32[]{:S(2)}) collective-permute-start(bf16[256,128]{1,0:T(8,128)(2,1)S(1)} %get-tuple-element.35), channel_id=1, source_target_pairs={{0,4},{4,0},{8,12},{12,8},{16,20},{20,16},{24,28},{28,24},{32,36},... | collective-permute-start | bytes 196616 | tf_op jit(solution)/shard_map/ppermute | solution.py:268
  54.7 2.1 %collective-permute-start.5 = (bf16[256,128]{1,0:T(8,128)(2,1)S(1)}, bf16[256,128]{1,0:T(8,128)(2,1)S(1)}, u32[]{:S(2)}, u32[]{:S(2)}) collective-permute-start(bf16[256,128]{1,0:T(8,128)(2,1)S(1)} %get-tuple-element.38), channel_id=1, source_target_pairs={{0,4},{4,0},{8,12},{12,8},{16,20},{20,16},{24,28},{28,24},{32,36},... | collective-permute-start | bytes 196616 | tf_op jit(solution)/shard_map/ppermute | solution.py:268
  72.4 2.1 %collective-permute-start.6 = (bf16[256,128]{1,0:T(8,128)(2,1)S(1)}, bf16[256,128]{1,0:T(8,128)(2,1)S(1)}, u32[]{:S(2)}, u32[]{:S(2)}) collective-permute-start(bf16[256,128]{1,0:T(8,128)(2,1)S(1)} %get-tuple-element.41), channel_id=1, source_target_pairs={{0,4},{4,0},{8,12},{12,8},{16,20},{20,16},{24,28},{28,24},{32,36},... | collective-permute-start | bytes 196616 | tf_op jit(solution)/shard_map/ppermute | solution.py:268

commit v7 on v6

--- a/solution.py
+++ b/solution.py
@@ -301,7 +301,6 @@
             pltpu.VMEM(history.shape, BF16),
             pltpu.SemaphoreType.DMA((3,)),
         ],
-        cost=pl.CostEstimate(flops=10**10, bytes_accessed=10**7, transcendentals=0),
     )
     parts = [
         lax.ppermute(x, "slab", [(z, (z + s) % slabs) for z in range(slabs)])
@@ -318,6 +317,7 @@
             pltpu.VMEM(weight.shape, BF16),
             pltpu.SemaphoreType.DMA((2,)),
         ],
+        cost=pl.CostEstimate(flops=10**10, bytes_accessed=10**7, transcendentals=0),
     )
     turned = call(turn_kernel, "turn", shape((patches, TURNED, src, src), BF16), [coupling])
     coupled, give = call(first_kernel, "first", field, [own, *parts, onehot, coupling, turned])

time: 89.9 us -> 89.7 us (level)
  transfers between devices with their start and end apart: 7 -> 7, of which waited for: 6 -> 5; matrix products, arithmetic and copies ran while one was open for 0% -> 0% of each run, Pallas kernels for 2% -> 3%
where the time goes in v7:
time: 89.7 us; the launch traced here: 89.4 us
  blocking collectives  61.8 us (69%)
  starting transfers between devices  11.2 us (12%)
  Pallas kernels  9.98 us (11%)
  waiting for transfers between devices  6.25 us (7%)
    all_to_all x4, blocking collectives, exchange(): lax.all_to_all(send, ('patch', 'slab'), 0, 0, axis_index_groups=groups, t...  61.8 us
    pallas_call x16, Pallas kernels, call(): pl.pallas_call(kernel, name=name, out_shape=outs, in_specs=[pl.BlockSpec(...  9.98 us
    ppermute x3, starting transfers between devices, on_device(): lax.ppermute(x, 'slab', [(z, (z + s) % slabs) for z in range(slabs)])  5.98 us
    ppermute x4, starting transfers between devices, exchange(): got = lax.ppermute(give, 'patch', cores)  5.22 us
    ppermute x3, waiting for transfers between devices, on_device(): lax.ppermute(x, 'slab', [(z, (z + s) % slabs) for z in range(slabs)])  3.22 us
    ppermute x4, waiting for transfers between devices, exchange(): got = lax.ppermute(give, 'patch', cores)  3.03 us
  transfers between devices with their start and end apart: 7, of which 5 were waited for; matrix products, arithmetic and copies ran while one was open for 0% of the time, Pallas kernels for 3%

profile of v7, /device:TPU:1, one launch (start us, length us, event | category | flops | bytes accessed | tf_op | source)
XLA Modules:
  0.0 89.4 jit_solution(12038197223620726190)
XLA Ops:
  0.0 1.4 %history.1 = (f32[4,128,128]{2,1,0:T(8,128)S(1)}, bf16[4,128,128]{2,1,0:T(8,128)(2,1)S(1)}, bf16[4,128,128]{2,1,0:T(8,128)(2,1)S(1)}, bf16[4,128,128]{2,1,0:T(8,128)(2,1)S(1)}) custom-call(s32[3,16,32]{2,1,0:T(8,128)} %bitcast.2, bf16[16,4,32]{2,1,0:T(4,128)(2,1)} %bitcast.4, bf16[16,64,128]{2,1,0:T(8,128)(2,1)} %hist_hbm.1), custom_call_target="tpu_custom_call" | custom-call | tf_op jit(solution)/shard_map/history/pallas_call | solution.py:233
  1.4 4.5 %collective-permute-start = (bf16[4,128,128]{2,1,0:T(8,128)(2,1)S(1)}, bf16[4,128,128]{2,1,0:T(8,128)(2,1)S(1)}, u32[]{:S(2)}, u32[]{:S(2)}) collective-permute-start(bf16[4,128,128]{2,1,0:T(8,128)(2,1)S(1)} %get-tuple-element.26), channel_id=1, source_target_pairs={{0,2},{1,3},{2,0},{3,1},{4,6},{5,7},{6,4},{7,5},{8,10},{9,11},{10,... | collective-permute-start | bytes 393224 | tf_op jit(solution)/shard_map/ppermute | solution.py:306
  5.9 0.4 collective-permute-start.1
  6.3 0.0 copy-start
  6.3 1.0 %collective-permute-start.2 = (bf16[4,128,128]{2,1,0:T(8,128)(2,1)S(1)}, bf16[4,128,128]{2,1,0:T(8,128)(2,1)S(1)}, u32[]{:S(2)}, u32[]{:S(2)}) collective-permute-start(bf16[4,128,128]{2,1,0:T(8,128)(2,1)S(1)} %get-tuple-element.28), channel_id=1, source_target_pairs={{0,1},{1,2},{2,3},{3,0},{4,5},{5,6},{6,7},{7,4},{8,9},{9,10},{10,1... | collective-permute-start | bytes 393224 | tf_op jit(solution)/shard_map/ppermute | solution.py:306
  7.4 1.5 %tables.1 = (f32[3,128,128]{2,1,0:T(8,128)S(1)}, bf16[512,128]{1,0:T(8,128)(2,1)S(1)}) custom-call(s32[3,16,32]{2,1,0:T(8,128)} %bitcast.3, bf16[16,4,32]{2,1,0:T(4,128)(2,1)} %bitcast.5), custom_call_target="tpu_custom_call" | custom-call | flops 10000000000 | bytes 10000000 | tf_op jit(solution)/shard_map/tables/pallas_call | solution.py:233
  8.8 0.0 copy-done
  8.9 0.3 turn.1.rest_5_.refs_7_
  9.2 0.0 copy-start.1
  9.2 0.0 copy-start.2
  9.2 0.0 collective-permute-done.rest_0_
  9.2 3.2 %collective-permute-done.1.rest_1_ = bf16[4,128,128]{2,1,0:T(8,128)(2,1)S(1)} collective-permute-done((bf16[4,128,128]{2,1,0:T(8,128)(2,1)S(1)}, bf16[4,128,128]{2,1,0:T(8,128)(2,1)S(1)}, u32[]{:S(2)}, u32[]{:S(2)}) %collective-permute-start.1) | collective-permute-done | bytes 131104 | tf_op jit(solution)/shard_map/ppermute | solution.py:306
  12.5 0.0 collective-permute-done.2.rest_2_
  12.5 1.1 %first.1 = (bf16[128,128]{1,0:T(8,128)(2,1)S(1)}, bf16[256,128]{1,0:T(8,128)(2,1)S(1)}) custom-call(f32[4,128,128]{2,1,0:T(8,128)S(1)} %get-tuple-element.25.own_ref, bf16[4,128,128]{2,1,0:T(8,128)(2,1)S(1)} %collective-permute-done.rest_0_, bf16[4,128,128]{2,1,0:T(8,128)(2,1)S(1)} %collective-permute-done.1.rest_1_, ...), custom_call_target="tpu_custom_call" | custom-call | tf_op jit(solution)/shard_map/first/pallas_call | solution.py:233
  13.5 1.6 %collective-permute-start.3 = (bf16[256,128]{1,0:T(8,128)(2,1)S(1)}, bf16[256,128]{1,0:T(8,128)(2,1)S(1)}, u32[]{:S(2)}, u32[]{:S(2)}) collective-permute-start(bf16[256,128]{1,0:T(8,128)(2,1)S(1)} %get-tuple-element.30), channel_id=1, source_target_pairs={{0,4},{4,0},{8,12},{12,8},{16,20},{20,16},{24,28},{28,24},{32,36},... | collective-permute-start | bytes 196616 | tf_op jit(solution)/shard_map/ppermute | solution.py:268
  15.1 0.1 keep.4.keep_ref
  15.3 0.8 collective-permute-done.3.got_ref
  16.0 0.1 add.1
  16.1 19.4 %all_to_all.20.refs_0_ = bf16[64,16,128]{2,1,0:T(8,128)(2,1)S(1)} all-to-all(bf16[64,16,128]{2,1,0:T(8,128)(2,1)S(1)} %get-tuple-element.31), channel_id=1, replica_groups={{0,105,27,114,40,89,51,2,120,17,67,42,80,97,11,122,32,73,59,82,104,25,1..., dimensions={0} | all-to-all | bytes 524288 | tf_op jit(solution)/shard_map/all_to_all | solution.py:279
  35.5 0.0 copy-done.1
  35.5 0.0 copy-done.2
  35.5 1.3 %step0.1 = (bf16[128,128]{1,0:T(8,128)(2,1)S(1)}, bf16[256,128]{1,0:T(8,128)(2,1)S(1)}, bf16[16,128]{1,0:T(8,128)(2,1)S(1)}) custom-call(bf16[64,16,128]{2,1,0:T(8,128)(2,1)S(1)} %all_to_all.20.refs_0_, f32[16,4,128]{2,1,0:T(4,128)S(1)} %copy-done.2, bf16[16,128,128]{2,1,0:T(8,128)(2,1)S(1)} %copy-done.1, f32[3,128,128]{2,1,0:T(8,128)S(1)} %get-tuple-element.32.refs_3_, ...), custom_call_target="tpu_custom_call" | custom-call | tf_op jit(solution)/shard_map/step0/pallas_call | solution.py:233
  36.9 1.2 %collective-permute-start.4 = (bf16[256,128]{1,0:T(8,128)(2,1)S(1)}, bf16[256,128]{1,0:T(8,128)(2,1)S(1)}, u32[]{:S(2)}, u32[]{:S(2)}) collective-permute-start(bf16[256,128]{1,0:T(8,128)(2,1)S(1)} %get-tuple-element.35), channel_id=1, source_target_pairs={{0,4},{4,0},{8,12},{12,8},{16,20},{20,16},{24,28},{28,24},{32,36},... | collective-permute-start | bytes 196616 | tf_op jit(solution)/shard_map/ppermute | solution.py:268
  38.1 0.1 keep.5.keep_ref
  38.2 0.8 collective-permute-done.4.got_ref
  39.0 0.1 join.3
  39.1 14.1 %all_to_all.21.refs_0_ = bf16[64,16,128]{2,1,0:T(8,128)(2,1)S(1)} all-to-all(bf16[64,16,128]{2,1,0:T(8,128)(2,1)S(1)} %join.3), channel_id=1, replica_groups={{0,105,27,114,40,89,51,2,120,17,67,42,80,97,11,122,32,73,59,82,104,25,1..., dimensions={0} | all-to-all | bytes 524288 | tf_op jit(solution)/shard_map/all_to_all | solution.py:279
  53.2 1.3 %step1.1 = (bf16[128,128]{1,0:T(8,128)(2,1)S(1)}, bf16[256,128]{1,0:T(8,128)(2,1)S(1)}, bf16[16,128]{1,0:T(8,128)(2,1)S(1)}) custom-call(bf16[64,16,128]{2,1,0:T(8,128)(2,1)S(1)} %all_to_all.21.refs_0_, f32[16,4,128]{2,1,0:T(4,128)S(1)} %copy-done.2, bf16[16,128,128]{2,1,0:T(8,128)(2,1)S(1)} %copy-done.1, f32[3,128,128]{2,1,0:T(8,128)S(1)} %get-tuple-element.32.refs_3_, ...), custom_call_target="tpu_custom_call" | custom-call | tf_op jit(solution)/shard_map/step1/pallas_call | solution.py:233
  54.6 1.2 %collective-permute-start.5 = (bf16[256,128]{1,0:T(8,128)(2,1)S(1)}, bf16[256,128]{1,0:T(8,128)(2,1)S(1)}, u32[]{:S(2)}, u32[]{:S(2)}) collective-permute-start(bf16[256,128]{1,0:T(8,128)(2,1)S(1)} %get-tuple-element.38), channel_id=1, source_target_pairs={{0,4},{4,0},{8,12},{12,8},{16,20},{20,16},{24,28},{28,24},{32,36},... | collective-permute-start | bytes 196616 | tf_op jit(solution)/shard_map/ppermute | solution.py:268
  55.8 0.1 keep.6.keep_ref
  55.9 0.8 collective-permute-done.5.got_ref
  56.7 0.1 join.4
  56.7 14.1 %all_to_all.22.refs_0_ = bf16[64,16,128]{2,1,0:T(8,128)(2,1)S(1)} all-to-all(bf16[64,16,128]{2,1,0:T(8,128)(2,1)S(1)} %join.4), channel_id=1, replica_groups={{0,105,27,114,40,89,51,2,120,17,67,42,80,97,11,122,32,73,59,82,104,25,1..., dimensions={0} | all-to-all | bytes 524288 | tf_op jit(solution)/shard_map/all_to_all | solution.py:279
  70.9 1.3 %step2.1 = (bf16[128,128]{1,0:T(8,128)(2,1)S(1)}, bf16[256,128]{1,0:T(8,128)(2,1)S(1)}, bf16[16,128]{1,0:T(8,128)(2,1)S(1)}) custom-call(bf16[64,16,128]{2,1,0:T(8,128)(2,1)S(1)} %all_to_all.22.refs_0_, f32[16,4,128]{2,1,0:T(4,128)S(1)} %copy-done.2, bf16[16,128,128]{2,1,0:T(8,128)(2,1)S(1)} %copy-done.1, f32[3,128,128]{2,1,0:T(8,128)S(1)} %get-tuple-element.32.refs_3_, ...), custom_call_target="tpu_custom_call" | custom-call | tf_op jit(solution)/shard_map/step2/pallas_call | solution.py:233
  72.2 1.2 %collective-permute-start.6 = (bf16[256,128]{1,0:T(8,128)(2,1)S(1)}, bf16[256,128]{1,0:T(8,128)(2,1)S(1)}, u32[]{:S(2)}, u32[]{:S(2)}) collective-permute-start(bf16[256,128]{1,0:T(8,128)(2,1)S(1)} %get-tuple-element.41), channel_id=1, source_target_pairs={{0,4},{4,0},{8,12},{12,8},{16,20},{20,16},{24,28},{28,24},{32,36},... | collective-permute-start | bytes 196616 | tf_op jit(solution)/shard_map/ppermute | solution.py:268
  73.4 0.1 keep.7.keep_ref
  73.6 0.8 collective-permute-done.6.got_ref
  74.3 0.1 join.5
  74.4 14.1 %all_to_all.23.recv_ref = bf16[64,16,128]{2,1,0:T(8,128)(2,1)S(1)} all-to-all(bf16[64,16,128]{2,1,0:T(8,128)(2,1)S(1)} %join.5), channel_id=1, replica_groups={{0,105,27,114,40,89,51,2,120,17,67,42,80,97,11,122,32,73,59,82,104,25,1..., dimensions={0} | all-to-all | bytes 524288 | tf_op jit(solution)/shard_map/all_to_all | solution.py:279
  88.5 0.9 last.1
Async XLA Ops:
  1.4 7.8 %collective-permute-start = (bf16[4,128,128]{2,1,0:T(8,128)(2,1)S(1)}, bf16[4,128,128]{2,1,0:T(8,128)(2,1)S(1)}, u32[]{:S(2)}, u32[]{:S(2)}) collective-permute-start(bf16[4,128,128]{2,1,0:T(8,128)(2,1)S(1)} %get-tuple-element.26), channel_id=1, source_target_pairs={{0,2},{1,3},{2,0},{3,1},{4,6},{5,7},{6,4},{7,5},{8,10},{9,11},{10,... | collective-permute-start | bytes 393224 | tf_op jit(solution)/shard_map/ppermute | solution.py:306
  5.9 6.5 %collective-permute-start.1 = (bf16[4,128,128]{2,1,0:T(8,128)(2,1)S(1)}, bf16[4,128,128]{2,1,0:T(8,128)(2,1)S(1)}, u32[]{:S(2)}, u32[]{:S(2)}) collective-permute-start(bf16[4,128,128]{2,1,0:T(8,128)(2,1)S(1)} %get-tuple-element.27), channel_id=1, source_target_pairs={{0,3},{1,0},{2,1},{3,2},{4,7},{5,4},{6,5},{7,6},{8,11},{9,8},{10,9... | collective-permute-start | bytes 393224 | tf_op jit(solution)/shard_map/ppermute | solution.py:306
  6.3 2.5 %copy-start = (bf16[16,8,128,128]{3,2,1,0:T(8,128)(2,1)S(1)}, bf16[16,8,128,128]{3,2,1,0:T(8,128)(2,1)}, u32[]{:S(2)}) copy-start(bf16[16,8,128,128]{3,2,1,0:T(8,128)(2,1)} %refs_6_.5) | copy-start | bytes 12582916
  6.3 6.1 %collective-permute-start.2 = (bf16[4,128,128]{2,1,0:T(8,128)(2,1)S(1)}, bf16[4,128,128]{2,1,0:T(8,128)(2,1)S(1)}, u32[]{:S(2)}, u32[]{:S(2)}) collective-permute-start(bf16[4,128,128]{2,1,0:T(8,128)(2,1)S(1)} %get-tuple-element.28), channel_id=1, source_target_pairs={{0,1},{1,2},{2,3},{3,0},{4,5},{5,6},{6,7},{7,4},{8,9},{9,10},{10,1... | collective-permute-start | bytes 393224 | tf_op jit(solution)/shard_map/ppermute | solution.py:306
  9.2 26.3 %copy-start.1 = (bf16[16,128,128]{2,1,0:T(8,128)(2,1)S(1)}, bf16[16,128,128]{2,1,0:T(8,128)(2,1)}, u32[]{:S(2)}) copy-start(bf16[16,128,128]{2,1,0:T(8,128)(2,1)} %sinv_ref.1) | copy-start | bytes 1572868
  9.2 26.3 %copy-start.2 = (f32[16,4,128]{2,1,0:T(4,128)S(1)}, f32[16,4,128]{2,1,0:T(4,128)}, u32[]{:S(2)}) copy-start(f32[16,4,128]{2,1,0:T(4,128)} %inc_ref.1) | copy-start | bytes 98308
  13.5 2.5 %collective-permute-start.3 = (bf16[256,128]{1,0:T(8,128)(2,1)S(1)}, bf16[256,128]{1,0:T(8,128)(2,1)S(1)}, u32[]{:S(2)}, u32[]{:S(2)}) collective-permute-start(bf16[256,128]{1,0:T(8,128)(2,1)S(1)} %get-tuple-element.30), channel_id=1, source_target_pairs={{0,4},{4,0},{8,12},{12,8},{16,20},{20,16},{24,28},{28,24},{32,36},... | collective-permute-start | bytes 196616 | tf_op jit(solution)/shard_map/ppermute | solution.py:268
  36.9 2.1 %collective-permute-start.4 = (bf16[256,128]{1,0:T(8,128)(2,1)S(1)}, bf16[256,128]{1,0:T(8,128)(2,1)S(1)}, u32[]{:S(2)}, u32[]{:S(2)}) collective-permute-start(bf16[256,128]{1,0:T(8,128)(2,1)S(1)} %get-tuple-element.35), channel_id=1, source_target_pairs={{0,4},{4,0},{8,12},{12,8},{16,20},{20,16},{24,28},{28,24},{32,36},... | collective-permute-start | bytes 196616 | tf_op jit(solution)/shard_map/ppermute | solution.py:268
  54.6 2.1 %collective-permute-start.5 = (bf16[256,128]{1,0:T(8,128)(2,1)S(1)}, bf16[256,128]{1,0:T(8,128)(2,1)S(1)}, u32[]{:S(2)}, u32[]{:S(2)}) collective-permute-start(bf16[256,128]{1,0:T(8,128)(2,1)S(1)} %get-tuple-element.38), channel_id=1, source_target_pairs={{0,4},{4,0},{8,12},{12,8},{16,20},{20,16},{24,28},{28,24},{32,36},... | collective-permute-start | bytes 196616 | tf_op jit(solution)/shard_map/ppermute | solution.py:268
  72.2 2.1 %collective-permute-start.6 = (bf16[256,128]{1,0:T(8,128)(2,1)S(1)}, bf16[256,128]{1,0:T(8,128)(2,1)S(1)}, u32[]{:S(2)}, u32[]{:S(2)}) collective-permute-start(bf16[256,128]{1,0:T(8,128)(2,1)S(1)} %get-tuple-element.41), channel_id=1, source_target_pairs={{0,4},{4,0},{8,12},{12,8},{16,20},{20,16},{24,28},{28,24},{32,36},... | collective-permute-start | bytes 196616 | tf_op jit(solution)/shard_map/ppermute | solution.py:268

commit v8 on v7

--- a/solution.py
+++ b/solution.py
@@ -256,8 +256,8 @@
     cores = [(i, i ^ 1) for i in range(2 * blocks)]
     wide = next(n for n in range(1, blocks + 1) if n * n >= blocks)
     chips = [
+        [(y * wide + x, z) for z in around(slabs) for y in around(blocks // wide) for x in around(wide)],
         [(y * wide + x, z) for y in around(blocks // wide) for x in around(wide) for z in around(slabs)],
-        [(y * wide + x, z) for x in around(wide) for z in around(slabs) for y in around(blocks // wide)],
     ]
     count = len(chips[0])
     chips[0] = [chips[0][i * STRIDE % count] for i in range(count)] if math.gcd(STRIDE, count) == 1 else chips[0]

time: 89.7 us -> 89.3 us (level)
  no operation moved by 1% of the time
where the time goes in v8:
time: 89.3 us; the launch traced here: 89 us
  blocking collectives  61.8 us (69%)
  starting transfers between devices  10.8 us (12%)
  Pallas kernels  9.97 us (11%)
  waiting for transfers between devices  6.25 us (7%)
    all_to_all x4, blocking collectives, exchange(): lax.all_to_all(send, ('patch', 'slab'), 0, 0, axis_index_groups=groups, t...  61.8 us
    pallas_call x16, Pallas kernels, call(): pl.pallas_call(kernel, name=name, out_shape=outs, in_specs=[pl.BlockSpec(...  9.97 us
    ppermute x3, starting transfers between devices, on_device(): lax.ppermute(x, 'slab', [(z, (z + s) % slabs) for z in range(slabs)])  5.98 us
    ppermute x4, starting transfers between devices, exchange(): got = lax.ppermute(give, 'patch', cores)  4.77 us
    ppermute x3, waiting for transfers between devices, on_device(): lax.ppermute(x, 'slab', [(z, (z + s) % slabs) for z in range(slabs)])  3.22 us
    ppermute x4, waiting for transfers between devices, exchange(): got = lax.ppermute(give, 'patch', cores)  3.03 us
  transfers between devices with their start and end apart: 7, of which 5 were waited for; matrix products, arithmetic and copies ran while one was open for 0% of the time, Pallas kernels for 3%

profile of v8, /device:TPU:1, one launch (start us, length us, event | category | flops | bytes accessed | tf_op | source)
XLA Modules:
  0.0 89.0 jit_solution(4841567548873367270)
XLA Ops:
  0.0 1.4 %history.1 = (f32[4,128,128]{2,1,0:T(8,128)S(1)}, bf16[4,128,128]{2,1,0:T(8,128)(2,1)S(1)}, bf16[4,128,128]{2,1,0:T(8,128)(2,1)S(1)}, bf16[4,128,128]{2,1,0:T(8,128)(2,1)S(1)}) custom-call(s32[3,16,32]{2,1,0:T(8,128)} %bitcast.2, bf16[16,4,32]{2,1,0:T(4,128)(2,1)} %bitcast.4, bf16[16,64,128]{2,1,0:T(8,128)(2,1)} %hist_hbm.1), custom_call_target="tpu_custom_call" | custom-call | tf_op jit(solution)/shard_map/history/pallas_call | solution.py:233
  1.4 4.5 %collective-permute-start = (bf16[4,128,128]{2,1,0:T(8,128)(2,1)S(1)}, bf16[4,128,128]{2,1,0:T(8,128)(2,1)S(1)}, u32[]{:S(2)}, u32[]{:S(2)}) collective-permute-start(bf16[4,128,128]{2,1,0:T(8,128)(2,1)S(1)} %get-tuple-element.26), channel_id=1, source_target_pairs={{0,2},{1,3},{2,0},{3,1},{4,6},{5,7},{6,4},{7,5},{8,10},{9,11},{10,... | collective-permute-start | bytes 393224 | tf_op jit(solution)/shard_map/ppermute | solution.py:306
  5.9 0.4 collective-permute-start.1
  6.3 0.0 copy-start
  6.3 1.0 %collective-permute-start.2 = (bf16[4,128,128]{2,1,0:T(8,128)(2,1)S(1)}, bf16[4,128,128]{2,1,0:T(8,128)(2,1)S(1)}, u32[]{:S(2)}, u32[]{:S(2)}) collective-permute-start(bf16[4,128,128]{2,1,0:T(8,128)(2,1)S(1)} %get-tuple-element.28), channel_id=1, source_target_pairs={{0,1},{1,2},{2,3},{3,0},{4,5},{5,6},{6,7},{7,4},{8,9},{9,10},{10,1... | collective-permute-start | bytes 393224 | tf_op jit(solution)/shard_map/ppermute | solution.py:306
  7.4 1.5 %tables.1 = (f32[3,128,128]{2,1,0:T(8,128)S(1)}, bf16[512,128]{1,0:T(8,128)(2,1)S(1)}) custom-call(s32[3,16,32]{2,1,0:T(8,128)} %bitcast.3, bf16[16,4,32]{2,1,0:T(4,128)(2,1)} %bitcast.5), custom_call_target="tpu_custom_call" | custom-call | flops 10000000000 | bytes 10000000 | tf_op jit(solution)/shard_map/tables/pallas_call | solution.py:233
  8.8 0.0 copy-done
  8.9 0.3 turn.1.rest_5_.refs_7_
  9.2 0.0 copy-start.1
  9.2 0.0 copy-start.2
  9.2 0.0 collective-permute-done.rest_0_
  9.2 3.2 %collective-permute-done.1.rest_1_ = bf16[4,128,128]{2,1,0:T(8,128)(2,1)S(1)} collective-permute-done((bf16[4,128,128]{2,1,0:T(8,128)(2,1)S(1)}, bf16[4,128,128]{2,1,0:T(8,128)(2,1)S(1)}, u32[]{:S(2)}, u32[]{:S(2)}) %collective-permute-start.1) | collective-permute-done | bytes 131104 | tf_op jit(solution)/shard_map/ppermute | solution.py:306
  12.5 0.0 collective-permute-done.2.rest_2_
  12.5 1.1 %first.1 = (bf16[128,128]{1,0:T(8,128)(2,1)S(1)}, bf16[256,128]{1,0:T(8,128)(2,1)S(1)}) custom-call(f32[4,128,128]{2,1,0:T(8,128)S(1)} %get-tuple-element.25.own_ref, bf16[4,128,128]{2,1,0:T(8,128)(2,1)S(1)} %collective-permute-done.rest_0_, bf16[4,128,128]{2,1,0:T(8,128)(2,1)S(1)} %collective-permute-done.1.rest_1_, ...), custom_call_target="tpu_custom_call" | custom-call | tf_op jit(solution)/shard_map/first/pallas_call | solution.py:233
  13.5 1.6 %collective-permute-start.3 = (bf16[256,128]{1,0:T(8,128)(2,1)S(1)}, bf16[256,128]{1,0:T(8,128)(2,1)S(1)}, u32[]{:S(2)}, u32[]{:S(2)}) collective-permute-start(bf16[256,128]{1,0:T(8,128)(2,1)S(1)} %get-tuple-element.30), channel_id=1, source_target_pairs={{0,4},{4,0},{8,12},{12,8},{16,20},{20,16},{24,28},{28,24},{32,36},... | collective-permute-start | bytes 196616 | tf_op jit(solution)/shard_map/ppermute | solution.py:268
  15.1 0.1 keep.4.keep_ref
  15.3 0.8 collective-permute-done.3.got_ref
  16.0 0.1 add.1
  16.1 19.3 %all_to_all.20.refs_0_ = bf16[64,16,128]{2,1,0:T(8,128)(2,1)S(1)} all-to-all(bf16[64,16,128]{2,1,0:T(8,128)(2,1)S(1)} %get-tuple-element.31), channel_id=1, replica_groups={{0,43,120,83,33,106,89,16,99,72,26,49,66,11,56,115,1,42,121,82,35,104,9..., dimensions={0} | all-to-all | bytes 524288 | tf_op jit(solution)/shard_map/all_to_all | solution.py:279
  35.4 0.0 copy-done.1
  35.4 0.0 copy-done.2
  35.4 1.3 %step0.1 = (bf16[128,128]{1,0:T(8,128)(2,1)S(1)}, bf16[256,128]{1,0:T(8,128)(2,1)S(1)}, bf16[16,128]{1,0:T(8,128)(2,1)S(1)}) custom-call(bf16[64,16,128]{2,1,0:T(8,128)(2,1)S(1)} %all_to_all.20.refs_0_, f32[16,4,128]{2,1,0:T(4,128)S(1)} %copy-done.2, bf16[16,128,128]{2,1,0:T(8,128)(2,1)S(1)} %copy-done.1, f32[3,128,128]{2,1,0:T(8,128)S(1)} %get-tuple-element.32.refs_3_, ...), custom_call_target="tpu_custom_call" | custom-call | tf_op jit(solution)/shard_map/step0/pallas_call | solution.py:233
  36.7 1.1 %collective-permute-start.4 = (bf16[256,128]{1,0:T(8,128)(2,1)S(1)}, bf16[256,128]{1,0:T(8,128)(2,1)S(1)}, u32[]{:S(2)}, u32[]{:S(2)}) collective-permute-start(bf16[256,128]{1,0:T(8,128)(2,1)S(1)} %get-tuple-element.35), channel_id=1, source_target_pairs={{0,4},{4,0},{8,12},{12,8},{16,20},{20,16},{24,28},{28,24},{32,36},... | collective-permute-start | bytes 196616 | tf_op jit(solution)/shard_map/ppermute | solution.py:268
  37.8 0.1 keep.5.keep_ref
  37.9 0.8 collective-permute-done.4.got_ref
  38.8 14.2 %all_to_all.21.refs_0_ = bf16[64,16,128]{2,1,0:T(8,128)(2,1)S(1)} all-to-all(bf16[64,16,128]{2,1,0:T(8,128)(2,1)S(1)} %join.3), channel_id=1, replica_groups={{0,43,120,83,33,106,89,16,99,72,26,49,66,11,56,115,1,42,121,82,35,104,9..., dimensions={0} | all-to-all | bytes 524288 | tf_op jit(solution)/shard_map/all_to_all | solution.py:279
  53.0 1.3 %step1.1 = (bf16[128,128]{1,0:T(8,128)(2,1)S(1)}, bf16[256,128]{1,0:T(8,128)(2,1)S(1)}, bf16[16,128]{1,0:T(8,128)(2,1)S(1)}) custom-call(bf16[64,16,128]{2,1,0:T(8,128)(2,1)S(1)} %all_to_all.21.refs_0_, f32[16,4,128]{2,1,0:T(4,128)S(1)} %copy-done.2, bf16[16,128,128]{2,1,0:T(8,128)(2,1)S(1)} %copy-done.1, f32[3,128,128]{2,1,0:T(8,128)S(1)} %get-tuple-element.32.refs_3_, ...), custom_call_target="tpu_custom_call" | custom-call | tf_op jit(solution)/shard_map/step1/pallas_call | solution.py:233
  54.3 1.1 %collective-permute-start.5 = (bf16[256,128]{1,0:T(8,128)(2,1)S(1)}, bf16[256,128]{1,0:T(8,128)(2,1)S(1)}, u32[]{:S(2)}, u32[]{:S(2)}) collective-permute-start(bf16[256,128]{1,0:T(8,128)(2,1)S(1)} %get-tuple-element.38), channel_id=1, source_target_pairs={{0,4},{4,0},{8,12},{12,8},{16,20},{20,16},{24,28},{28,24},{32,36},... | collective-permute-start | bytes 196616 | tf_op jit(solution)/shard_map/ppermute | solution.py:268
  55.4 0.1 keep.6.keep_ref
  55.5 0.8 collective-permute-done.5.got_ref
  56.3 14.2 %all_to_all.22.refs_0_ = bf16[64,16,128]{2,1,0:T(8,128)(2,1)S(1)} all-to-all(bf16[64,16,128]{2,1,0:T(8,128)(2,1)S(1)} %join.4), channel_id=1, replica_groups={{0,43,120,83,33,106,89,16,99,72,26,49,66,11,56,115,1,42,121,82,35,104,9..., dimensions={0} | all-to-all | bytes 524288 | tf_op jit(solution)/shard_map/all_to_all | solution.py:279
  70.5 1.3 %step2.1 = (bf16[128,128]{1,0:T(8,128)(2,1)S(1)}, bf16[256,128]{1,0:T(8,128)(2,1)S(1)}, bf16[16,128]{1,0:T(8,128)(2,1)S(1)}) custom-call(bf16[64,16,128]{2,1,0:T(8,128)(2,1)S(1)} %all_to_all.22.refs_0_, f32[16,4,128]{2,1,0:T(4,128)S(1)} %copy-done.2, bf16[16,128,128]{2,1,0:T(8,128)(2,1)S(1)} %copy-done.1, f32[3,128,128]{2,1,0:T(8,128)S(1)} %get-tuple-element.32.refs_3_, ...), custom_call_target="tpu_custom_call" | custom-call | tf_op jit(solution)/shard_map/step2/pallas_call | solution.py:233
  71.9 1.1 %collective-permute-start.6 = (bf16[256,128]{1,0:T(8,128)(2,1)S(1)}, bf16[256,128]{1,0:T(8,128)(2,1)S(1)}, u32[]{:S(2)}, u32[]{:S(2)}) collective-permute-start(bf16[256,128]{1,0:T(8,128)(2,1)S(1)} %get-tuple-element.41), channel_id=1, source_target_pairs={{0,4},{4,0},{8,12},{12,8},{16,20},{20,16},{24,28},{28,24},{32,36},... | collective-permute-start | bytes 196616 | tf_op jit(solution)/shard_map/ppermute | solution.py:268
  72.9 0.1 keep.7.keep_ref
  73.1 0.8 collective-permute-done.6.got_ref
  73.9 14.2 %all_to_all.23.recv_ref = bf16[64,16,128]{2,1,0:T(8,128)(2,1)S(1)} all-to-all(bf16[64,16,128]{2,1,0:T(8,128)(2,1)S(1)} %join.5), channel_id=1, replica_groups={{0,43,120,83,33,106,89,16,99,72,26,49,66,11,56,115,1,42,121,82,35,104,9..., dimensions={0} | all-to-all | bytes 524288 | tf_op jit(solution)/shard_map/all_to_all | solution.py:279
  88.1 0.9 last.1
  (3 shorter events, 0.1 us)
Async XLA Ops:
  1.4 7.8 %collective-permute-start = (bf16[4,128,128]{2,1,0:T(8,128)(2,1)S(1)}, bf16[4,128,128]{2,1,0:T(8,128)(2,1)S(1)}, u32[]{:S(2)}, u32[]{:S(2)}) collective-permute-start(bf16[4,128,128]{2,1,0:T(8,128)(2,1)S(1)} %get-tuple-element.26), channel_id=1, source_target_pairs={{0,2},{1,3},{2,0},{3,1},{4,6},{5,7},{6,4},{7,5},{8,10},{9,11},{10,... | collective-permute-start | bytes 393224 | tf_op jit(solution)/shard_map/ppermute | solution.py:306
  5.9 6.5 %collective-permute-start.1 = (bf16[4,128,128]{2,1,0:T(8,128)(2,1)S(1)}, bf16[4,128,128]{2,1,0:T(8,128)(2,1)S(1)}, u32[]{:S(2)}, u32[]{:S(2)}) collective-permute-start(bf16[4,128,128]{2,1,0:T(8,128)(2,1)S(1)} %get-tuple-element.27), channel_id=1, source_target_pairs={{0,3},{1,0},{2,1},{3,2},{4,7},{5,4},{6,5},{7,6},{8,11},{9,8},{10,9... | collective-permute-start | bytes 393224 | tf_op jit(solution)/shard_map/ppermute | solution.py:306
  6.3 2.5 %copy-start = (bf16[16,8,128,128]{3,2,1,0:T(8,128)(2,1)S(1)}, bf16[16,8,128,128]{3,2,1,0:T(8,128)(2,1)}, u32[]{:S(2)}) copy-start(bf16[16,8,128,128]{3,2,1,0:T(8,128)(2,1)} %refs_6_.5) | copy-start | bytes 12582916
  6.3 6.1 %collective-permute-start.2 = (bf16[4,128,128]{2,1,0:T(8,128)(2,1)S(1)}, bf16[4,128,128]{2,1,0:T(8,128)(2,1)S(1)}, u32[]{:S(2)}, u32[]{:S(2)}) collective-permute-start(bf16[4,128,128]{2,1,0:T(8,128)(2,1)S(1)} %get-tuple-element.28), channel_id=1, source_target_pairs={{0,1},{1,2},{2,3},{3,0},{4,5},{5,6},{6,7},{7,4},{8,9},{9,10},{10,1... | collective-permute-start | bytes 393224 | tf_op jit(solution)/shard_map/ppermute | solution.py:306
  9.2 26.2 %copy-start.1 = (bf16[16,128,128]{2,1,0:T(8,128)(2,1)S(1)}, bf16[16,128,128]{2,1,0:T(8,128)(2,1)}, u32[]{:S(2)}) copy-start(bf16[16,128,128]{2,1,0:T(8,128)(2,1)} %sinv_ref.1) | copy-start | bytes 1572868
  9.2 26.2 %copy-start.2 = (f32[16,4,128]{2,1,0:T(4,128)S(1)}, f32[16,4,128]{2,1,0:T(4,128)}, u32[]{:S(2)}) copy-start(f32[16,4,128]{2,1,0:T(4,128)} %inc_ref.1) | copy-start | bytes 98308
  13.5 2.5 %collective-permute-start.3 = (bf16[256,128]{1,0:T(8,128)(2,1)S(1)}, bf16[256,128]{1,0:T(8,128)(2,1)S(1)}, u32[]{:S(2)}, u32[]{:S(2)}) collective-permute-start(bf16[256,128]{1,0:T(8,128)(2,1)S(1)} %get-tuple-element.30), channel_id=1, source_target_pairs={{0,4},{4,0},{8,12},{12,8},{16,20},{20,16},{24,28},{28,24},{32,36},... | collective-permute-start | bytes 196616 | tf_op jit(solution)/shard_map/ppermute | solution.py:268
  36.7 2.0 %collective-permute-start.4 = (bf16[256,128]{1,0:T(8,128)(2,1)S(1)}, bf16[256,128]{1,0:T(8,128)(2,1)S(1)}, u32[]{:S(2)}, u32[]{:S(2)}) collective-permute-start(bf16[256,128]{1,0:T(8,128)(2,1)S(1)} %get-tuple-element.35), channel_id=1, source_target_pairs={{0,4},{4,0},{8,12},{12,8},{16,20},{20,16},{24,28},{28,24},{32,36},... | collective-permute-start | bytes 196616 | tf_op jit(solution)/shard_map/ppermute | solution.py:268
  54.3 2.0 %collective-permute-start.5 = (bf16[256,128]{1,0:T(8,128)(2,1)S(1)}, bf16[256,128]{1,0:T(8,128)(2,1)S(1)}, u32[]{:S(2)}, u32[]{:S(2)}) collective-permute-start(bf16[256,128]{1,0:T(8,128)(2,1)S(1)} %get-tuple-element.38), channel_id=1, source_target_pairs={{0,4},{4,0},{8,12},{12,8},{16,20},{20,16},{24,28},{28,24},{32,36},... | collective-permute-start | bytes 196616 | tf_op jit(solution)/shard_map/ppermute | solution.py:268
  71.9 2.0 %collective-permute-start.6 = (bf16[256,128]{1,0:T(8,128)(2,1)S(1)}, bf16[256,128]{1,0:T(8,128)(2,1)S(1)}, u32[]{:S(2)}, u32[]{:S(2)}) collective-permute-start(bf16[256,128]{1,0:T(8,128)(2,1)S(1)} %get-tuple-element.41), channel_id=1, source_target_pairs={{0,4},{4,0},{8,12},{12,8},{16,20},{20,16},{24,28},{28,24},{32,36},... | collective-permute-start | bytes 196616 | tf_op jit(solution)/shard_map/ppermute | solution.py:268

commit v9 on v8

--- a/solution.py
+++ b/solution.py
@@ -186,9 +186,11 @@
 
 def amplitude_of(step, recv_ref, inc_ref, sinv_ref):
     sources, patches, src = recv_ref.shape
-    group = sources // 4
+    group = sources // 8
     total = [jnp.sum(recv_ref[i : i + group].astype(F32), axis=0) for i in range(0, sources, group)]
-    total = (total[0] + total[1]) + (total[2] + total[3])
+    while len(total) > 1:
+        total = [a + b for a, b in zip(total[::2], total[1::2])]
+    total = total[0]
     drive = inc_ref[:, step, :] - total
     halves = []
     group = 8

time: 89.3 us -> 89.2 us (level)
  no operation moved by 1% of the time
where the time goes in v9:
time: 89.2 us; the launch traced here: 88.9 us
  blocking collectives  61.8 us (69%)
  starting transfers between devices  10.8 us (12%)
  Pallas kernels  9.95 us (11%)
  waiting for transfers between devices  6.25 us (7%)
    all_to_all x4, blocking collectives, exchange(): lax.all_to_all(send, ('patch', 'slab'), 0, 0, axis_index_groups=groups, t...  61.8 us
    pallas_call x16, Pallas kernels, call(): pl.pallas_call(kernel, name=name, out_shape=outs, in_specs=[pl.BlockSpec(...  9.95 us
    ppermute x3, starting transfers between devices, on_device(): lax.ppermute(x, 'slab', [(z, (z + s) % slabs) for z in range(slabs)])  5.98 us
    ppermute x4, starting transfers between devices, exchange(): got = lax.ppermute(give, 'patch', cores)  4.77 us
    ppermute x3, waiting for transfers between devices, on_device(): lax.ppermute(x, 'slab', [(z, (z + s) % slabs) for z in range(slabs)])  3.22 us
    ppermute x4, waiting for transfers between devices, exchange(): got = lax.ppermute(give, 'patch', cores)  3.03 us
  transfers between devices with their start and end apart: 7, of which 5 were waited for; matrix products, arithmetic and copies ran while one was open for 0% of the time, Pallas kernels for 3%

profile of v9, /device:TPU:1, one launch (start us, length us, event | category | flops | bytes accessed | tf_op | source)
XLA Modules:
  0.0 88.9 jit_solution(9059420337309201893)
XLA Ops:
  0.0 1.4 %history.1 = (f32[4,128,128]{2,1,0:T(8,128)S(1)}, bf16[4,128,128]{2,1,0:T(8,128)(2,1)S(1)}, bf16[4,128,128]{2,1,0:T(8,128)(2,1)S(1)}, bf16[4,128,128]{2,1,0:T(8,128)(2,1)S(1)}) custom-call(s32[3,16,32]{2,1,0:T(8,128)} %bitcast.2, bf16[16,4,32]{2,1,0:T(4,128)(2,1)} %bitcast.4, bf16[16,64,128]{2,1,0:T(8,128)(2,1)} %hist_hbm.1), custom_call_target="tpu_custom_call" | custom-call | tf_op jit(solution)/shard_map/history/pallas_call | solution.py:235
  1.4 4.5 %collective-permute-start = (bf16[4,128,128]{2,1,0:T(8,128)(2,1)S(1)}, bf16[4,128,128]{2,1,0:T(8,128)(2,1)S(1)}, u32[]{:S(2)}, u32[]{:S(2)}) collective-permute-start(bf16[4,128,128]{2,1,0:T(8,128)(2,1)S(1)} %get-tuple-element.26), channel_id=1, source_target_pairs={{0,2},{1,3},{2,0},{3,1},{4,6},{5,7},{6,4},{7,5},{8,10},{9,11},{10,... | collective-permute-start | bytes 393224 | tf_op jit(solution)/shard_map/ppermute | solution.py:308
  5.9 0.4 collective-permute-start.1
  6.3 0.0 copy-start
  6.3 1.0 %collective-permute-start.2 = (bf16[4,128,128]{2,1,0:T(8,128)(2,1)S(1)}, bf16[4,128,128]{2,1,0:T(8,128)(2,1)S(1)}, u32[]{:S(2)}, u32[]{:S(2)}) collective-permute-start(bf16[4,128,128]{2,1,0:T(8,128)(2,1)S(1)} %get-tuple-element.28), channel_id=1, source_target_pairs={{0,1},{1,2},{2,3},{3,0},{4,5},{5,6},{6,7},{7,4},{8,9},{9,10},{10,1... | collective-permute-start | bytes 393224 | tf_op jit(solution)/shard_map/ppermute | solution.py:308
  7.4 1.5 %tables.1 = (f32[3,128,128]{2,1,0:T(8,128)S(1)}, bf16[512,128]{1,0:T(8,128)(2,1)S(1)}) custom-call(s32[3,16,32]{2,1,0:T(8,128)} %bitcast.3, bf16[16,4,32]{2,1,0:T(4,128)(2,1)} %bitcast.5), custom_call_target="tpu_custom_call" | custom-call | flops 10000000000 | bytes 10000000 | tf_op jit(solution)/shard_map/tables/pallas_call | solution.py:235
  8.8 0.0 copy-done
  8.9 0.3 turn.1.rest_5_.refs_7_
  9.2 0.0 copy-start.1
  9.2 0.0 copy-start.2
  9.2 0.0 collective-permute-done.rest_0_
  9.2 3.2 %collective-permute-done.1.rest_1_ = bf16[4,128,128]{2,1,0:T(8,128)(2,1)S(1)} collective-permute-done((bf16[4,128,128]{2,1,0:T(8,128)(2,1)S(1)}, bf16[4,128,128]{2,1,0:T(8,128)(2,1)S(1)}, u32[]{:S(2)}, u32[]{:S(2)}) %collective-permute-start.1) | collective-permute-done | bytes 131104 | tf_op jit(solution)/shard_map/ppermute | solution.py:308
  12.5 0.0 collective-permute-done.2.rest_2_
  12.5 1.1 %first.1 = (bf16[128,128]{1,0:T(8,128)(2,1)S(1)}, bf16[256,128]{1,0:T(8,128)(2,1)S(1)}) custom-call(f32[4,128,128]{2,1,0:T(8,128)S(1)} %get-tuple-element.25.own_ref, bf16[4,128,128]{2,1,0:T(8,128)(2,1)S(1)} %collective-permute-done.rest_0_, bf16[4,128,128]{2,1,0:T(8,128)(2,1)S(1)} %collective-permute-done.1.rest_1_, ...), custom_call_target="tpu_custom_call" | custom-call | tf_op jit(solution)/shard_map/first/pallas_call | solution.py:235
  13.5 1.6 %collective-permute-start.3 = (bf16[256,128]{1,0:T(8,128)(2,1)S(1)}, bf16[256,128]{1,0:T(8,128)(2,1)S(1)}, u32[]{:S(2)}, u32[]{:S(2)}) collective-permute-start(bf16[256,128]{1,0:T(8,128)(2,1)S(1)} %get-tuple-element.30), channel_id=1, source_target_pairs={{0,4},{4,0},{8,12},{12,8},{16,20},{20,16},{24,28},{28,24},{32,36},... | collective-permute-start | bytes 196616 | tf_op jit(solution)/shard_map/ppermute | solution.py:270
  15.1 0.1 keep.4.keep_ref
  15.3 0.8 collective-permute-done.3.got_ref
  16.0 0.1 add.1
  16.1 19.3 %all_to_all.20.refs_0_ = bf16[64,16,128]{2,1,0:T(8,128)(2,1)S(1)} all-to-all(bf16[64,16,128]{2,1,0:T(8,128)(2,1)S(1)} %get-tuple-element.31), channel_id=1, replica_groups={{0,43,120,83,33,106,89,16,99,72,26,49,66,11,56,115,1,42,121,82,35,104,9..., dimensions={0} | all-to-all | bytes 524288 | tf_op jit(solution)/shard_map/all_to_all | solution.py:281
  35.4 0.0 copy-done.1
  35.4 0.0 copy-done.2
  35.4 1.3 %step0.1 = (bf16[128,128]{1,0:T(8,128)(2,1)S(1)}, bf16[256,128]{1,0:T(8,128)(2,1)S(1)}, bf16[16,128]{1,0:T(8,128)(2,1)S(1)}) custom-call(bf16[64,16,128]{2,1,0:T(8,128)(2,1)S(1)} %all_to_all.20.refs_0_, f32[16,4,128]{2,1,0:T(4,128)S(1)} %copy-done.2, bf16[16,128,128]{2,1,0:T(8,128)(2,1)S(1)} %copy-done.1, f32[3,128,128]{2,1,0:T(8,128)S(1)} %get-tuple-element.32.refs_3_, ...), custom_call_target="tpu_custom_call" | custom-call | tf_op jit(solution)/shard_map/step0/pallas_call | solution.py:235
  36.7 1.1 %collective-permute-start.4 = (bf16[256,128]{1,0:T(8,128)(2,1)S(1)}, bf16[256,128]{1,0:T(8,128)(2,1)S(1)}, u32[]{:S(2)}, u32[]{:S(2)}) collective-permute-start(bf16[256,128]{1,0:T(8,128)(2,1)S(1)} %get-tuple-element.35), channel_id=1, source_target_pairs={{0,4},{4,0},{8,12},{12,8},{16,20},{20,16},{24,28},{28,24},{32,36},... | collective-permute-start | bytes 196616 | tf_op jit(solution)/shard_map/ppermute | solution.py:270
  37.8 0.1 keep.5.keep_ref
  37.9 0.8 collective-permute-done.4.got_ref
  38.8 14.2 %all_to_all.21.refs_0_ = bf16[64,16,128]{2,1,0:T(8,128)(2,1)S(1)} all-to-all(bf16[64,16,128]{2,1,0:T(8,128)(2,1)S(1)} %join.3), channel_id=1, replica_groups={{0,43,120,83,33,106,89,16,99,72,26,49,66,11,56,115,1,42,121,82,35,104,9..., dimensions={0} | all-to-all | bytes 524288 | tf_op jit(solution)/shard_map/all_to_all | solution.py:281
  52.9 1.3 %step1.1 = (bf16[128,128]{1,0:T(8,128)(2,1)S(1)}, bf16[256,128]{1,0:T(8,128)(2,1)S(1)}, bf16[16,128]{1,0:T(8,128)(2,1)S(1)}) custom-call(bf16[64,16,128]{2,1,0:T(8,128)(2,1)S(1)} %all_to_all.21.refs_0_, f32[16,4,128]{2,1,0:T(4,128)S(1)} %copy-done.2, bf16[16,128,128]{2,1,0:T(8,128)(2,1)S(1)} %copy-done.1, f32[3,128,128]{2,1,0:T(8,128)S(1)} %get-tuple-element.32.refs_3_, ...), custom_call_target="tpu_custom_call" | custom-call | tf_op jit(solution)/shard_map/step1/pallas_call | solution.py:235
  54.3 1.1 %collective-permute-start.5 = (bf16[256,128]{1,0:T(8,128)(2,1)S(1)}, bf16[256,128]{1,0:T(8,128)(2,1)S(1)}, u32[]{:S(2)}, u32[]{:S(2)}) collective-permute-start(bf16[256,128]{1,0:T(8,128)(2,1)S(1)} %get-tuple-element.38), channel_id=1, source_target_pairs={{0,4},{4,0},{8,12},{12,8},{16,20},{20,16},{24,28},{28,24},{32,36},... | collective-permute-start | bytes 196616 | tf_op jit(solution)/shard_map/ppermute | solution.py:270
  55.4 0.1 keep.6.keep_ref
  55.5 0.8 collective-permute-done.5.got_ref
  56.3 14.2 %all_to_all.22.refs_0_ = bf16[64,16,128]{2,1,0:T(8,128)(2,1)S(1)} all-to-all(bf16[64,16,128]{2,1,0:T(8,128)(2,1)S(1)} %join.4), channel_id=1, replica_groups={{0,43,120,83,33,106,89,16,99,72,26,49,66,11,56,115,1,42,121,82,35,104,9..., dimensions={0} | all-to-all | bytes 524288 | tf_op jit(solution)/shard_map/all_to_all | solution.py:281
  70.5 1.3 %step2.1 = (bf16[128,128]{1,0:T(8,128)(2,1)S(1)}, bf16[256,128]{1,0:T(8,128)(2,1)S(1)}, bf16[16,128]{1,0:T(8,128)(2,1)S(1)}) custom-call(bf16[64,16,128]{2,1,0:T(8,128)(2,1)S(1)} %all_to_all.22.refs_0_, f32[16,4,128]{2,1,0:T(4,128)S(1)} %copy-done.2, bf16[16,128,128]{2,1,0:T(8,128)(2,1)S(1)} %copy-done.1, f32[3,128,128]{2,1,0:T(8,128)S(1)} %get-tuple-element.32.refs_3_, ...), custom_call_target="tpu_custom_call" | custom-call | tf_op jit(solution)/shard_map/step2/pallas_call | solution.py:235
  71.8 1.1 %collective-permute-start.6 = (bf16[256,128]{1,0:T(8,128)(2,1)S(1)}, bf16[256,128]{1,0:T(8,128)(2,1)S(1)}, u32[]{:S(2)}, u32[]{:S(2)}) collective-permute-start(bf16[256,128]{1,0:T(8,128)(2,1)S(1)} %get-tuple-element.41), channel_id=1, source_target_pairs={{0,4},{4,0},{8,12},{12,8},{16,20},{20,16},{24,28},{28,24},{32,36},... | collective-permute-start | bytes 196616 | tf_op jit(solution)/shard_map/ppermute | solution.py:270
  72.9 0.1 keep.7.keep_ref
  73.1 0.8 collective-permute-done.6.got_ref
  73.9 14.2 %all_to_all.23.recv_ref = bf16[64,16,128]{2,1,0:T(8,128)(2,1)S(1)} all-to-all(bf16[64,16,128]{2,1,0:T(8,128)(2,1)S(1)} %join.5), channel_id=1, replica_groups={{0,43,120,83,33,106,89,16,99,72,26,49,66,11,56,115,1,42,121,82,35,104,9..., dimensions={0} | all-to-all | bytes 524288 | tf_op jit(solution)/shard_map/all_to_all | solution.py:281
  88.1 0.9 last.1
  (3 shorter events, 0.1 us)
Async XLA Ops:
  1.4 7.8 %collective-permute-start = (bf16[4,128,128]{2,1,0:T(8,128)(2,1)S(1)}, bf16[4,128,128]{2,1,0:T(8,128)(2,1)S(1)}, u32[]{:S(2)}, u32[]{:S(2)}) collective-permute-start(bf16[4,128,128]{2,1,0:T(8,128)(2,1)S(1)} %get-tuple-element.26), channel_id=1, source_target_pairs={{0,2},{1,3},{2,0},{3,1},{4,6},{5,7},{6,4},{7,5},{8,10},{9,11},{10,... | collective-permute-start | bytes 393224 | tf_op jit(solution)/shard_map/ppermute | solution.py:308
  5.9 6.5 %collective-permute-start.1 = (bf16[4,128,128]{2,1,0:T(8,128)(2,1)S(1)}, bf16[4,128,128]{2,1,0:T(8,128)(2,1)S(1)}, u32[]{:S(2)}, u32[]{:S(2)}) collective-permute-start(bf16[4,128,128]{2,1,0:T(8,128)(2,1)S(1)} %get-tuple-element.27), channel_id=1, source_target_pairs={{0,3},{1,0},{2,1},{3,2},{4,7},{5,4},{6,5},{7,6},{8,11},{9,8},{10,9... | collective-permute-start | bytes 393224 | tf_op jit(solution)/shard_map/ppermute | solution.py:308
  6.3 2.5 %copy-start = (bf16[16,8,128,128]{3,2,1,0:T(8,128)(2,1)S(1)}, bf16[16,8,128,128]{3,2,1,0:T(8,128)(2,1)}, u32[]{:S(2)}) copy-start(bf16[16,8,128,128]{3,2,1,0:T(8,128)(2,1)} %refs_6_.5) | copy-start | bytes 12582916
  6.3 6.1 %collective-permute-start.2 = (bf16[4,128,128]{2,1,0:T(8,128)(2,1)S(1)}, bf16[4,128,128]{2,1,0:T(8,128)(2,1)S(1)}, u32[]{:S(2)}, u32[]{:S(2)}) collective-permute-start(bf16[4,128,128]{2,1,0:T(8,128)(2,1)S(1)} %get-tuple-element.28), channel_id=1, source_target_pairs={{0,1},{1,2},{2,3},{3,0},{4,5},{5,6},{6,7},{7,4},{8,9},{9,10},{10,1... | collective-permute-start | bytes 393224 | tf_op jit(solution)/shard_map/ppermute | solution.py:308
  9.2 26.2 %copy-start.1 = (bf16[16,128,128]{2,1,0:T(8,128)(2,1)S(1)}, bf16[16,128,128]{2,1,0:T(8,128)(2,1)}, u32[]{:S(2)}) copy-start(bf16[16,128,128]{2,1,0:T(8,128)(2,1)} %sinv_ref.1) | copy-start | bytes 1572868
  9.2 26.2 %copy-start.2 = (f32[16,4,128]{2,1,0:T(4,128)S(1)}, f32[16,4,128]{2,1,0:T(4,128)}, u32[]{:S(2)}) copy-start(f32[16,4,128]{2,1,0:T(4,128)} %inc_ref.1) | copy-start | bytes 98308
  13.5 2.5 %collective-permute-start.3 = (bf16[256,128]{1,0:T(8,128)(2,1)S(1)}, bf16[256,128]{1,0:T(8,128)(2,1)S(1)}, u32[]{:S(2)}, u32[]{:S(2)}) collective-permute-start(bf16[256,128]{1,0:T(8,128)(2,1)S(1)} %get-tuple-element.30), channel_id=1, source_target_pairs={{0,4},{4,0},{8,12},{12,8},{16,20},{20,16},{24,28},{28,24},{32,36},... | collective-permute-start | bytes 196616 | tf_op jit(solution)/shard_map/ppermute | solution.py:270
  36.7 2.0 %collective-permute-start.4 = (bf16[256,128]{1,0:T(8,128)(2,1)S(1)}, bf16[256,128]{1,0:T(8,128)(2,1)S(1)}, u32[]{:S(2)}, u32[]{:S(2)}) collective-permute-start(bf16[256,128]{1,0:T(8,128)(2,1)S(1)} %get-tuple-element.35), channel_id=1, source_target_pairs={{0,4},{4,0},{8,12},{12,8},{16,20},{20,16},{24,28},{28,24},{32,36},... | collective-permute-start | bytes 196616 | tf_op jit(solution)/shard_map/ppermute | solution.py:270
  54.3 2.0 %collective-permute-start.5 = (bf16[256,128]{1,0:T(8,128)(2,1)S(1)}, bf16[256,128]{1,0:T(8,128)(2,1)S(1)}, u32[]{:S(2)}, u32[]{:S(2)}) collective-permute-start(bf16[256,128]{1,0:T(8,128)(2,1)S(1)} %get-tuple-element.38), channel_id=1, source_target_pairs={{0,4},{4,0},{8,12},{12,8},{16,20},{20,16},{24,28},{28,24},{32,36},... | collective-permute-start | bytes 196616 | tf_op jit(solution)/shard_map/ppermute | solution.py:270
  71.8 2.0 %collective-permute-start.6 = (bf16[256,128]{1,0:T(8,128)(2,1)S(1)}, bf16[256,128]{1,0:T(8,128)(2,1)S(1)}, u32[]{:S(2)}, u32[]{:S(2)}) collective-permute-start(bf16[256,128]{1,0:T(8,128)(2,1)S(1)} %get-tuple-element.41), channel_id=1, source_target_pairs={{0,4},{4,0},{8,12},{12,8},{16,20},{20,16},{24,28},{28,24},{32,36},... | collective-permute-start | bytes 196616 | tf_op jit(solution)/shard_map/ppermute | solution.py:270
